TPU v7x, 32 devices: a whole 2x2x4 slice. The times are simulated.
32 devices in a mesh: groups: 2 (over y), replica: 4 (over z), tensor: 4 (over x, core).
Axes of the slice: x: 2, y: 2, z: 4, core: 2. Of those that a mesh axis runs over, the one named last changes fastest.
Arguments:
- activations: bfloat16 [256, 8192], P(('groups', 'replica'), 'tensor'), parts along dimension 0, may hold values from -6 to 6
- value_matrix: bfloat16 [8192, 1024], P('tensor'), may hold values from -0.0625 to 0.0625
- value_offset_bias: float32 [1024], P('tensor'), may hold values from -3 to 3
- adapter_down_factors: bfloat16 [32, 64, 8192], P(('groups', 'replica'), None, 'tensor'), parts along dimension 0, may hold values from -0.0625 to 0.0625
- adapter_up_factors: bfloat16 [32, 64, 1024], P(('groups', 'replica')), parts along dimension 0, may hold values from -0.75 to 0.75
- adapter_replica: int32 [256, 1], P(('groups', 'replica')), parts along dimension 0, may hold values from 0 to 3; in each aligned block of 32 rows (0 to 31, 32 to 63, ...) at most 16 rows name the same one
- adapter_position: int32 [256], P(('groups', 'replica')), parts along dimension 0, may hold values from 0 to 3
- queries: bfloat16 [256, 64, 128], P(('groups', 'replica'), 'tensor'), parts along dimension 0, may hold values from -88 to 88
- cached_key_rows: bfloat16 [256, 8, 96, 128], P(('groups', 'replica'), 'tensor'), parts along dimension 0, may hold values from -4 to 4
- cached_value_rows: bfloat16 [256, 8, 96, 128], P(('groups', 'replica'), 'tensor'), parts along dimension 0, may hold values from -6 to 6
- incoming_keys: bfloat16 [256, 8, 128], P(('groups', 'replica'), 'tensor'), parts along dimension 0, may hold values from -6 to 6
- lengths: int32 [256], P(('groups', 'replica')), parts along dimension 0, may hold values from 2 to 96, as said below
Outputs:
- context: bfloat16 [256, 64, 128], P(('groups', 'replica'), 'tensor'), parts along dimension 0
- incoming_values: bfloat16 [256, 8, 128], P(('groups', 'replica'), 'tensor'), parts along dimension 0
There are 2 independent parts, one for each index of `groups`. A program takes and returns all parts, laid end to end along the dimension named above; an argument that names none is the same for every part. Nothing has to cross between parts.
Inputs may be any that keep to these rules, and one draw needn't show every extreme that they name: `adapter_replica`: among the 32 requests of one replica (aligned blocks of rows), no replica index is named by more than 16; in some blocks one is named exactly 16 times. `lengths`: some request has exactly 96 cached tokens.
All inputs are finite; a program needn't handle non-finite values.
Results may differ from a plain program's by a relative error of at most 0.0051.
Values may be sent and summed in bfloat16 or wider, within the bound.
No kernel may reach another device: no remote copies, remote signals or barrier semaphores. Data moves between devices by JAX's collectives and lax.ppermute only.
A program may use at most 64 MiB of HBM per device.

v0:
```python
import jax
import jax.numpy as jnp
from jax import lax
from jax.sharding import PartitionSpec as P

adapter_scale = 0.5


def partial_product(broadcast_rows, up_factor):
    upper = broadcast_rows.astype(jnp.bfloat16)
    lower = (broadcast_rows - upper.astype(jnp.float32)).astype(jnp.bfloat16)
    first = jnp.dot(upper, up_factor, preferred_element_type=jnp.float32)
    return first + jnp.dot(lower, up_factor, preferred_element_type=jnp.float32)


def per_device(
    activations,
    value_matrix,
    value_offset_bias,
    adapter_down_factors,
    adapter_up_factors,
    adapter_replica,
    adapter_position,
    queries,
    cached_key_rows,
    cached_value_rows,
    incoming_keys,
    lengths,
):
    own_rows = activations.shape[0]
    local_features = activations.shape[1]
    replicas = lax.axis_size("replica")
    capacity = max(2, 2 * own_rows // replicas)
    tensor_size = lax.axis_size("tensor")
    kv_width = value_matrix.shape[1]
    head_columns = kv_width // tensor_size
    local_adapters = adapter_down_factors.shape[0]
    rank_columns = adapter_down_factors.shape[1]
    home_ids = adapter_replica[:, 0]
    home_hot = (home_ids[:, None] == jnp.arange(replicas, dtype=jnp.int32)[None, :]).astype(
        jnp.int32
    )
    before = jnp.cumsum(home_hot, axis=0) - home_hot
    position = jnp.sum(before * home_hot, axis=1)
    flat_index = home_ids * capacity + position
    send_rows = (
        jnp.zeros((replicas * capacity, local_features), jnp.bfloat16)
        .at[flat_index]
        .set(activations)
    )
    send_rows = send_rows.reshape(replicas, capacity, local_features)
    send_slots = (
        jnp.full((replicas * capacity,), -1.0, jnp.bfloat16)
        .at[flat_index]
        .set(adapter_position.astype(jnp.bfloat16))
    )
    send_slots = send_slots.reshape(replicas, capacity)
    down_flattened = adapter_down_factors.reshape(local_adapters * rank_columns, local_features)
    head_offset = lax.axis_index("tensor") * head_columns
    got_rows = lax.all_to_all(send_rows, "replica", split_axis=0, concat_axis=0, tiled=True)
    got_slots = lax.all_to_all(send_slots, "replica", split_axis=0, concat_axis=0, tiled=True)
    sources = got_slots.shape[0]
    slot_count = got_slots.shape[1]
    flat_rows = got_rows.reshape(sources * slot_count, local_features)
    slot_ids = got_slots.reshape(sources * slot_count).astype(jnp.int32)
    slot_hot = (slot_ids[:, None] == jnp.arange(local_adapters, dtype=jnp.int32)[None, :]).astype(
        jnp.float32
    )
    projected = lax.dot_general(
        flat_rows, down_flattened, (((1,), (1,)), ((), ())), preferred_element_type=jnp.float32
    )
    reduced = jnp.sum(
        projected.reshape(-1, local_adapters, rank_columns) * slot_hot[:, :, None], axis=1
    )
    reduced = lax.psum(reduced, "tensor")
    broadcast_rows = (slot_hot[:, :, None] * reduced[:, None, :]).reshape(
        -1, local_adapters * rank_columns
    )
    up_portion = lax.dynamic_slice_in_dim(adapter_up_factors, head_offset, head_columns, 2)
    up_portion = up_portion.reshape(local_adapters * rank_columns, head_columns)
    final_output = adapter_scale * partial_product(broadcast_rows, up_portion)
    final_output = final_output.reshape(sources, slot_count, head_columns)
    returned = lax.all_to_all(final_output, "replica", split_axis=0, concat_axis=0, tiled=True)
    picked = returned.reshape(replicas * capacity, returned.shape[2])[flat_index]
    base_part = jnp.dot(activations, value_matrix, preferred_element_type=jnp.float32)
    summed = lax.psum_scatter(base_part, "tensor", scatter_dimension=1, tiled=True)
    heads_local = cached_key_rows.shape[1]
    head_size = cached_key_rows.shape[3]
    cache_len = cached_key_rows.shape[2]
    incoming_values = (
        (summed + value_offset_bias + picked)
        .astype(jnp.bfloat16)
        .reshape(own_rows, heads_local, head_size)
    )
    group_size = queries.shape[1] // heads_local
    score_scale = 1.0 / head_size**0.5
    query_blocks = queries.reshape(own_rows, heads_local, group_size, head_size)
    cached = (
        jnp.einsum(
            "rhgd,rhld->rhgl", query_blocks, cached_key_rows, preferred_element_type=jnp.float32
        )
        * score_scale
    )
    valid_slots = jnp.arange(cache_len)[None, :] < lengths[:, None]
    cached = jnp.where(valid_slots[:, None, None, :], cached, -1e30)
    fresh_score = (
        jnp.einsum("rhgd,rhd->rhg", query_blocks, incoming_keys, preferred_element_type=jnp.float32)
        * score_scale
    )
    row_max = jnp.maximum(jnp.max(cached, axis=-1), fresh_score)
    weights_cached = jnp.exp(cached - row_max[..., None])
    weights_fresh = jnp.exp(fresh_score - row_max)
    row_total = jnp.sum(weights_cached, axis=-1) + weights_fresh
    probs_cached = (weights_cached / row_total[..., None]).astype(jnp.bfloat16)
    probs_fresh = (weights_fresh / row_total).astype(jnp.bfloat16)
    context = jnp.einsum(
        "rhgl,rhld->rhgd", probs_cached, cached_value_rows, preferred_element_type=jnp.float32
    )
    context = context + jnp.einsum(
        "rhg,rhd->rhgd", probs_fresh, incoming_values, preferred_element_type=jnp.float32
    )
    context = context.reshape(own_rows, heads_local * group_size, head_size).astype(jnp.bfloat16)
    return (context, incoming_values)


def solution(mesh):
    in_specs = (
        P(("groups", "replica"), "tensor"),
        P("tensor", None),
        P("tensor"),
        P(("groups", "replica"), None, "tensor"),
        P(("groups", "replica"), None, None),
        P(("groups", "replica"), None),
        P(("groups", "replica")),
        P(("groups", "replica"), "tensor", None),
        P(("groups", "replica"), "tensor", None, None),
        P(("groups", "replica"), "tensor", None, None),
        P(("groups", "replica"), "tensor", None),
        P(("groups", "replica")),
    )
    out_specs = (P(("groups", "replica"), "tensor", None), P(("groups", "replica"), "tensor", None))
    return jax.shard_map(
        per_device, mesh=mesh, in_specs=in_specs, out_specs=out_specs, check_vma=False
    )
```

profile of v0, /device:TPU:0, one launch (start us, length us, event | category | flops | bytes accessed | tf_op | source)
XLA Modules:
  0.0 73.4 jit_solution(17088056705634470426)
XLA Ops:
  7.2 0.0 copy-start
  7.2 0.8 %fusion.23 = s32[32,4]{1,0:T(8,128)S(1)} fusion(s32[32]{0:T(128)} %bitcast.55), kind=kLoop, calls=%fused_computation.37 | loop fusion | flops 256 | bytes 640 | tf_op jit(solution)/shard_map/convert_element_type | solution.py:40
  8.0 0.1 reduce_window_sum.11
  8.1 0.8 %select_reduce_fusion = s32[32]{0:T(128)S(1)} fusion(s32[32,4]{1,0:T(8,128)S(1)} %reduce_window_sum.11, s32[32]{0:T(128)} %bitcast.56), kind=kLoop, calls=%fused_computation.35 | loop fusion | flops 608 | bytes 768 | tf_op jit(solution)/shard_map/reduce_sum | solution.py:44
  8.9 0.7 fusion.28
  9.6 0.7 convert_element_type.54
  10.2 0.8 %scatter_custom_fusion = bf16[64]{0:T(256)(128)(2,1)S(1)} fusion(s32[32]{0:T(128)S(1)} %fusion.28, bf16[32]{0:T(256)(128)(2,1)S(1)} %convert_element_type.54, bf16[]{:T(256)} %constant.4.clone.1), kind=kCustom, calls=%fused_computation.54 | custom fusion | bytes 130 | tf_op jit(solution)/shard_map/scatter | solution.py:55
  11.0 0.7 all_to_all.16
  11.7 6.3 %all-to-all-start = ((bf16[4,1,16]{2,1,0:T(2,128)(2,1)}), bf16[4,1,16]{2,1,0:T(2,128)(2,1)S(1)}, u32[]{:S(2)}, u32[]{:S(2)}) async-start(bf16[4,1,16]{2,1,0:T(2,128)(2,1)} %all_to_all.16), calls=%async_computation.1 | async-start | bytes 4096 | tf_op jit(solution)/shard_map/all_to_all | solution.py:61
  18.0 0.0 copy-start.5
  18.0 0.0 copy-start.1
  18.0 0.0 reduce-scatter.2.cloned.1.call-start
  18.0 3.9 %fusion.34 = f32[32,1024]{1,0:T(8,128)} fusion(bf16[32,2048]{1,0:T(8,128)(2,1)} %param.12, bf16[2048,1024]{1,0:T(8,128)(2,1)} %param.13), kind=kOutput, calls=%fused_computation.57 | convolution fusion | flops 134217728 | bytes 4456448 | tf_op jit(solution)/shard_map/dot_general | solution.py:85
  21.9 0.0 copy-start.6
  21.9 0.0 reduce-scatter.2.cloned.1.call-update
  21.9 0.0 copy-done.5
  21.9 0.1 iota_compare_fusion.1
  22.0 0.0 copy-done.1
  22.0 1.9 %fusion.33 = (f32[32,2,8]{2,1,0:T(2,128)S(1)}, f32[32,2,8,96]{3,2,1,0:T(8,128)S(1)}) fusion(bf16[32,2,96,128]{3,2,1,0:T(8,128)(2,1)S(1)} %copy-done.1, bf16[32,16,128]{2,1,0:T(8,128)(2,1)} %param.19, pred[32,96]{1,0:T(8,128)(4,1)S(1)} %iota_compare_fusion.1), kind=kOutput, calls=%fused_computation.56 | convolution fusion | flops 12729856 | bytes 1905664 | tf_op jit(solution)/shard_map/rhgd,rhld->rhgl/dot_general | solution.py:99
  23.9 0.0 copy-start.2
  23.9 0.1 copy.19
  24.0 0.0 copy-done.6
  24.0 1.2 %fusion.8 = f32[32,2,1,8]{3,2,1,0:T(1,128)S(1)} fusion(bf16[32,16,128]{2,1,0:T(8,128)(2,1)} %param.19, bf16[32,2,128,1]{2,1,0,3:T(2,128)(2,1)S(1)} %bitcast.57), kind=kOutput, calls=%fused_computation.20 | convolution fusion | flops 131072 | bytes 149504 | tf_op jit(solution)/shard_map/rhgd,rhd->rhg/dot_general | solution.py:107
  25.2 0.1 copy.26
  25.3 0.1 copy.20
  25.4 0.3 fusion.6
  25.7 1.8 %scatter_custom_fusion.1 = bf16[64,2048]{1,0:T(8,128)(2,1)} fusion(s32[32]{0:T(128)S(1)} %fusion.28, bf16[32,2048]{1,0:T(8,128)(2,1)} %param.12, bf16[]{:T(256)} %constant.8.clone.1), kind=kCustom, calls=%fused_computation.23 | custom fusion | bytes 262656 | tf_op jit(solution)/shard_map/scatter | solution.py:49
  27.5 0.1 copy.21
  27.6 0.0 all-to-all-done
  27.6 5.1 %all-to-all-start.1 = ((bf16[4,16,2048]{2,1,0:T(8,128)(2,1)}), bf16[4,16,2048]{2,1,0:T(8,128)(2,1)S(1)}, u32[]{:S(2)}, u32[]{:S(2)}) async-start(bf16[4,16,2048]{2,1,0:T(8,128)(2,1)} %bitcast.6), calls=%async_computation.2 | async-start | bytes 524288 | tf_op jit(solution)/shard_map/all_to_all | solution.py:60
  32.7 0.1 copy.22
  32.8 0.1 copy.23
  32.9 0.1 reshape.96
  33.0 8.0 %all-to-all-done.1 = bf16[4,16,2048]{2,1,0:T(8,128)(2,1)S(1)} async-done(((bf16[4,16,2048]{2,1,0:T(8,128)(2,1)}), bf16[4,16,2048]{2,1,0:T(8,128)(2,1)S(1)}, u32[]{:S(2)}, u32[]{:S(2)}) %all-to-all-start.1) | async-done | bytes 262176 | tf_op jit(solution)/shard_map/all_to_all | solution.py:60
  41.0 0.0 copy-done.2
  41.0 0.6 fusion.3
  41.6 10.3 %psum.7 = f32[64,64]{1,0:T(8,128)S(1)} all-reduce(f32[64,64]{1,0:T(8,128)S(1)} %fusion.3), channel_id=1, replica_groups=mesh['groups'=2,'replica'=4,'tensor'=4] {'tensor'}, use_global_device_ids=true, to_apply=%region_8.9 | all-reduce | flops 4096 | bytes 32768 | tf_op jit(solution)/shard_map/psum | solution.py:75
  51.9 1.2 %convolution_bitcast_fusion = f32[64,256]{1,0:T(8,128)S(1)} fusion(bf16[4,64,1024]{2,1,0:T(8,128)(2,1)} %param.16, s32[]{:T(128)S(6)} %select_n.15, f32[64,64]{1,0:T(8,128)S(1)} %psum.7, f32[64,4]{0,1:T(4,128)S(1)} %fusion.27), kind=kOutput, calls=%fused_computation.10 | convolution fusion | flops 8470528 | bytes 214020 | tf_op jit(solution)/shard_map/dot_general | solution.py:13
  53.0 1.8 %fusion.5 = f32[64,256]{1,0:T(8,128)} fusion(f32[64,256]{1,0:T(8,128)S(1)} %convolution_bitcast_fusion, bf16[4,64,1024]{2,1,0:T(8,128)(2,1)} %param.16, s32[]{:T(128)S(6)} %select_n.15, f32[64,64]{1,0:T(8,128)S(1)} %psum.7, f32[64,4]{0,1:T(4,128)S(1)} %fusion.27), kind=kOutput, calls=%fused_computation.13 | convolution fusion | flops 8454144 | bytes 279556 | tf_op jit(solution)/shard_map/dot_general | solution.py:12
  54.9 3.3 %all-to-all-start.2 = ((f32[4,16,256]{2,1,0:T(8,128)}), f32[4,16,256]{2,1,0:T(8,128)S(1)}, u32[]{:S(2)}, u32[]{:S(2)}) async-start(f32[4,16,256]{2,1,0:T(8,128)} %bitcast.11), calls=%async_computation.3 | async-start | bytes 131072 | tf_op jit(solution)/shard_map/all_to_all | solution.py:83
  58.2 5.7 %all-to-all-done.2 = f32[4,16,256]{2,1,0:T(8,128)S(1)} async-done(((f32[4,16,256]{2,1,0:T(8,128)}), f32[4,16,256]{2,1,0:T(8,128)S(1)}, u32[]{:S(2)}, u32[]{:S(2)}) %all-to-all-start.2) | async-done | bytes 65568 | tf_op jit(solution)/shard_map/all_to_all | solution.py:83
  63.9 0.6 gather_fusion
  64.5 0.0 reduce-scatter.2.cloned.1.call-done
  64.5 0.0 copy-done.4
  64.5 0.8 %add_convert_fusion = bf16[32,256]{1,0:T(8,128)(2,1)S(1)} fusion(f32[32,256]{1,0:T(8,128)S(1)} %gather_fusion, f32[32,256]{1,0:T(8,128)} %reduce-scatter.2.cloned.1.call-done, f32[256]{0:T(256)S(1)} %copy-done.4), kind=kLoop, calls=%fused_computation.33 | loop fusion | flops 24576 | bytes 82944 | tf_op jit(solution)/shard_map/convert_element_type | solution.py:92
  65.3 0.0 copy-done
  65.3 1.3 %fusion.2 = bf16[32,16,128]{2,1,0:T(8,128)(2,1)} fusion(bf16[32,2,96,128]{3,2,1,0:T(8,128)(2,1)S(1)} %copy-done, f32[32,2,8,96]{3,2,1,0:T(8,128)S(1)} %get-tuple-element.5, f32[32,2,128]{2,1,0:T(2,128)S(1)} %convert.8, f32[32,2,8]{2,1,0:T(2,128)S(1)} %copy.23, f32[32,2,8]{2,1,0:T(2,128)S(1)} %copy.22, f32[32,2,8]{2,1,0:T(2,128)S(1)} %copy.20), kind=kOutput, calls=%fused_computation.7 | convolution fusion | flops 12926976 | bytes 1939456 | tf_op jit(solution)/shard_map/rhgl,rhld->rhgd/dot_general | solution.py:116
  66.6 0.0 copy-done.3
  (9 shorter events, 0.1 us)
Async XLA Ops:
  7.2 58.1 %copy-start = (bf16[32,2,96,128]{3,2,1,0:T(8,128)(2,1)S(1)}, bf16[32,2,96,128]{3,2,1,0:T(8,128)(2,1)}, u32[]{:S(2)}) copy-start(bf16[32,2,96,128]{3,2,1,0:T(8,128)(2,1)} %param.21) | copy-start | bytes 4718596
  11.7 15.9 %all-to-all-start = ((bf16[4,1,16]{2,1,0:T(2,128)(2,1)}), bf16[4,1,16]{2,1,0:T(2,128)(2,1)S(1)}, u32[]{:S(2)}, u32[]{:S(2)}) async-start(bf16[4,1,16]{2,1,0:T(2,128)(2,1)} %all_to_all.16), calls=%async_computation.1 | async-start | bytes 4096 | tf_op jit(solution)/shard_map/all_to_all | solution.py:61
  18.0 3.9 %copy-start.5 = (s32[32]{0:T(128)S(1)}, s32[32]{0:T(128)}, u32[]{:S(2)}) copy-start(s32[32]{0:T(128)} %param.23) | copy-start | bytes 388
  18.0 4.0 %copy-start.1 = (bf16[32,2,96,128]{3,2,1,0:T(8,128)(2,1)S(1)}, bf16[32,2,96,128]{3,2,1,0:T(8,128)(2,1)}, u32[]{:S(2)}) copy-start(bf16[32,2,96,128]{3,2,1,0:T(8,128)(2,1)} %param.20) | copy-start | bytes 4718596
  18.0 46.5 %reduce-scatter.2.cloned.1.call-start = ((), (), s32[]{:S(2)}) async-start(), calls=%async_computation.4 | async-start | bytes 163840 | tf_op jit(solution)/shard_map/reduce_scatter | solution.py:86
  21.9 2.1 %copy-start.6 = (bf16[32,2,128]{2,1,0:T(2,128)(2,1)S(1)}, bf16[32,2,128]{2,1,0:T(2,128)(2,1)}, u32[]{:S(2)}) copy-start(bf16[32,2,128]{2,1,0:T(2,128)(2,1)} %param.22) | copy-start | bytes 49156
  23.9 17.0 %copy-start.2 = (bf16[4,64,2048]{2,1,0:T(8,128)(2,1)S(1)}, bf16[4,64,2048]{2,1,0:T(8,128)(2,1)}, u32[]{:S(2)}) copy-start(bf16[4,64,2048]{2,1,0:T(8,128)(2,1)} %param.15) | copy-start | bytes 3145732
  27.5 37.0 %copy-start.4 = (f32[256]{0:T(256)S(1)}, f32[256]{0:T(256)}, u32[]{:S(2)}) copy-start(f32[256]{0:T(256)} %param.14) | copy-start | bytes 3076
  27.6 13.4 %all-to-all-start.1 = ((bf16[4,16,2048]{2,1,0:T(8,128)(2,1)}), bf16[4,16,2048]{2,1,0:T(8,128)(2,1)S(1)}, u32[]{:S(2)}, u32[]{:S(2)}) async-start(bf16[4,16,2048]{2,1,0:T(8,128)(2,1)} %bitcast.6), calls=%async_computation.2 | async-start | bytes 524288 | tf_op jit(solution)/shard_map/all_to_all | solution.py:60
  54.9 9.0 %all-to-all-start.2 = ((f32[4,16,256]{2,1,0:T(8,128)}), f32[4,16,256]{2,1,0:T(8,128)S(1)}, u32[]{:S(2)}, u32[]{:S(2)}) async-start(f32[4,16,256]{2,1,0:T(8,128)} %bitcast.11), calls=%async_computation.3 | async-start | bytes 131072 | tf_op jit(solution)/shard_map/all_to_all | solution.py:83
  65.3 1.3 %copy-start.3 = (bf16[32,2,128]{2,1,0:T(2,128)(2,1)}, bf16[32,2,128]{2,1,0:T(2,128)(2,1)S(1)}, u32[]{:S(2)}) copy-start(bf16[32,2,128]{2,1,0:T(2,128)(2,1)S(1)} %reshape.95) | copy-start | bytes 49156
Sparse Core Ops, SparseCore 0:
  22.0 21.0 reduce-scatter.1
where the time goes:
time: 74 us; the launch traced here: 73.4 us
  starting transfers between devices  14.7 us (20%)
  between operations  14.2 us (19%)
  waiting for transfers between devices  13.7 us (19%)
  matrix products  11.8 us (16%)
  blocking collectives  10.3 us (14%)
  local copies, waits for them, and re-layouts  4.48 us (6%)
  other arithmetic  4.25 us (6%)
    psum x1, blocking collectives, per_device(): reduced = lax.psum(reduced, 'tensor')  10.3 us
    all_to_all x1, waiting for transfers between devices, per_device(): lax.all_to_all(send_rows, 'replica', split_axis=0, concat_axis=0, tiled=T...  7.99 us
    all_to_all x1, starting transfers between devices, per_device(): lax.all_to_all(send_slots, 'replica', split_axis=0, concat_axis=0, tiled=...  6.32 us
    all_to_all x1, waiting for transfers between devices, per_device(): lax.all_to_all(final_output, 'replica', split_axis=0, concat_axis=0, tile...  5.7 us
    all_to_all x1, starting transfers between devices, per_device(): lax.all_to_all(send_rows, 'replica', split_axis=0, concat_axis=0, tiled=T...  5.06 us
    dot_general x1, matrix products, per_device(): jnp.dot(activations, value_matrix, preferred_element_type=jnp.float32)  3.85 us
    all_to_all x1, starting transfers between devices, per_device(): lax.all_to_all(final_output, 'replica', split_axis=0, concat_axis=0, tile...  3.28 us
    dot_general x1, matrix products, per_device(): jnp.einsum('rhgd,rhld->rhgl', query_blocks, cached_key_rows, preferred_el...  1.92 us
  transfers between devices with their start and end apart: 4, of which 2 were waited for; matrix products, arithmetic and copies ran while one was open for 19% of the time, Pallas kernels for 0%

commit v1 on v0

v1 whole, which is shorter than its diff:
```python
import functools

import jax
import jax.numpy as jnp
from jax import lax
from jax.experimental import pallas as pl
from jax.experimental.pallas import tpu as pltpu
from jax.sharding import PartitionSpec as P

adapter_scale = 0.5
lanes = 128
f32 = jnp.float32
bf16 = jnp.bfloat16
VMEM = pl.BlockSpec(memory_space=pltpu.VMEM)


def call(kernel, name, outs, args, flops, limit=32 << 20, **more):
    read = sum(a.size * a.dtype.itemsize for a in args)
    write = sum(o.size * o.dtype.itemsize for o in outs)
    return pl.pallas_call(
        kernel,
        name=name,
        out_shape=outs,
        cost_estimate=pl.CostEstimate(flops=flops, bytes_accessed=read + write, transcendentals=0),
        compiler_params=pltpu.CompilerParams(vmem_limit_bytes=limit),
        **more,
    )(*args)


def struct(shape, dtype):
    return jax.ShapeDtypeStruct(shape, dtype)


def placement(home_ref, blocks, capacity, relative):
    home = home_ref[...]
    rows = home.shape[0]
    if relative:
        home = home ^ lax.axis_index("replica")
    hot = (home == lax.broadcasted_iota(jnp.int32, (rows, blocks), 1)).astype(f32)
    row = lax.broadcasted_iota(jnp.int32, (rows, rows), 0)
    column = lax.broadcasted_iota(jnp.int32, (rows, rows), 1)
    below = (column < row).astype(bf16)
    before = jnp.dot(below, hot.astype(bf16), preferred_element_type=f32)
    position = jnp.sum(before * hot, axis=1, keepdims=True).astype(jnp.int32)
    flat = home * capacity + position
    return flat == lax.broadcasted_iota(jnp.int32, (rows, blocks * capacity), 1)


def pack_kernel(blocks, capacity, relative, home_ref, slot_ref, rows_ref, *outs):
    place = placement(home_ref, blocks, capacity, relative)
    rows, width = rows_ref.shape
    square = lax.broadcasted_iota(jnp.int32, (rows, rows), 0) == lax.broadcasted_iota(
        jnp.int32, (rows, rows), 1
    )
    slot = jnp.sum(jnp.where(square, slot_ref[...], 0), axis=1, keepdims=True) + 1
    spread = jnp.broadcast_to(slot.astype(f32), (rows, lanes)).astype(bf16)
    turned = place.astype(f32).astype(bf16)
    over = (((0,), (0,)), ((), ()))
    packed = lax.dot_general(turned, rows_ref[...], over, preferred_element_type=f32).astype(bf16)
    slots = lax.dot_general(turned, spread, over, preferred_element_type=f32).astype(bf16)
    size = outs[0].shape[0]
    for b, out in enumerate(outs):
        out[:, :width] = packed[b * size : (b + 1) * size]
        out[:, width:] = slots[b * size : (b + 1) * size]


def rank_kernel(pieces, adapters, *refs):
    got = refs[:pieces]
    down_ref, base_ref, rank_ref, slot_ref = refs[pieces : pieces + 4]
    messages = refs[pieces + 4 :]
    features = down_ref.shape[1]
    rows = jnp.concatenate([ref[:, :features] for ref in got], axis=0)
    slots = jnp.concatenate([ref[:, features:] for ref in got], axis=0).astype(f32)
    slot_ref[...] = slots
    across = (((1,), (1,)), ((), ()))
    projected = lax.dot_general(rows, down_ref[...], across, preferred_element_type=f32)
    width = down_ref.shape[0] // adapters
    total = None
    for a in range(adapters):
        term = projected[:, a * width : (a + 1) * width]
        term = jnp.where(slots[:, :width] == a + 1.0, term, 0.0)
        total = term if total is None else total + term
    rank_ref[...] = total
    upper = total.astype(bf16)
    lower = (total - upper.astype(f32)).astype(bf16)
    pair = jnp.concatenate([upper, lower], axis=1)
    me = lax.axis_index("tensor")
    for d, message in enumerate(messages):
        block = base_ref[me ^ (d + 1)].astype(bf16)
        at = 0
        for c in range(block.shape[1] // lanes):
            message[at : at + block.shape[0], :] = block[:, c * lanes : (c + 1) * lanes]
            at += block.shape[0]
        message[at:, :] = pair


def up_kernel(peers, adapters, *refs):
    got = refs[:peers]
    rank_ref, slot_ref, up_ref = refs[peers : peers + 3]
    outs = refs[peers + 3 :]
    total = rank_ref[...]
    count, width = total.shape
    for ref in got:
        pair = ref[ref.shape[0] - count :, :].astype(f32)
        total = total + (pair[:, :width] + pair[:, width:])
    slots = slot_ref[:, :width]
    wide = jnp.concatenate(
        [jnp.where(slots == a + 1.0, total, 0.0) for a in range(adapters)], axis=1
    )
    upper = wide.astype(bf16)
    lower = (wide - upper.astype(f32)).astype(bf16)
    term = jnp.dot(upper, up_ref[...], preferred_element_type=f32)
    term = adapter_scale * (term + jnp.dot(lower, up_ref[...], preferred_element_type=f32))
    term = term.astype(bf16)
    size = outs[0].shape[0]
    for b, out in enumerate(outs):
        out[...] = term[b * size : (b + 1) * size]


def sum_kernel(peers, *refs):
    got = refs[:peers]
    base_ref, bias_ref, out = refs[peers:]
    total = base_ref[lax.axis_index("tensor")] + bias_ref[...]
    rows = total.shape[0]
    for c in range(total.shape[1] // lanes):
        part = total[:, c * lanes : (c + 1) * lanes]
        for ref in got:
            part = part + ref[c * rows : (c + 1) * rows, :].astype(f32)
        out[:, c * lanes : (c + 1) * lanes] = part


def last_kernel(pieces, blocks, capacity, relative, *refs):
    got = refs[:pieces]
    home_ref, base_ref, cached_ref, fresh_ref, context_ref, values_ref = refs[pieces:]
    place = placement(home_ref, blocks, capacity, relative).astype(f32).astype(bf16)
    terms = jnp.concatenate([ref[...] for ref in got], axis=0)
    picked = jnp.dot(place, terms, preferred_element_type=f32)
    values = (base_ref[...] + picked).astype(bf16)
    heads, size = values_ref.shape[1:]
    group = cached_ref.shape[1] // heads
    for h in range(heads):
        value = values[:, h * size : (h + 1) * size].astype(f32)
        values_ref[:, h, :] = value.astype(bf16)
        own = slice(h * group, (h + 1) * group)
        context = cached_ref[:, own, :] + fresh_ref[:, own, :] * value[:, None, :]
        context_ref[:, own, :] = context.astype(bf16)


def base_kernel(rows_ref, matrix_ref, out):
    parts, _, width = out.shape
    product = jnp.dot(rows_ref[...], matrix_ref[...], preferred_element_type=f32)

    @pl.when(pl.program_id(0) == 0)
    def _():
        for t in range(parts):
            out[t] = product[:, t * width : (t + 1) * width]

    @pl.when(pl.program_id(0) > 0)
    def _():
        for t in range(parts):
            out[t] += product[:, t * width : (t + 1) * width]


def attention_kernel(length_ref, query_ref, key_ref, value_ref, new_ref, cached_ref, fresh_ref):
    requests, heads, length, size = key_ref.shape
    group = query_ref.shape[1] // heads
    scale = 1.0 / size**0.5
    step = pl.program_id(0)
    slot = lax.broadcasted_iota(jnp.int32, (group, length), 1)
    for r in range(requests):
        valid = slot < length_ref[step * requests + r]
        for h in range(heads):
            own = slice(h * group, (h + 1) * group)
            query = query_ref[r, own, :]
            across = (((1,), (1,)), ((), ()))
            scores = lax.dot_general(query, key_ref[r, h], across, preferred_element_type=f32)
            scores = jnp.where(valid, scores * scale, -1e30)
            new = new_ref[r, h : h + 1, :].astype(f32)
            fresh = jnp.sum(query.astype(f32) * new, axis=1, keepdims=True) * scale
            top = jnp.maximum(jnp.max(scores, axis=1, keepdims=True), fresh)
            weights = jnp.exp(scores - top)
            alone = jnp.exp(fresh - top)
            total = jnp.sum(weights, axis=1, keepdims=True) + alone
            probs = (weights / total).astype(bf16)
            cached_ref[r, own, :] = jnp.dot(probs, value_ref[r, h], preferred_element_type=f32)
            share = jnp.broadcast_to(alone / total, (group, size))
            fresh_ref[r, own, :] = share.astype(bf16).astype(f32)


def attention(lengths, queries, keys, values, new_keys):
    rows, heads, length, size = keys.shape
    query_heads = queries.shape[1]
    steps = 4
    part = rows // steps
    shape = (rows, query_heads, size)
    q_spec = pl.BlockSpec((part, query_heads, size), lambda i, _: (i, 0, 0))
    kv_spec = pl.BlockSpec((part, heads, length, size), lambda i, _: (i, 0, 0, 0))
    n_spec = pl.BlockSpec((part, heads, size), lambda i, _: (i, 0, 0))
    return call(
        attention_kernel,
        "attention",
        [struct(shape, f32), struct(shape, f32)],
        [lengths, queries, keys, values, new_keys],
        4 * rows * query_heads * length * size,
        grid_spec=pltpu.PrefetchScalarGridSpec(
            num_scalar_prefetch=1,
            grid=(steps,),
            in_specs=[q_spec, kv_spec, kv_spec, n_spec],
            out_specs=[q_spec, q_spec],
        ),
    )


def base_product(rows, matrix, parts):
    count, depth = rows.shape
    width = matrix.shape[1] // parts
    steps = 4
    return call(
        base_kernel,
        "base",
        [struct((parts, count, width), f32)],
        [rows, matrix],
        2 * count * depth * matrix.shape[1],
        grid=(steps,),
        in_specs=[
            pl.BlockSpec((count, depth // steps), lambda i: (0, i)),
            pl.BlockSpec((depth // steps, matrix.shape[1]), lambda i: (i, 0)),
        ],
        out_specs=[pl.BlockSpec((parts, count, width), lambda i: (0, 0, 0))],
    )[0]


def exchange(blocks, axis):
    size = lax.axis_size(axis)
    got = [
        lax.ppermute(block, axis, [(i, i ^ (d + 1)) for i in range(size)])
        for d, block in enumerate(blocks[1:])
    ]
    return [blocks[0]] + got


def per_device(
    activations,
    value_matrix,
    value_offset_bias,
    adapter_down_factors,
    adapter_up_factors,
    adapter_replica,
    adapter_position,
    queries,
    cached_key_rows,
    cached_value_rows,
    incoming_keys,
    lengths,
):
    rows, features = activations.shape
    replicas = lax.axis_size("replica")
    parts = lax.axis_size("tensor")
    capacity = max(2, 2 * rows // replicas)
    adapters, rank, _ = adapter_down_factors.shape
    width = value_matrix.shape[1] // parts
    heads, size = incoming_keys.shape[1:]
    slots = replicas * capacity
    direct = capacity % 16 == 0

    def move(blocks):
        if direct:
            return exchange(blocks, "replica")
        block = blocks[0].reshape(replicas, capacity, -1)
        block = lax.all_to_all(block, "replica", split_axis=0, concat_axis=0, tiled=True)
        return [block.reshape(slots, -1)]

    pieces = replicas if direct else 1
    piece = slots // pieces
    packed = call(
        functools.partial(pack_kernel, replicas, capacity, direct),
        "pack",
        [struct((piece, features + lanes), bf16)] * pieces,
        [adapter_replica, adapter_position.reshape(1, rows), activations],
        2 * rows * slots * features,
        in_specs=[VMEM] * 3,
        out_specs=[VMEM] * pieces,
    )
    got = move(packed)
    base = base_product(activations, value_matrix, parts)
    cached, fresh = attention(
        lengths, queries, cached_key_rows, cached_value_rows, incoming_keys
    )
    long = rows * (width // lanes) + slots
    rank_own, slot_ids, *messages = call(
        functools.partial(rank_kernel, pieces, adapters),
        "rank",
        [struct((slots, rank), f32), struct((slots, lanes), f32)]
        + [struct((long, lanes), bf16)] * (parts - 1),
        [*got, adapter_down_factors.reshape(adapters * rank, features), base],
        2 * slots * adapters * rank * features,
        in_specs=[VMEM] * (pieces + 2),
        out_specs=[VMEM] * (parts + 1),
    )
    heard = exchange([None, *messages], "tensor")[1:]
    up_local = lax.dynamic_slice_in_dim(
        adapter_up_factors, lax.axis_index("tensor") * width, width, 2
    ).reshape(adapters * rank, width)
    terms = call(
        functools.partial(up_kernel, parts - 1, adapters),
        "up",
        [struct((piece, width), bf16)] * pieces,
        [*heard, rank_own, slot_ids, up_local],
        4 * slots * adapters * rank * width,
        in_specs=[VMEM] * (parts + 2),
        out_specs=[VMEM] * pieces,
    )
    returned = move(terms)
    total = call(
        functools.partial(sum_kernel, parts - 1),
        "base_sum",
        [struct((rows, width), f32)],
        [*heard, base, value_offset_bias.reshape(1, width)],
        parts * rows * width,
        in_specs=[VMEM] * (parts + 1),
        out_specs=[VMEM],
    )[0]
    context, values = call(
        functools.partial(last_kernel, pieces, replicas, capacity, direct),
        "last",
        [struct(queries.shape, bf16), struct((rows, heads, size), bf16)],
        [*returned, adapter_replica, total, cached, fresh],
        2 * rows * slots * width,
        in_specs=[VMEM] * (pieces + 4),
        out_specs=[VMEM] * 2,
    )
    return (context, values)


def solution(mesh):
    rows = P(("groups", "replica"))
    split = P(("groups", "replica"), "tensor")
    in_specs = (
        split,
        P("tensor", None),
        P("tensor"),
        P(("groups", "replica"), None, "tensor"),
        rows,
        rows,
        rows,
        split,
        split,
        split,
        split,
        rows,
    )
    return jax.shard_map(
        per_device, mesh=mesh, in_specs=in_specs, out_specs=(split, split), check_vma=False
    )
```

time: 74 us -> 48.1 us (0.65)
  Pallas kernels: 0 us -> 24.7 us
  between operations: 14.2 us -> 0.78 us
  matrix products: 11.8 us -> 0 us
  blocking collectives: 10.3 us -> 0 us
  waiting for transfers between devices: 13.7 us -> 4.81 us
  other arithmetic: 4.25 us -> 0 us
  starting transfers between devices: 14.7 us -> 12.1 us
  local copies, waits for them, and re-layouts: 4.48 us -> 5.51 us
    pallas_call x0 -> x7, Pallas kernels: none -> 24.7 us  [call(): pl.pallas_call(kernel, name=name, out_shape=outs, cost_estimate=pl.CostEs...]
    all_to_all x3 -> x0, starting transfers between devices: 14.7 us -> none  [the longest x1 6.32 us: per_device(): lax.all_to_all(send_slots, 'replica', split_axis=0, concat_axis=0, tiled=...]
    all_to_all x3 -> x0, waiting for transfers between devices: 13.7 us -> none  [the longest x1 7.99 us: per_device(): lax.all_to_all(send_rows, 'replica', split_axis=0, concat_axis=0, tiled=T...]
    ppermute x0 -> x9, starting transfers between devices: none -> 12.1 us  [exchange(): lax.ppermute(block, axis, [(i, i ^ d + 1) for i in range(size)])]
    dot_general x7 -> x0, matrix products: 11.8 us -> none  [the longest x1 3.85 us: per_device(): jnp.dot(activations, value_matrix, preferred_element_type=jnp.float32)]
    psum x1 -> x0, blocking collectives: 10.3 us -> none  [per_device(): reduced = lax.psum(reduced, 'tensor')]
    unnamed x14 -> x25, local copies, waits for them, and re-layouts: 0.03 us -> 5.49 us
    ppermute x0 -> x9, waiting for transfers between devices: none -> 4.81 us  [exchange(): lax.ppermute(block, axis, [(i, i ^ d + 1) for i in range(size)])]
  transfers between devices with their start and end apart: 4 -> 9, of which waited for: 2 -> 4; matrix products, arithmetic and copies ran while one was open for 19% -> 0% of each run, Pallas kernels for 0% -> 46%
where the time goes in v1:
time: 48.1 us; the launch traced here: 47.9 us
  Pallas kernels  24.7 us (51%)
  starting transfers between devices  12.1 us (25%)
  local copies, waits for them, and re-layouts  5.51 us (11%)
  waiting for transfers between devices  4.81 us (10%)
  between operations  0.78 us (2%)
    pallas_call x7, Pallas kernels, call(): pl.pallas_call(kernel, name=name, out_shape=outs, cost_estimate=pl.CostEs...  24.7 us
    ppermute x9, starting transfers between devices, exchange(): lax.ppermute(block, axis, [(i, i ^ d + 1) for i in range(size)])  12.1 us
    unnamed x25, local copies, waits for them, and re-layouts  5.49 us
    ppermute x9, waiting for transfers between devices, exchange(): lax.ppermute(block, axis, [(i, i ^ d + 1) for i in range(size)])  4.81 us
  transfers between devices with their start and end apart: 9, of which 4 were waited for; matrix products, arithmetic and copies ran while one was open for 0% of the time, Pallas kernels for 46%

profile of v1, /device:TPU:0, one launch (start us, length us, event | category | flops | bytes accessed | tf_op | source)
XLA Modules:
  0.0 47.9 jit_solution(5440331178839998464)
XLA Ops:
  0.6 0.0 copy-start
  0.6 0.8 %copy.14.home_ref.refs_4_ = s32[32,1]{1,0:T(8,128)S(1)} copy(s32[32,1]{0,1:T(1,128)} %param.17) | data formatting | bytes 256 | tf_op args[5]
  1.4 0.0 copy-start.5
  1.4 0.9 %copy-done.5 = bf16[32,2048]{1,0:T(8,128)(2,1)S(1)} copy-done((bf16[32,2048]{1,0:T(8,128)(2,1)S(1)}, bf16[32,2048]{1,0:T(8,128)(2,1)}, u32[]{:S(2)}) %copy-start.5) | copy-done | bytes 131096
  2.3 0.0 copy-start.10
  2.3 0.7 %copy-done.10 = s32[32]{0:T(128)S(1)} copy-done((s32[32]{0:T(128)S(1)}, s32[32]{0:T(128)}, u32[]{:S(2)}) %copy-start.10) | copy-done | bytes 152
  3.0 0.6 %pack.1 = (bf16[16,2176]{1,0:T(8,128)(2,1)S(1)}, bf16[16,2176]{1,0:T(8,128)(2,1)S(1)}, bf16[16,2176]{1,0:T(8,128)(2,1)S(1)}, bf16[16,2176]{1,0:T(8,128)(2,1)S(1)}) custom-call(s32[32,1]{1,0:T(8,128)S(1)} %copy.14.home_ref.refs_4_, s32[1,32]{1,0:T(1,128)S(1)} %bitcast.7, bf16[32,2048]{1,0:T(8,128)(2,1)S(1)} %copy-done.5), custom_call_target="tpu_custom_call" | custom-call | flops 8388608 | bytes 409856 | tf_op jit(solution)/shard_map/pack/pallas_call | solution.py:20
  3.6 3.1 %collective-permute-start = (bf16[16,2176]{1,0:T(8,128)(2,1)S(1)}, bf16[16,2176]{1,0:T(8,128)(2,1)S(1)}, u32[]{:S(2)}, u32[]{:S(2)}) collective-permute-start(bf16[16,2176]{1,0:T(8,128)(2,1)S(1)} %get-tuple-element.18), channel_id=1, source_target_pairs={{0,4},{4,0},{8,12},{12,8},{1,5},{5,1},{9,13},{13,9},{2,6},{6,2},{1... | collective-permute-start | bytes 208904 | tf_op jit(solution)/shard_map/ppermute | solution.py:236
  6.7 2.6 %collective-permute-start.1 = (bf16[16,2176]{1,0:T(8,128)(2,1)S(1)}, bf16[16,2176]{1,0:T(8,128)(2,1)S(1)}, u32[]{:S(2)}, u32[]{:S(2)}) collective-permute-start(bf16[16,2176]{1,0:T(8,128)(2,1)S(1)} %get-tuple-element.19), channel_id=1, source_target_pairs={{0,8},{4,12},{8,0},{12,4},{1,9},{5,13},{9,1},{13,5},{2,10},{6,14},... | collective-permute-start | bytes 208904 | tf_op jit(solution)/shard_map/ppermute | solution.py:236
  9.3 0.0 collective-permute-start.2
  9.3 0.0 copy-start.1
  9.3 2.2 %copy-done.1 = bf16[2048,1024]{1,0:T(8,128)(2,1)S(1)} copy-done((bf16[2048,1024]{1,0:T(8,128)(2,1)S(1)}, bf16[2048,1024]{1,0:T(8,128)(2,1)}, u32[]{:S(2)}) %copy-start.1) | copy-done | bytes 4194328
  11.5 0.0 copy-start.6
  11.5 0.9 %copy-done.6 = bf16[32,2048]{1,0:T(8,128)(2,1)S(1)} copy-done((bf16[32,2048]{1,0:T(8,128)(2,1)S(1)}, bf16[32,2048]{1,0:T(8,128)(2,1)}, u32[]{:S(2)}) %copy-start.6) | copy-done | bytes 131096
  12.4 0.0 copy-start.4
  12.4 1.3 %base.1.refs_5_.refs_3_ = f32[4,32,256]{2,1,0:T(8,128)S(1)} custom-call(bf16[32,2048]{1,0:T(8,128)(2,1)S(1)} %copy-done.6, bf16[2048,1024]{1,0:T(8,128)(2,1)S(1)} %copy-done.1), custom_call_target="tpu_custom_call" | custom-call | flops 134217728 | bytes 4456448 | tf_op jit(solution)/shard_map/base/pallas_call | solution.py:20
  13.6 0.0 copy-start.2
  13.7 0.0 copy-start.7
  13.7 0.0 copy-start.8
  13.7 0.0 copy-start.11
  13.7 0.0 collective-permute-done.refs_1_
  13.7 0.5 %collective-permute-done.1.refs_2_ = bf16[16,2176]{1,0:T(8,128)(2,1)S(1)} collective-permute-done((bf16[16,2176]{1,0:T(8,128)(2,1)S(1)}, bf16[16,2176]{1,0:T(8,128)(2,1)S(1)}, u32[]{:S(2)}, u32[]{:S(2)}) %collective-permute-start.1) | collective-permute-done | bytes 69664 | tf_op jit(solution)/shard_map/ppermute | solution.py:236
  14.2 1.3 %collective-permute-done.2.refs_3_ = bf16[16,2176]{1,0:T(8,128)(2,1)S(1)} collective-permute-done((bf16[16,2176]{1,0:T(8,128)(2,1)S(1)}, bf16[16,2176]{1,0:T(8,128)(2,1)S(1)}, u32[]{:S(2)}, u32[]{:S(2)}) %collective-permute-start.2) | collective-permute-done | bytes 69664 | tf_op jit(solution)/shard_map/ppermute | solution.py:236
  15.5 0.0 copy-done.4
  15.5 0.6 %rank.1 = (f32[64,64]{1,0:T(8,128)S(1)}, f32[64,128]{1,0:T(8,128)S(1)}, bf16[128,128]{1,0:T(8,128)(2,1)S(1)}, bf16[128,128]{1,0:T(8,128)(2,1)S(1)}, bf16[128,128]{1,0:T(8,128)(2,1)S(1)}) custom-call(bf16[16,2176]{1,0:T(8,128)(2,1)S(1)} %get-tuple-element.17.refs_0_, bf16[16,2176]{1,0:T(8,128)(2,1)S(1)} %collective-permute-done.refs_1_, ...), custom_call_target="tpu_custom_call" | custom-call | flops 67108864 | bytes 1605632 | tf_op jit(solution)/shard_map/rank/pallas_call | solution.py:20
  16.1 0.1 collective-permute-start.3
  16.2 1.6 %collective-permute-start.4 = (bf16[128,128]{1,0:T(8,128)(2,1)S(1)}, bf16[128,128]{1,0:T(8,128)(2,1)S(1)}, u32[]{:S(2)}, u32[]{:S(2)}) collective-permute-start(bf16[128,128]{1,0:T(8,128)(2,1)S(1)} %get-tuple-element.22), channel_id=1, source_target_pairs={{0,2},{1,3},{2,0},{3,1},{4,6},{5,7},{6,4},{7,5},{8,10},{9,11},{10,... | collective-permute-start | bytes 98312 | tf_op jit(solution)/shard_map/ppermute | solution.py:236
  17.7 0.3 collective-permute-start.5
  18.0 0.0 copy-done
  18.1 0.0 collective-permute-done.3.refs_0_
  18.1 2.1 %collective-permute-done.4.refs_1_ = bf16[128,128]{1,0:T(8,128)(2,1)S(1)} collective-permute-done((bf16[128,128]{1,0:T(8,128)(2,1)S(1)}, bf16[128,128]{1,0:T(8,128)(2,1)S(1)}, u32[]{:S(2)}, u32[]{:S(2)}) %collective-permute-start.4) | collective-permute-done | bytes 32800 | tf_op jit(solution)/shard_map/ppermute | solution.py:236
  20.2 0.9 %collective-permute-done.5.refs_2_ = bf16[128,128]{1,0:T(8,128)(2,1)S(1)} collective-permute-done((bf16[128,128]{1,0:T(8,128)(2,1)S(1)}, bf16[128,128]{1,0:T(8,128)(2,1)S(1)}, u32[]{:S(2)}, u32[]{:S(2)}) %collective-permute-start.5) | collective-permute-done | bytes 32800 | tf_op jit(solution)/shard_map/ppermute | solution.py:236
  21.1 0.3 up.1
  21.4 0.8 %collective-permute-start.6 = (bf16[16,256]{1,0:T(8,128)(2,1)S(1)}, bf16[16,256]{1,0:T(8,128)(2,1)S(1)}, u32[]{:S(2)}, u32[]{:S(2)}) collective-permute-start(bf16[16,256]{1,0:T(8,128)(2,1)S(1)} %get-tuple-element.27), channel_id=1, source_target_pairs={{0,4},{4,0},{8,12},{12,8},{1,5},{5,1},{9,13},{13,9},{2,6},{6,2},{1... | collective-permute-start | bytes 24584 | tf_op jit(solution)/shard_map/ppermute | solution.py:236
  22.2 1.8 %collective-permute-start.7 = (bf16[16,256]{1,0:T(8,128)(2,1)S(1)}, bf16[16,256]{1,0:T(8,128)(2,1)S(1)}, u32[]{:S(2)}, u32[]{:S(2)}) collective-permute-start(bf16[16,256]{1,0:T(8,128)(2,1)S(1)} %get-tuple-element.28), channel_id=1, source_target_pairs={{0,8},{4,12},{8,0},{12,4},{1,9},{5,13},{9,1},{13,5},{2,10},{6,14},... | collective-permute-start | bytes 24584 | tf_op jit(solution)/shard_map/ppermute | solution.py:236
  24.1 0.0 copy-start.9
  24.1 1.8 %collective-permute-start.8 = (bf16[16,256]{1,0:T(8,128)(2,1)S(1)}, bf16[16,256]{1,0:T(8,128)(2,1)S(1)}, u32[]{:S(2)}, u32[]{:S(2)}) collective-permute-start(bf16[16,256]{1,0:T(8,128)(2,1)S(1)} %get-tuple-element.29), channel_id=1, source_target_pairs={{0,12},{4,8},{8,4},{12,0},{1,13},{5,9},{9,5},{13,1},{2,14},{6,10},... | collective-permute-start | bytes 24584 | tf_op jit(solution)/shard_map/ppermute | solution.py:236
  25.8 0.0 copy-done.3
  25.8 0.0 copy-done.2
  25.8 0.0 copy-done.7
  25.8 0.0 copy-done.8
  25.8 0.0 copy-done.11
  25.8 20.7 %attention.1 = (f32[32,16,128]{2,1,0:T(8,128)S(1)}, f32[32,16,128]{2,1,0:T(8,128)S(1)}) custom-call(s32[32]{0:T(128)S(1)} %copy-done.11, bf16[32,16,128]{2,1,0:T(8,128)(2,1)S(1)} %copy-done.7, bf16[32,2,96,128]{3,2,1,0:T(8,128)(2,1)S(1)} %copy-done.2, bf16[32,2,96,128]{3,2,1,0:T(8,128)(2,1)S(1)} %copy-done.3, bf16[32,2,128]{2,1,0:T(2,128)(2,1)S(1)} %copy-done.8), custom_call_target="tpu_custom_call" | custom-call | flops 25165824 | bytes 3817600 | tf_op jit(solution)/shard_map/attention/pallas_call | solution.py:20
  46.6 0.0 copy-done.9
  46.6 0.0 collective-permute-done.6.refs_1_
  46.7 0.0 collective-permute-done.7.refs_2_
  46.7 0.0 collective-permute-done.8.refs_3_
  46.7 1.2 %last.1 = (bf16[32,16,128]{2,1,0:T(8,128)(2,1)}, bf16[32,2,128]{2,1,0:T(2,128)(2,1)}) custom-call(bf16[16,256]{1,0:T(8,128)(2,1)S(1)} %get-tuple-element.26.refs_0_, bf16[16,256]{1,0:T(8,128)(2,1)S(1)} %collective-permute-done.6.refs_1_, bf16[16,256]{1,0:T(8,128)(2,1)S(1)} %collective-permute-done.7.refs_2_, ...), custom_call_target="tpu_custom_call" | custom-call | flops 1048576 | bytes 737408 | tf_op jit(solution)/shard_map/last/pallas_call | solution.py:20
  (3 shorter events, 0.1 us)
Async XLA Ops:
  0.6 17.4 %copy-start = (bf16[4,64,1024]{2,1,0:T(8,128)(2,1)S(1)}, bf16[4,64,1024]{2,1,0:T(8,128)(2,1)}, u32[]{:S(2)}) copy-start(bf16[4,64,1024]{2,1,0:T(8,128)(2,1)} %param.16) | copy-start | bytes 1572868
  1.4 0.9 %copy-start.5 = (bf16[32,2048]{1,0:T(8,128)(2,1)S(1)}, bf16[32,2048]{1,0:T(8,128)(2,1)}, u32[]{:S(2)}) copy-start(bf16[32,2048]{1,0:T(8,128)(2,1)} %rows_ref.3) | copy-start | bytes 393220
  2.3 0.7 %copy-start.10 = (s32[32]{0:T(128)S(1)}, s32[32]{0:T(128)}, u32[]{:S(2)}) copy-start(s32[32]{0:T(128)} %param.18) | copy-start | bytes 388
  3.6 10.1 %collective-permute-start = (bf16[16,2176]{1,0:T(8,128)(2,1)S(1)}, bf16[16,2176]{1,0:T(8,128)(2,1)S(1)}, u32[]{:S(2)}, u32[]{:S(2)}) collective-permute-start(bf16[16,2176]{1,0:T(8,128)(2,1)S(1)} %get-tuple-element.18), channel_id=1, source_target_pairs={{0,4},{4,0},{8,12},{12,8},{1,5},{5,1},{9,13},{13,9},{2,6},{6,2},{1... | collective-permute-start | bytes 208904 | tf_op jit(solution)/shard_map/ppermute | solution.py:236
  6.7 7.5 %collective-permute-start.1 = (bf16[16,2176]{1,0:T(8,128)(2,1)S(1)}, bf16[16,2176]{1,0:T(8,128)(2,1)S(1)}, u32[]{:S(2)}, u32[]{:S(2)}) collective-permute-start(bf16[16,2176]{1,0:T(8,128)(2,1)S(1)} %get-tuple-element.19), channel_id=1, source_target_pairs={{0,8},{4,12},{8,0},{12,4},{1,9},{5,13},{9,1},{13,5},{2,10},{6,14},... | collective-permute-start | bytes 208904 | tf_op jit(solution)/shard_map/ppermute | solution.py:236
  9.3 6.2 %collective-permute-start.2 = (bf16[16,2176]{1,0:T(8,128)(2,1)S(1)}, bf16[16,2176]{1,0:T(8,128)(2,1)S(1)}, u32[]{:S(2)}, u32[]{:S(2)}) collective-permute-start(bf16[16,2176]{1,0:T(8,128)(2,1)S(1)} %get-tuple-element.20), channel_id=1, source_target_pairs={{0,12},{4,8},{8,4},{12,0},{1,13},{5,9},{9,5},{13,1},{2,14},{6,10},... | collective-permute-start | bytes 208904 | tf_op jit(solution)/shard_map/ppermute | solution.py:236
  9.3 2.2 %copy-start.1 = (bf16[2048,1024]{1,0:T(8,128)(2,1)S(1)}, bf16[2048,1024]{1,0:T(8,128)(2,1)}, u32[]{:S(2)}) copy-start(bf16[2048,1024]{1,0:T(8,128)(2,1)} %matrix_ref.1) | copy-start | bytes 12582916
  11.5 0.9 %copy-start.6 = (bf16[32,2048]{1,0:T(8,128)(2,1)S(1)}, bf16[32,2048]{1,0:T(8,128)(2,1)}, u32[]{:S(2)}) copy-start(bf16[32,2048]{1,0:T(8,128)(2,1)} %rows_ref.3) | copy-start | bytes 393220
  12.4 3.1 %copy-start.4 = (bf16[4,64,2048]{2,1,0:T(8,128)(2,1)S(1)}, bf16[4,64,2048]{2,1,0:T(8,128)(2,1)}, u32[]{:S(2)}) copy-start(bf16[4,64,2048]{2,1,0:T(8,128)(2,1)} %param.15) | copy-start | bytes 3145732
  12.4 13.4 %copy-start.3 = (bf16[32,2,96,128]{3,2,1,0:T(8,128)(2,1)S(1)}, bf16[32,2,96,128]{3,2,1,0:T(8,128)(2,1)}, u32[]{:S(2)}) copy-start(bf16[32,2,96,128]{3,2,1,0:T(8,128)(2,1)} %value_ref.1) | copy-start | bytes 4718596
  13.6 12.2 %copy-start.2 = (bf16[32,2,96,128]{3,2,1,0:T(8,128)(2,1)S(1)}, bf16[32,2,96,128]{3,2,1,0:T(8,128)(2,1)}, u32[]{:S(2)}) copy-start(bf16[32,2,96,128]{3,2,1,0:T(8,128)(2,1)} %key_ref.1) | copy-start | bytes 4718596
  13.7 12.2 %copy-start.7 = (bf16[32,16,128]{2,1,0:T(8,128)(2,1)S(1)}, bf16[32,16,128]{2,1,0:T(8,128)(2,1)}, u32[]{:S(2)}) copy-start(bf16[32,16,128]{2,1,0:T(8,128)(2,1)} %query_ref.1) | copy-start | bytes 393220
  13.7 12.2 %copy-start.8 = (bf16[32,2,128]{2,1,0:T(2,128)(2,1)S(1)}, bf16[32,2,128]{2,1,0:T(2,128)(2,1)}, u32[]{:S(2)}) copy-start(bf16[32,2,128]{2,1,0:T(2,128)(2,1)} %new_ref.1) | copy-start | bytes 49156
  13.7 12.2 %copy-start.11 = (s32[32]{0:T(128)S(1)}, s32[32]{0:T(128)}, u32[]{:S(2)}) copy-start(s32[32]{0:T(128)} %length_ref.1) | copy-start | bytes 388
  16.1 2.0 %collective-permute-start.3 = (bf16[128,128]{1,0:T(8,128)(2,1)S(1)}, bf16[128,128]{1,0:T(8,128)(2,1)S(1)}, u32[]{:S(2)}, u32[]{:S(2)}) collective-permute-start(bf16[128,128]{1,0:T(8,128)(2,1)S(1)} %get-tuple-element.21), channel_id=1, source_target_pairs={{0,1},{1,0},{2,3},{3,2},{4,5},{5,4},{6,7},{7,6},{8,9},{9,8},{10,11... | collective-permute-start | bytes 98312 | tf_op jit(solution)/shard_map/ppermute | solution.py:236
  16.2 4.0 %collective-permute-start.4 = (bf16[128,128]{1,0:T(8,128)(2,1)S(1)}, bf16[128,128]{1,0:T(8,128)(2,1)S(1)}, u32[]{:S(2)}, u32[]{:S(2)}) collective-permute-start(bf16[128,128]{1,0:T(8,128)(2,1)S(1)} %get-tuple-element.22), channel_id=1, source_target_pairs={{0,2},{1,3},{2,0},{3,1},{4,6},{5,7},{6,4},{7,5},{8,10},{9,11},{10,... | collective-permute-start | bytes 98312 | tf_op jit(solution)/shard_map/ppermute | solution.py:236
  17.7 3.3 %collective-permute-start.5 = (bf16[128,128]{1,0:T(8,128)(2,1)S(1)}, bf16[128,128]{1,0:T(8,128)(2,1)S(1)}, u32[]{:S(2)}, u32[]{:S(2)}) collective-permute-start(bf16[128,128]{1,0:T(8,128)(2,1)S(1)} %get-tuple-element.23), channel_id=1, source_target_pairs={{0,3},{1,2},{2,1},{3,0},{4,7},{5,6},{6,5},{7,4},{8,11},{9,10},{10,... | collective-permute-start | bytes 98312 | tf_op jit(solution)/shard_map/ppermute | solution.py:236
  21.4 25.3 %collective-permute-start.6 = (bf16[16,256]{1,0:T(8,128)(2,1)S(1)}, bf16[16,256]{1,0:T(8,128)(2,1)S(1)}, u32[]{:S(2)}, u32[]{:S(2)}) collective-permute-start(bf16[16,256]{1,0:T(8,128)(2,1)S(1)} %get-tuple-element.27), channel_id=1, source_target_pairs={{0,4},{4,0},{8,12},{12,8},{1,5},{5,1},{9,13},{13,9},{2,6},{6,2},{1... | collective-permute-start | bytes 24584 | tf_op jit(solution)/shard_map/ppermute | solution.py:236
  22.2 24.4 %collective-permute-start.7 = (bf16[16,256]{1,0:T(8,128)(2,1)S(1)}, bf16[16,256]{1,0:T(8,128)(2,1)S(1)}, u32[]{:S(2)}, u32[]{:S(2)}) collective-permute-start(bf16[16,256]{1,0:T(8,128)(2,1)S(1)} %get-tuple-element.28), channel_id=1, source_target_pairs={{0,8},{4,12},{8,0},{12,4},{1,9},{5,13},{9,1},{13,5},{2,10},{6,14},... | collective-permute-start | bytes 24584 | tf_op jit(solution)/shard_map/ppermute | solution.py:236
  24.1 22.5 %copy-start.9 = (f32[256]{0:T(256)S(1)}, f32[256]{0:T(256)}, u32[]{:S(2)}) copy-start(f32[256]{0:T(256)} %param.14) | copy-start | bytes 3076
  24.1 22.6 %collective-permute-start.8 = (bf16[16,256]{1,0:T(8,128)(2,1)S(1)}, bf16[16,256]{1,0:T(8,128)(2,1)S(1)}, u32[]{:S(2)}, u32[]{:S(2)}) collective-permute-start(bf16[16,256]{1,0:T(8,128)(2,1)S(1)} %get-tuple-element.29), channel_id=1, source_target_pairs={{0,12},{4,8},{8,4},{12,0},{1,13},{5,9},{9,5},{13,1},{2,14},{6,10},... | collective-permute-start | bytes 24584 | tf_op jit(solution)/shard_map/ppermute | solution.py:236

commit v2 on v1

--- a/solution.py
+++ b/solution.py
@@ -12,9 +12,10 @@
 f32 = jnp.float32
 bf16 = jnp.bfloat16
 VMEM = pl.BlockSpec(memory_space=pltpu.VMEM)
-
-
-def call(kernel, name, outs, args, flops, limit=32 << 20, **more):
+HBM = pl.BlockSpec(memory_space=pltpu.HBM)
+
+
+def call(kernel, name, outs, args, flops, limit=16 << 20, **more):
     read = sum(a.size * a.dtype.itemsize for a in args)
     write = sum(o.size * o.dtype.itemsize for o in outs)
     return pl.pallas_call(
@@ -27,37 +28,57 @@
     )(*args)
 
 
+def stay(array):
+    return pltpu.with_memory_space_constraint(array, pltpu.HBM)
+
+
 def struct(shape, dtype):
     return jax.ShapeDtypeStruct(shape, dtype)
 
 
-def placement(home_ref, blocks, capacity, relative):
-    home = home_ref[...]
+def column(row):
+    count = row.shape[1]
+    square = lax.broadcasted_iota(jnp.int32, (count, count), 0) == lax.broadcasted_iota(
+        jnp.int32, (count, count), 1
+    )
+    return jnp.sum(jnp.where(square, row, 0), axis=1, keepdims=True)
+
+
+def placement(home_row, blocks, capacity, relative):
+    home = column(home_row)
     rows = home.shape[0]
     if relative:
         home = home ^ lax.axis_index("replica")
     hot = (home == lax.broadcasted_iota(jnp.int32, (rows, blocks), 1)).astype(f32)
-    row = lax.broadcasted_iota(jnp.int32, (rows, rows), 0)
-    column = lax.broadcasted_iota(jnp.int32, (rows, rows), 1)
-    below = (column < row).astype(bf16)
+    at = lax.broadcasted_iota(jnp.int32, (rows, rows), 0)
+    below = (lax.broadcasted_iota(jnp.int32, (rows, rows), 1) < at).astype(bf16)
     before = jnp.dot(below, hot.astype(bf16), preferred_element_type=f32)
     position = jnp.sum(before * hot, axis=1, keepdims=True).astype(jnp.int32)
     flat = home * capacity + position
     return flat == lax.broadcasted_iota(jnp.int32, (rows, blocks * capacity), 1)
 
 
-def pack_kernel(blocks, capacity, relative, home_ref, slot_ref, rows_ref, *outs):
-    place = placement(home_ref, blocks, capacity, relative)
+def pack_kernel(blocks, capacity, relative, home_hbm, slot_hbm, rows_hbm, rows_ref, *refs):
+    outs, (home_ref, slot_ref, semaphores) = refs[:-3], refs[-3:]
+    copies = [
+        pltpu.make_async_copy(source, target, semaphores.at[i])
+        for i, (source, target) in enumerate(
+            [(home_hbm, home_ref), (slot_hbm, slot_ref), (rows_hbm, rows_ref)]
+        )
+    ]
+    for copy in copies:
+        copy.start()
+    copies[0].wait()
+    place = placement(home_ref[...], blocks, capacity, relative)
     rows, width = rows_ref.shape
-    square = lax.broadcasted_iota(jnp.int32, (rows, rows), 0) == lax.broadcasted_iota(
-        jnp.int32, (rows, rows), 1
-    )
-    slot = jnp.sum(jnp.where(square, slot_ref[...], 0), axis=1, keepdims=True) + 1
-    spread = jnp.broadcast_to(slot.astype(f32), (rows, lanes)).astype(bf16)
+    copies[1].wait()
+    slot = (column(slot_ref[...]) + 1).astype(f32)
+    spread = jnp.broadcast_to(slot, (rows, lanes)).astype(bf16)
     turned = place.astype(f32).astype(bf16)
     over = (((0,), (0,)), ((), ()))
+    slots = lax.dot_general(turned, spread, over, preferred_element_type=f32).astype(bf16)
+    copies[2].wait()
     packed = lax.dot_general(turned, rows_ref[...], over, preferred_element_type=f32).astype(bf16)
-    slots = lax.dot_general(turned, spread, over, preferred_element_type=f32).astype(bf16)
     size = outs[0].shape[0]
     for b, out in enumerate(outs):
         out[:, :width] = packed[b * size : (b + 1) * size]
@@ -132,7 +153,7 @@
 def last_kernel(pieces, blocks, capacity, relative, *refs):
     got = refs[:pieces]
     home_ref, base_ref, cached_ref, fresh_ref, context_ref, values_ref = refs[pieces:]
-    place = placement(home_ref, blocks, capacity, relative).astype(f32).astype(bf16)
+    place = placement(home_ref[...], blocks, capacity, relative).astype(f32).astype(bf16)
     terms = jnp.concatenate([ref[...] for ref in got], axis=0)
     picked = jnp.dot(place, terms, preferred_element_type=f32)
     values = (base_ref[...] + picked).astype(bf16)
@@ -148,86 +169,75 @@
 
 def base_kernel(rows_ref, matrix_ref, out):
     parts, _, width = out.shape
-    product = jnp.dot(rows_ref[...], matrix_ref[...], preferred_element_type=f32)
-
-    @pl.when(pl.program_id(0) == 0)
-    def _():
-        for t in range(parts):
-            out[t] = product[:, t * width : (t + 1) * width]
-
-    @pl.when(pl.program_id(0) > 0)
-    def _():
-        for t in range(parts):
-            out[t] += product[:, t * width : (t + 1) * width]
-
-
-def attention_kernel(length_ref, query_ref, key_ref, value_ref, new_ref, cached_ref, fresh_ref):
-    requests, heads, length, size = key_ref.shape
-    group = query_ref.shape[1] // heads
-    scale = 1.0 / size**0.5
-    step = pl.program_id(0)
-    slot = lax.broadcasted_iota(jnp.int32, (group, length), 1)
-    for r in range(requests):
-        valid = slot < length_ref[step * requests + r]
-        for h in range(heads):
-            own = slice(h * group, (h + 1) * group)
-            query = query_ref[r, own, :]
-            across = (((1,), (1,)), ((), ()))
-            scores = lax.dot_general(query, key_ref[r, h], across, preferred_element_type=f32)
-            scores = jnp.where(valid, scores * scale, -1e30)
-            new = new_ref[r, h : h + 1, :].astype(f32)
-            fresh = jnp.sum(query.astype(f32) * new, axis=1, keepdims=True) * scale
-            top = jnp.maximum(jnp.max(scores, axis=1, keepdims=True), fresh)
-            weights = jnp.exp(scores - top)
-            alone = jnp.exp(fresh - top)
-            total = jnp.sum(weights, axis=1, keepdims=True) + alone
-            probs = (weights / total).astype(bf16)
-            cached_ref[r, own, :] = jnp.dot(probs, value_ref[r, h], preferred_element_type=f32)
-            share = jnp.broadcast_to(alone / total, (group, size))
-            fresh_ref[r, own, :] = share.astype(bf16).astype(f32)
-
-
-def attention(lengths, queries, keys, values, new_keys):
-    rows, heads, length, size = keys.shape
-    query_heads = queries.shape[1]
-    steps = 4
-    part = rows // steps
-    shape = (rows, query_heads, size)
-    q_spec = pl.BlockSpec((part, query_heads, size), lambda i, _: (i, 0, 0))
-    kv_spec = pl.BlockSpec((part, heads, length, size), lambda i, _: (i, 0, 0, 0))
-    n_spec = pl.BlockSpec((part, heads, size), lambda i, _: (i, 0, 0))
-    return call(
-        attention_kernel,
-        "attention",
-        [struct(shape, f32), struct(shape, f32)],
-        [lengths, queries, keys, values, new_keys],
-        4 * rows * query_heads * length * size,
-        grid_spec=pltpu.PrefetchScalarGridSpec(
-            num_scalar_prefetch=1,
-            grid=(steps,),
-            in_specs=[q_spec, kv_spec, kv_spec, n_spec],
-            out_specs=[q_spec, q_spec],
-        ),
-    )
+    for t in range(parts):
+        block = matrix_ref[:, t * width : (t + 1) * width]
+        out[t] = jnp.dot(rows_ref[...], block, preferred_element_type=f32)
 
 
 def base_product(rows, matrix, parts):
     count, depth = rows.shape
     width = matrix.shape[1] // parts
-    steps = 4
     return call(
         base_kernel,
         "base",
         [struct((parts, count, width), f32)],
         [rows, matrix],
         2 * count * depth * matrix.shape[1],
-        grid=(steps,),
-        in_specs=[
-            pl.BlockSpec((count, depth // steps), lambda i: (0, i)),
-            pl.BlockSpec((depth // steps, matrix.shape[1]), lambda i: (i, 0)),
+        in_specs=[VMEM] * 2,
+        out_specs=[VMEM],
+    )[0]
+
+
+def attention_kernel(
+    length_ref, query_ref, key_ref, value_ref, new_ref, cached_ref, fresh_ref, score_ref, prob_ref
+):
+    requests, heads, length, size = key_ref.shape
+    group = query_ref.shape[1] // heads
+    scale = 1.0 / size**0.5
+    count = requests * heads
+    across = (((1,), (1,)), ((), ()))
+    pairs = [(r, h) for r in range(requests) for h in range(heads)]
+    for i, (r, h) in enumerate(pairs):
+        query = query_ref[r, h * group : (h + 1) * group, :]
+        score_ref[i] = lax.dot_general(query, key_ref[r, h], across, preferred_element_type=f32)
+    filled = jnp.concatenate(
+        [jnp.full((heads, 1, length), length_ref[r], jnp.int32) for r in range(requests)], axis=0
+    )
+    valid = lax.broadcasted_iota(jnp.int32, (count, group, length), 2) < filled
+    scores = jnp.where(valid, score_ref[...] * scale, -1e30)
+    query = query_ref[...].reshape(count, group, size).astype(f32)
+    new = new_ref[...].astype(f32).reshape(count, 1, size)
+    fresh = jnp.sum(query * new, axis=2, keepdims=True) * scale
+    top = jnp.maximum(jnp.max(scores, axis=2, keepdims=True), fresh)
+    weights = jnp.exp(scores - top)
+    alone = jnp.exp(fresh - top)
+    total = jnp.sum(weights, axis=2, keepdims=True) + alone
+    prob_ref[...] = (weights / total).astype(bf16)
+    share = jnp.broadcast_to((alone / total).astype(bf16).astype(f32), (count, group, size))
+    fresh_ref[...] = share.reshape(requests, heads * group, size)
+    for i, (r, h) in enumerate(pairs):
+        own = slice(h * group, (h + 1) * group)
+        cached_ref[r, own, :] = jnp.dot(prob_ref[i], value_ref[r, h], preferred_element_type=f32)
+
+
+def attention(lengths, queries, keys, values, new_keys):
+    rows, heads, length, size = keys.shape
+    query_heads = queries.shape[1]
+    group = query_heads // heads
+    shape = struct((rows, query_heads, size), f32)
+    return call(
+        attention_kernel,
+        "attention",
+        [shape, shape],
+        [lengths, queries, keys, values, new_keys],
+        4 * rows * query_heads * length * size,
+        in_specs=[pl.BlockSpec(memory_space=pltpu.SMEM)] + [VMEM] * 4,
+        out_specs=[VMEM] * 2,
+        scratch_shapes=[
+            pltpu.VMEM((rows * heads, group, length), f32),
+            pltpu.VMEM((rows * heads, group, length), bf16),
         ],
-        out_specs=[pl.BlockSpec((parts, count, width), lambda i: (0, 0, 0))],
-    )[0]
+    )
 
 
 def exchange(blocks, axis):
@@ -262,6 +272,7 @@
     heads, size = incoming_keys.shape[1:]
     slots = replicas * capacity
     direct = capacity % 16 == 0
+    home_row = adapter_replica.reshape(1, rows)
 
     def move(blocks):
         if direct:
@@ -272,20 +283,26 @@
 
     pieces = replicas if direct else 1
     piece = slots // pieces
-    packed = call(
+    local_rows, *packed = call(
         functools.partial(pack_kernel, replicas, capacity, direct),
         "pack",
-        [struct((piece, features + lanes), bf16)] * pieces,
-        [adapter_replica, adapter_position.reshape(1, rows), activations],
-        2 * rows * slots * features,
-        in_specs=[VMEM] * 3,
-        out_specs=[VMEM] * pieces,
+        [struct(activations.shape, bf16)] + [struct((piece, features + lanes), bf16)] * pieces,
+        [stay(home_row), stay(adapter_position.reshape(1, rows)), stay(activations)],
+        4_000_000_000,
+        in_specs=[HBM] * 3,
+        out_specs=[VMEM] * (pieces + 1),
+        scratch_shapes=[
+            pltpu.VMEM((1, rows), jnp.int32),
+            pltpu.VMEM((1, rows), jnp.int32),
+            pltpu.SemaphoreType.DMA((3,)),
+        ],
     )
     got = move(packed)
-    base = base_product(activations, value_matrix, parts)
+    base = base_product(local_rows, value_matrix, parts)
     cached, fresh = attention(
         lengths, queries, cached_key_rows, cached_value_rows, incoming_keys
     )
+    base, cached, fresh = lax.optimization_barrier((base, cached, fresh))
     long = rows * (width // lanes) + slots
     rank_own, slot_ids, *messages = call(
         functools.partial(rank_kernel, pieces, adapters),
@@ -324,7 +341,7 @@
         functools.partial(last_kernel, pieces, replicas, capacity, direct),
         "last",
         [struct(queries.shape, bf16), struct((rows, heads, size), bf16)],
-        [*returned, adapter_replica, total, cached, fresh],
+        [*returned, home_row, total, cached, fresh],
         2 * rows * slots * width,
         in_specs=[VMEM] * (pieces + 4),
         out_specs=[VMEM] * 2,

time: 48.1 us -> 29.3 us (0.61)
  Pallas kernels: 24.7 us -> 6.33 us
  local copies, waits for them, and re-layouts: 5.51 us -> 0.06 us
  waiting for transfers between devices: 4.81 us -> 9.93 us
    pallas_call x7, Pallas kernels: 24.7 us -> 6.33 us  [call(): pl.pallas_call(kernel, name=name, out_shape=outs, cost_estimate=pl.CostEs...]
    unnamed x25 -> x20, local copies, waits for them, and re-layouts: 5.49 us -> 0.05 us
    ppermute x9, waiting for transfers between devices: 4.81 us -> 9.93 us  [exchange(): lax.ppermute(block, axis, [(i, i ^ d + 1) for i in range(size)])]
  transfers between devices with their start and end apart: 9 -> 9, of which waited for: 4 -> 6; matrix products, arithmetic and copies ran while one was open for 0% -> 0% of each run, Pallas kernels for 46% -> 9%
where the time goes in v2:
time: 29.3 us; the launch traced here: 29.2 us
  starting transfers between devices  12.1 us (41%)
  waiting for transfers between devices  9.93 us (34%)
  Pallas kernels  6.33 us (22%)
  between operations  0.8 us (3%)
    ppermute x9, starting transfers between devices, exchange(): lax.ppermute(block, axis, [(i, i ^ d + 1) for i in range(size)])  12.1 us
    ppermute x9, waiting for transfers between devices, exchange(): lax.ppermute(block, axis, [(i, i ^ d + 1) for i in range(size)])  9.93 us
    pallas_call x7, Pallas kernels, call(): pl.pallas_call(kernel, name=name, out_shape=outs, cost_estimate=pl.CostEs...  6.33 us
  transfers between devices with their start and end apart: 9, of which 6 were waited for; matrix products, arithmetic and copies ran while one was open for 0% of the time, Pallas kernels for 9%

profile of v2, /device:TPU:0, one launch (start us, length us, event | category | flops | bytes accessed | tf_op | source)
XLA Modules:
  0.0 29.2 jit_solution(12389188516510596637)
XLA Ops:
  0.6 0.0 copy-start
  0.6 0.0 copy-start.2
  0.7 0.0 copy-start.3
  0.7 0.0 copy-start.5
  0.7 0.0 copy-start.6
  0.7 0.0 copy-start.9
  0.7 0.0 copy-start.1
  0.7 1.5 %pack.1 = (bf16[32,2048]{1,0:T(8,128)(2,1)S(1)}, bf16[16,2176]{1,0:T(8,128)(2,1)S(1)}, bf16[16,2176]{1,0:T(8,128)(2,1)S(1)}, bf16[16,2176]{1,0:T(8,128)(2,1)S(1)}, bf16[16,2176]{1,0:T(8,128)(2,1)S(1)}) custom-call(s32[1,32]{1,0:T(1,128)} %bitcast.8, s32[1,32]{1,0:T(1,128)} %bitcast.10, bf16[32,2048]{1,0:T(8,128)(2,1)} %rows_hbm.1), custom_call_target="tpu_custom_call" | custom-call | flops 4000000000 | bytes 540928 | tf_op jit(solution)/shard_map/pack/pallas_call | solution.py:21
  2.3 3.1 %collective-permute-start = (bf16[16,2176]{1,0:T(8,128)(2,1)S(1)}, bf16[16,2176]{1,0:T(8,128)(2,1)S(1)}, u32[]{:S(2)}, u32[]{:S(2)}) collective-permute-start(bf16[16,2176]{1,0:T(8,128)(2,1)S(1)} %get-tuple-element.22), channel_id=1, source_target_pairs={{0,4},{4,0},{8,12},{12,8},{1,5},{5,1},{9,13},{13,9},{2,6},{6,2},{1... | collective-permute-start | bytes 208904 | tf_op jit(solution)/shard_map/ppermute | solution.py:246
  5.3 2.6 %collective-permute-start.1 = (bf16[16,2176]{1,0:T(8,128)(2,1)S(1)}, bf16[16,2176]{1,0:T(8,128)(2,1)S(1)}, u32[]{:S(2)}, u32[]{:S(2)}) collective-permute-start(bf16[16,2176]{1,0:T(8,128)(2,1)S(1)} %get-tuple-element.23), channel_id=1, source_target_pairs={{0,8},{4,12},{8,0},{12,4},{1,9},{5,13},{9,1},{13,5},{2,10},{6,14},... | collective-permute-start | bytes 208904 | tf_op jit(solution)/shard_map/ppermute | solution.py:246
  7.9 0.0 collective-permute-start.2
  7.9 0.0 copy-done.2
  7.9 0.0 copy-done.3
  7.9 0.0 copy-done.5
  8.0 0.0 copy-done.6
  8.0 0.0 copy-done.9
  8.0 1.9 %attention.1 = (f32[32,16,128]{2,1,0:T(8,128)S(1)}, f32[32,16,128]{2,1,0:T(8,128)S(1)}) custom-call(s32[32]{0:T(128)S(1)} %copy-done.9, bf16[32,16,128]{2,1,0:T(8,128)(2,1)S(1)} %copy-done.5, bf16[32,2,96,128]{3,2,1,0:T(8,128)(2,1)S(1)} %copy-done.2, bf16[32,2,96,128]{3,2,1,0:T(8,128)(2,1)S(1)} %copy-done.3, bf16[32,2,128]{2,1,0:T(2,128)(2,1)S(1)} %copy-done.6), custom_call_target="tpu_custom_call" | custom-call | flops 25165824 | bytes 3817600 | tf_op jit(solution)/shard_map/attention/pallas_call | solution.py:21
  9.9 0.0 copy-done.1
  9.9 0.0 copy-start.4
  9.9 0.8 %base.1.refs_5_.refs_3_ = f32[4,32,256]{2,1,0:T(8,128)S(1)} custom-call(bf16[32,2048]{1,0:T(8,128)(2,1)S(1)} %get-tuple-element.25.rows_ref, bf16[2048,1024]{1,0:T(8,128)(2,1)S(1)} %copy-done.1), custom_call_target="tpu_custom_call" | custom-call | flops 134217728 | bytes 4456448 | tf_op jit(solution)/shard_map/base/pallas_call | solution.py:21
  10.7 0.0 copy-start.7
  10.7 0.0 copy-start.8
  10.8 0.0 collective-permute-done.refs_1_
  10.8 2.1 %collective-permute-done.1.refs_2_ = bf16[16,2176]{1,0:T(8,128)(2,1)S(1)} collective-permute-done((bf16[16,2176]{1,0:T(8,128)(2,1)S(1)}, bf16[16,2176]{1,0:T(8,128)(2,1)S(1)}, u32[]{:S(2)}, u32[]{:S(2)}) %collective-permute-start.1) | collective-permute-done | bytes 69664 | tf_op jit(solution)/shard_map/ppermute | solution.py:246
  12.9 1.3 %collective-permute-done.2.refs_3_ = bf16[16,2176]{1,0:T(8,128)(2,1)S(1)} collective-permute-done((bf16[16,2176]{1,0:T(8,128)(2,1)S(1)}, bf16[16,2176]{1,0:T(8,128)(2,1)S(1)}, u32[]{:S(2)}, u32[]{:S(2)}) %collective-permute-start.2) | collective-permute-done | bytes 69664 | tf_op jit(solution)/shard_map/ppermute | solution.py:246
  14.1 0.0 copy-done.4
  14.2 0.6 %rank.1 = (f32[64,64]{1,0:T(8,128)S(1)}, f32[64,128]{1,0:T(8,128)S(1)}, bf16[128,128]{1,0:T(8,128)(2,1)S(1)}, bf16[128,128]{1,0:T(8,128)(2,1)S(1)}, bf16[128,128]{1,0:T(8,128)(2,1)S(1)}) custom-call(bf16[16,2176]{1,0:T(8,128)(2,1)S(1)} %get-tuple-element.21.refs_0_, bf16[16,2176]{1,0:T(8,128)(2,1)S(1)} %collective-permute-done.refs_1_, ...), custom_call_target="tpu_custom_call" | custom-call | flops 67108864 | bytes 1605632 | tf_op jit(solution)/shard_map/rank/pallas_call | solution.py:21
  14.7 0.1 collective-permute-start.3
  14.8 1.6 %collective-permute-start.4 = (bf16[128,128]{1,0:T(8,128)(2,1)S(1)}, bf16[128,128]{1,0:T(8,128)(2,1)S(1)}, u32[]{:S(2)}, u32[]{:S(2)}) collective-permute-start(bf16[128,128]{1,0:T(8,128)(2,1)S(1)} %get-tuple-element.30), channel_id=1, source_target_pairs={{0,2},{1,3},{2,0},{3,1},{4,6},{5,7},{6,4},{7,5},{8,10},{9,11},{10,... | collective-permute-start | bytes 98312 | tf_op jit(solution)/shard_map/ppermute | solution.py:246
  16.4 0.3 %collective-permute-start.5 = (bf16[128,128]{1,0:T(8,128)(2,1)S(1)}, bf16[128,128]{1,0:T(8,128)(2,1)S(1)}, u32[]{:S(2)}, u32[]{:S(2)}) collective-permute-start(bf16[128,128]{1,0:T(8,128)(2,1)S(1)} %get-tuple-element.31), channel_id=1, source_target_pairs={{0,3},{1,2},{2,1},{3,0},{4,7},{5,6},{6,5},{7,4},{8,11},{9,10},{10,... | collective-permute-start | bytes 98312 | tf_op jit(solution)/shard_map/ppermute | solution.py:246
  16.7 0.0 copy-done
  16.7 0.0 collective-permute-done.3.refs_0_
  16.7 2.1 %collective-permute-done.4.refs_1_ = bf16[128,128]{1,0:T(8,128)(2,1)S(1)} collective-permute-done((bf16[128,128]{1,0:T(8,128)(2,1)S(1)}, bf16[128,128]{1,0:T(8,128)(2,1)S(1)}, u32[]{:S(2)}, u32[]{:S(2)}) %collective-permute-start.4) | collective-permute-done | bytes 32800 | tf_op jit(solution)/shard_map/ppermute | solution.py:246
  18.8 0.9 %collective-permute-done.5.refs_2_ = bf16[128,128]{1,0:T(8,128)(2,1)S(1)} collective-permute-done((bf16[128,128]{1,0:T(8,128)(2,1)S(1)}, bf16[128,128]{1,0:T(8,128)(2,1)S(1)}, u32[]{:S(2)}, u32[]{:S(2)}) %collective-permute-start.5) | collective-permute-done | bytes 32800 | tf_op jit(solution)/shard_map/ppermute | solution.py:246
  19.7 0.3 up.1
  20.0 0.8 %collective-permute-start.6 = (bf16[16,256]{1,0:T(8,128)(2,1)S(1)}, bf16[16,256]{1,0:T(8,128)(2,1)S(1)}, u32[]{:S(2)}, u32[]{:S(2)}) collective-permute-start(bf16[16,256]{1,0:T(8,128)(2,1)S(1)} %get-tuple-element.35), channel_id=1, source_target_pairs={{0,4},{4,0},{8,12},{12,8},{1,5},{5,1},{9,13},{13,9},{2,6},{6,2},{1... | collective-permute-start | bytes 24584 | tf_op jit(solution)/shard_map/ppermute | solution.py:246
  20.9 1.7 %collective-permute-start.7 = (bf16[16,256]{1,0:T(8,128)(2,1)S(1)}, bf16[16,256]{1,0:T(8,128)(2,1)S(1)}, u32[]{:S(2)}, u32[]{:S(2)}) collective-permute-start(bf16[16,256]{1,0:T(8,128)(2,1)S(1)} %get-tuple-element.36), channel_id=1, source_target_pairs={{0,8},{4,12},{8,0},{12,4},{1,9},{5,13},{9,1},{13,5},{2,10},{6,14},... | collective-permute-start | bytes 24584 | tf_op jit(solution)/shard_map/ppermute | solution.py:246
  22.6 1.9 %collective-permute-start.8 = (bf16[16,256]{1,0:T(8,128)(2,1)S(1)}, bf16[16,256]{1,0:T(8,128)(2,1)S(1)}, u32[]{:S(2)}, u32[]{:S(2)}) collective-permute-start(bf16[16,256]{1,0:T(8,128)(2,1)S(1)} %get-tuple-element.37), channel_id=1, source_target_pairs={{0,12},{4,8},{8,4},{12,0},{1,13},{5,9},{9,5},{13,1},{2,14},{6,10},... | collective-permute-start | bytes 24584 | tf_op jit(solution)/shard_map/ppermute | solution.py:246
  24.5 0.0 copy-done.7
  24.5 0.0 collective-permute-done.6.refs_1_
  24.5 0.9 %collective-permute-done.7.refs_2_ = bf16[16,256]{1,0:T(8,128)(2,1)S(1)} collective-permute-done((bf16[16,256]{1,0:T(8,128)(2,1)S(1)}, bf16[16,256]{1,0:T(8,128)(2,1)S(1)}, u32[]{:S(2)}, u32[]{:S(2)}) %collective-permute-start.7) | collective-permute-done | bytes 8224 | tf_op jit(solution)/shard_map/ppermute | solution.py:246
  25.4 2.6 %collective-permute-done.8.refs_3_ = bf16[16,256]{1,0:T(8,128)(2,1)S(1)} collective-permute-done((bf16[16,256]{1,0:T(8,128)(2,1)S(1)}, bf16[16,256]{1,0:T(8,128)(2,1)S(1)}, u32[]{:S(2)}, u32[]{:S(2)}) %collective-permute-start.8) | collective-permute-done | bytes 8224 | tf_op jit(solution)/shard_map/ppermute | solution.py:246
  28.0 0.0 copy-done.8
  28.0 1.1 %last.1 = (bf16[32,16,128]{2,1,0:T(8,128)(2,1)}, bf16[32,2,128]{2,1,0:T(2,128)(2,1)}) custom-call(bf16[16,256]{1,0:T(8,128)(2,1)S(1)} %get-tuple-element.34.refs_0_, bf16[16,256]{1,0:T(8,128)(2,1)S(1)} %collective-permute-done.6.refs_1_, bf16[16,256]{1,0:T(8,128)(2,1)S(1)} %collective-permute-done.7.refs_2_, ...), custom_call_target="tpu_custom_call" | custom-call | flops 1048576 | bytes 737408 | tf_op jit(solution)/shard_map/last/pallas_call | solution.py:21
  (2 shorter events, 0.0 us)
Async XLA Ops:
  0.6 16.1 %copy-start = (bf16[4,64,1024]{2,1,0:T(8,128)(2,1)S(1)}, bf16[4,64,1024]{2,1,0:T(8,128)(2,1)}, u32[]{:S(2)}) copy-start(bf16[4,64,1024]{2,1,0:T(8,128)(2,1)} %param.16) | copy-start | bytes 1572868
  0.6 7.3 %copy-start.2 = (bf16[32,2,96,128]{3,2,1,0:T(8,128)(2,1)S(1)}, bf16[32,2,96,128]{3,2,1,0:T(8,128)(2,1)}, u32[]{:S(2)}) copy-start(bf16[32,2,96,128]{3,2,1,0:T(8,128)(2,1)} %key_ref.1) | copy-start | bytes 4718596
  0.7 7.3 %copy-start.3 = (bf16[32,2,96,128]{3,2,1,0:T(8,128)(2,1)S(1)}, bf16[32,2,96,128]{3,2,1,0:T(8,128)(2,1)}, u32[]{:S(2)}) copy-start(bf16[32,2,96,128]{3,2,1,0:T(8,128)(2,1)} %value_ref.1) | copy-start | bytes 4718596
  0.7 7.3 %copy-start.5 = (bf16[32,16,128]{2,1,0:T(8,128)(2,1)S(1)}, bf16[32,16,128]{2,1,0:T(8,128)(2,1)}, u32[]{:S(2)}) copy-start(bf16[32,16,128]{2,1,0:T(8,128)(2,1)} %query_ref.1) | copy-start | bytes 393220
  0.7 7.3 %copy-start.6 = (bf16[32,2,128]{2,1,0:T(2,128)(2,1)S(1)}, bf16[32,2,128]{2,1,0:T(2,128)(2,1)}, u32[]{:S(2)}) copy-start(bf16[32,2,128]{2,1,0:T(2,128)(2,1)} %new_ref.1) | copy-start | bytes 49156
  0.7 7.3 %copy-start.9 = (s32[32]{0:T(128)S(1)}, s32[32]{0:T(128)}, u32[]{:S(2)}) copy-start(s32[32]{0:T(128)} %length_ref.1) | copy-start | bytes 388
  0.7 9.2 %copy-start.1 = (bf16[2048,1024]{1,0:T(8,128)(2,1)S(1)}, bf16[2048,1024]{1,0:T(8,128)(2,1)}, u32[]{:S(2)}) copy-start(bf16[2048,1024]{1,0:T(8,128)(2,1)} %matrix_ref.1) | copy-start | bytes 12582916
  2.3 8.5 %collective-permute-start = (bf16[16,2176]{1,0:T(8,128)(2,1)S(1)}, bf16[16,2176]{1,0:T(8,128)(2,1)S(1)}, u32[]{:S(2)}, u32[]{:S(2)}) collective-permute-start(bf16[16,2176]{1,0:T(8,128)(2,1)S(1)} %get-tuple-element.22), channel_id=1, source_target_pairs={{0,4},{4,0},{8,12},{12,8},{1,5},{5,1},{9,13},{13,9},{2,6},{6,2},{1... | collective-permute-start | bytes 208904 | tf_op jit(solution)/shard_map/ppermute | solution.py:246
  5.3 7.5 %collective-permute-start.1 = (bf16[16,2176]{1,0:T(8,128)(2,1)S(1)}, bf16[16,2176]{1,0:T(8,128)(2,1)S(1)}, u32[]{:S(2)}, u32[]{:S(2)}) collective-permute-start(bf16[16,2176]{1,0:T(8,128)(2,1)S(1)} %get-tuple-element.23), channel_id=1, source_target_pairs={{0,8},{4,12},{8,0},{12,4},{1,9},{5,13},{9,1},{13,5},{2,10},{6,14},... | collective-permute-start | bytes 208904 | tf_op jit(solution)/shard_map/ppermute | solution.py:246
  7.9 6.2 %collective-permute-start.2 = (bf16[16,2176]{1,0:T(8,128)(2,1)S(1)}, bf16[16,2176]{1,0:T(8,128)(2,1)S(1)}, u32[]{:S(2)}, u32[]{:S(2)}) collective-permute-start(bf16[16,2176]{1,0:T(8,128)(2,1)S(1)} %get-tuple-element.24), channel_id=1, source_target_pairs={{0,12},{4,8},{8,4},{12,0},{1,13},{5,9},{9,5},{13,1},{2,14},{6,10},... | collective-permute-start | bytes 208904 | tf_op jit(solution)/shard_map/ppermute | solution.py:246
  9.9 4.3 %copy-start.4 = (bf16[4,64,2048]{2,1,0:T(8,128)(2,1)S(1)}, bf16[4,64,2048]{2,1,0:T(8,128)(2,1)}, u32[]{:S(2)}) copy-start(bf16[4,64,2048]{2,1,0:T(8,128)(2,1)} %param.15) | copy-start | bytes 3145732
  10.7 13.7 %copy-start.7 = (f32[256]{0:T(256)S(1)}, f32[256]{0:T(256)}, u32[]{:S(2)}) copy-start(f32[256]{0:T(256)} %param.14) | copy-start | bytes 3076
  10.7 17.3 %copy-start.8 = (s32[32,1]{0,1:T(1,128)S(1)}, s32[32,1]{0,1:T(1,128)}, u32[]{:S(2)}) copy-start(s32[32,1]{0,1:T(1,128)} %param.17) | copy-start | bytes 388
  14.7 2.0 %collective-permute-start.3 = (bf16[128,128]{1,0:T(8,128)(2,1)S(1)}, bf16[128,128]{1,0:T(8,128)(2,1)S(1)}, u32[]{:S(2)}, u32[]{:S(2)}) collective-permute-start(bf16[128,128]{1,0:T(8,128)(2,1)S(1)} %get-tuple-element.29), channel_id=1, source_target_pairs={{0,1},{1,0},{2,3},{3,2},{4,5},{5,4},{6,7},{7,6},{8,9},{9,8},{10,11... | collective-permute-start | bytes 98312 | tf_op jit(solution)/shard_map/ppermute | solution.py:246
  14.8 4.0 %collective-permute-start.4 = (bf16[128,128]{1,0:T(8,128)(2,1)S(1)}, bf16[128,128]{1,0:T(8,128)(2,1)S(1)}, u32[]{:S(2)}, u32[]{:S(2)}) collective-permute-start(bf16[128,128]{1,0:T(8,128)(2,1)S(1)} %get-tuple-element.30), channel_id=1, source_target_pairs={{0,2},{1,3},{2,0},{3,1},{4,6},{5,7},{6,4},{7,5},{8,10},{9,11},{10,... | collective-permute-start | bytes 98312 | tf_op jit(solution)/shard_map/ppermute | solution.py:246
  16.4 3.3 %collective-permute-start.5 = (bf16[128,128]{1,0:T(8,128)(2,1)S(1)}, bf16[128,128]{1,0:T(8,128)(2,1)S(1)}, u32[]{:S(2)}, u32[]{:S(2)}) collective-permute-start(bf16[128,128]{1,0:T(8,128)(2,1)S(1)} %get-tuple-element.31), channel_id=1, source_target_pairs={{0,3},{1,2},{2,1},{3,0},{4,7},{5,6},{6,5},{7,4},{8,11},{9,10},{10,... | collective-permute-start | bytes 98312 | tf_op jit(solution)/shard_map/ppermute | solution.py:246
  20.0 4.5 %collective-permute-start.6 = (bf16[16,256]{1,0:T(8,128)(2,1)S(1)}, bf16[16,256]{1,0:T(8,128)(2,1)S(1)}, u32[]{:S(2)}, u32[]{:S(2)}) collective-permute-start(bf16[16,256]{1,0:T(8,128)(2,1)S(1)} %get-tuple-element.35), channel_id=1, source_target_pairs={{0,4},{4,0},{8,12},{12,8},{1,5},{5,1},{9,13},{13,9},{2,6},{6,2},{1... | collective-permute-start | bytes 24584 | tf_op jit(solution)/shard_map/ppermute | solution.py:246
  20.9 4.5 %collective-permute-start.7 = (bf16[16,256]{1,0:T(8,128)(2,1)S(1)}, bf16[16,256]{1,0:T(8,128)(2,1)S(1)}, u32[]{:S(2)}, u32[]{:S(2)}) collective-permute-start(bf16[16,256]{1,0:T(8,128)(2,1)S(1)} %get-tuple-element.36), channel_id=1, source_target_pairs={{0,8},{4,12},{8,0},{12,4},{1,9},{5,13},{9,1},{13,5},{2,10},{6,14},... | collective-permute-start | bytes 24584 | tf_op jit(solution)/shard_map/ppermute | solution.py:246
  22.6 5.4 %collective-permute-start.8 = (bf16[16,256]{1,0:T(8,128)(2,1)S(1)}, bf16[16,256]{1,0:T(8,128)(2,1)S(1)}, u32[]{:S(2)}, u32[]{:S(2)}) collective-permute-start(bf16[16,256]{1,0:T(8,128)(2,1)S(1)} %get-tuple-element.37), channel_id=1, source_target_pairs={{0,12},{4,8},{8,4},{12,0},{1,13},{5,9},{9,5},{13,1},{2,14},{6,10},... | collective-permute-start | bytes 24584 | tf_op jit(solution)/shard_map/ppermute | solution.py:246

commit v3 on v2

--- a/solution.py
+++ b/solution.py
@@ -8,6 +8,7 @@
 from jax.sharding import PartitionSpec as P
 
 adapter_scale = 0.5
+pack_cost = 40_000_000_000
 lanes = 128
 f32 = jnp.float32
 bf16 = jnp.bfloat16
@@ -44,11 +45,22 @@
     return jnp.sum(jnp.where(square, row, 0), axis=1, keepdims=True)
 
 
-def placement(home_row, blocks, capacity, relative):
+def orders(blocks):
+    if blocks == 4:
+        return [0, 2, 1, 3], [0, 2, 1, 3]
+    return list(range(blocks)), list(range(blocks))
+
+
+def placement(home_row, blocks, capacity, relative, ordered):
     home = column(home_row)
     rows = home.shape[0]
     if relative:
-        home = home ^ lax.axis_index("replica")
+        step = home ^ lax.axis_index("replica")
+        home = step
+        if ordered:
+            odd = lax.axis_index("tensor") % 2 == 1
+            for at, (a, b) in enumerate(zip(*orders(blocks))):
+                home = jnp.where(step == jnp.where(odd, b, a), at, home)
     hot = (home == lax.broadcasted_iota(jnp.int32, (rows, blocks), 1)).astype(f32)
     at = lax.broadcasted_iota(jnp.int32, (rows, rows), 0)
     below = (lax.broadcasted_iota(jnp.int32, (rows, rows), 1) < at).astype(bf16)
@@ -69,7 +81,7 @@
     for copy in copies:
         copy.start()
     copies[0].wait()
-    place = placement(home_ref[...], blocks, capacity, relative)
+    place = placement(home_ref[...], blocks, capacity, relative, True)
     rows, width = rows_ref.shape
     copies[1].wait()
     slot = (column(slot_ref[...]) + 1).astype(f32)
@@ -115,7 +127,7 @@
         message[at:, :] = pair
 
 
-def up_kernel(peers, adapters, *refs):
+def up_kernel(peers, adapters, crossing, *refs):
     got = refs[:peers]
     rank_ref, slot_ref, up_ref = refs[peers : peers + 3]
     outs = refs[peers + 3 :]
@@ -130,17 +142,31 @@
     )
     upper = wide.astype(bf16)
     lower = (wide - upper.astype(f32)).astype(bf16)
-    term = jnp.dot(upper, up_ref[...], preferred_element_type=f32)
-    term = adapter_scale * (term + jnp.dot(lower, up_ref[...], preferred_element_type=f32))
-    term = term.astype(bf16)
+    half = outs[0].shape[1]
+    first = pl.multiple_of(lax.axis_index("tensor") // 2 * 2 * half, 2 * half)
+    factor = up_ref[:, pl.ds(first, 2 * half)]
+    term = jnp.dot(upper, factor, preferred_element_type=f32)
+    term = adapter_scale * (term + jnp.dot(lower, factor, preferred_element_type=f32))
+    term = term.astype(bf16).astype(f32)
+    odd = lax.axis_index("tensor") % 2 == 1
+    own = jnp.where(odd, term[:, half:], term[:, :half])
+    if not crossing:
+        outs[0][...] = own.astype(bf16)
+        return
+    other = jnp.where(odd, term[:, :half], term[:, half:])
     size = outs[0].shape[0]
-    for b, out in enumerate(outs):
-        out[...] = term[b * size : (b + 1) * size]
-
-
-def sum_kernel(peers, *refs):
+    outs[0][...] = own[:size].astype(bf16)
+    even_order, odd_order = orders(len(outs))
+    for d in range(1, len(outs)):
+        a, b = even_order.index(d) * size, odd_order.index(d) * size
+        outs[d][...] = jnp.where(odd, other[b : b + size], other[a : a + size]).astype(bf16)
+
+
+def sum_kernel(peers, blocks, capacity, relative, *refs):
     got = refs[:peers]
-    base_ref, bias_ref, out = refs[peers:]
+    base_ref, bias_ref, home_ref, out, place_ref = refs[peers:]
+    place = placement(home_ref[...], blocks, capacity, relative, False)
+    place_ref[...] = place.astype(f32).astype(bf16)
     total = base_ref[lax.axis_index("tensor")] + bias_ref[...]
     rows = total.shape[0]
     for c in range(total.shape[1] // lanes):
@@ -150,12 +176,11 @@
         out[:, c * lanes : (c + 1) * lanes] = part
 
 
-def last_kernel(pieces, blocks, capacity, relative, *refs):
+def last_kernel(pieces, *refs):
     got = refs[:pieces]
-    home_ref, base_ref, cached_ref, fresh_ref, context_ref, values_ref = refs[pieces:]
-    place = placement(home_ref[...], blocks, capacity, relative).astype(f32).astype(bf16)
+    place_ref, base_ref, cached_ref, fresh_ref, context_ref, values_ref = refs[pieces:]
     terms = jnp.concatenate([ref[...] for ref in got], axis=0)
-    picked = jnp.dot(place, terms, preferred_element_type=f32)
+    picked = jnp.dot(place_ref[...], terms, preferred_element_type=f32)
     values = (base_ref[...] + picked).astype(bf16)
     heads, size = values_ref.shape[1:]
     group = cached_ref.shape[1] // heads
@@ -240,13 +265,14 @@
     )
 
 
-def exchange(blocks, axis):
-    size = lax.axis_size(axis)
-    got = [
-        lax.ppermute(block, axis, [(i, i ^ (d + 1)) for i in range(size)])
-        for d, block in enumerate(blocks[1:])
-    ]
-    return [blocks[0]] + got
+def send(block, target):
+    replicas, parts = lax.axis_size("replica"), lax.axis_size("tensor")
+    pairs = []
+    for r in range(replicas):
+        for t in range(parts):
+            to_r, to_t = target(r, t)
+            pairs.append((r * parts + t, to_r * parts + to_t))
+    return lax.ppermute(block, ("replica", "tensor"), pairs)
 
 
 def per_device(
@@ -274,12 +300,10 @@
     direct = capacity % 16 == 0
     home_row = adapter_replica.reshape(1, rows)
 
-    def move(blocks):
-        if direct:
-            return exchange(blocks, "replica")
-        block = blocks[0].reshape(replicas, capacity, -1)
+    def shuffle(block):
+        block = block.reshape(replicas, capacity, -1)
         block = lax.all_to_all(block, "replica", split_axis=0, concat_axis=0, tiled=True)
-        return [block.reshape(slots, -1)]
+        return block.reshape(slots, -1)
 
     pieces = replicas if direct else 1
     piece = slots // pieces
@@ -288,7 +312,7 @@
         "pack",
         [struct(activations.shape, bf16)] + [struct((piece, features + lanes), bf16)] * pieces,
         [stay(home_row), stay(adapter_position.reshape(1, rows)), stay(activations)],
-        4_000_000_000,
+        pack_cost,
         in_specs=[HBM] * 3,
         out_specs=[VMEM] * (pieces + 1),
         scratch_shapes=[
@@ -297,7 +321,12 @@
             pltpu.SemaphoreType.DMA((3,)),
         ],
     )
-    got = move(packed)
+    if direct:
+        got = packed[:1]
+        for block, a, b in list(zip(packed, *orders(replicas)))[1:]:
+            got.append(send(block, lambda r, t: (r ^ (b if t % 2 else a), t)))
+    else:
+        got = [shuffle(packed[0])]
     base = base_product(local_rows, value_matrix, parts)
     cached, fresh = attention(
         lengths, queries, cached_key_rows, cached_value_rows, incoming_keys
@@ -314,34 +343,37 @@
         in_specs=[VMEM] * (pieces + 2),
         out_specs=[VMEM] * (parts + 1),
     )
-    heard = exchange([None, *messages], "tensor")[1:]
-    up_local = lax.dynamic_slice_in_dim(
-        adapter_up_factors, lax.axis_index("tensor") * width, width, 2
-    ).reshape(adapters * rank, width)
+    heard = [send(m, lambda r, t: (r, t ^ (d + 1))) for d, m in enumerate(messages)]
+    up_rows = adapter_up_factors.reshape(adapters * rank, parts * width)
     terms = call(
-        functools.partial(up_kernel, parts - 1, adapters),
+        functools.partial(up_kernel, parts - 1, adapters, direct),
         "up",
         [struct((piece, width), bf16)] * pieces,
-        [*heard, rank_own, slot_ids, up_local],
-        4 * slots * adapters * rank * width,
+        [*heard, rank_own, slot_ids, up_rows],
+        8 * slots * adapters * rank * width,
         in_specs=[VMEM] * (parts + 2),
         out_specs=[VMEM] * pieces,
     )
-    returned = move(terms)
-    total = call(
-        functools.partial(sum_kernel, parts - 1),
+    if direct:
+        returned = [terms[0]]
+        for d in range(1, replicas):
+            returned.append(send(terms[d], lambda r, t: (r ^ d, t ^ 1)))
+    else:
+        returned = [shuffle(terms[0])]
+    total, place = call(
+        functools.partial(sum_kernel, parts - 1, replicas, capacity, direct),
         "base_sum",
-        [struct((rows, width), f32)],
-        [*heard, base, value_offset_bias.reshape(1, width)],
+        [struct((rows, width), f32), struct((rows, slots), bf16)],
+        [*heard, base, value_offset_bias.reshape(1, width), home_row],
         parts * rows * width,
-        in_specs=[VMEM] * (parts + 1),
-        out_specs=[VMEM],
-    )[0]
+        in_specs=[VMEM] * (parts + 2),
+        out_specs=[VMEM] * 2,
+    )
     context, values = call(
-        functools.partial(last_kernel, pieces, replicas, capacity, direct),
+        functools.partial(last_kernel, pieces),
         "last",
         [struct(queries.shape, bf16), struct((rows, heads, size), bf16)],
-        [*returned, home_row, total, cached, fresh],
+        [*returned, place, total, cached, fresh],
         2 * rows * slots * width,
         in_specs=[VMEM] * (pieces + 4),
         out_specs=[VMEM] * 2,

time: 29.3 us -> 27.6 us (0.942)
  waiting for transfers between devices: 9.93 us -> 8.7 us
  starting transfers between devices: 12.1 us -> 11.6 us
    ppermute x9, waiting for transfers between devices: 9.93 us -> 8.7 us  [send(): return lax.ppermute(block, ('replica', 'tensor'), pairs)]
    ppermute x9, starting transfers between devices: 12.1 us -> 11.6 us  [send(): return lax.ppermute(block, ('replica', 'tensor'), pairs)]
  transfers between devices with their start and end apart: 9 -> 9, of which waited for: 6 -> 4; matrix products, arithmetic and copies ran while one was open for 0% -> 0% of each run, Pallas kernels for 9% -> 11%
where the time goes in v3:
time: 27.6 us; the launch traced here: 27.5 us
  starting transfers between devices  11.6 us (42%)
  waiting for transfers between devices  8.7 us (32%)
  Pallas kernels  6.37 us (23%)
  between operations  0.81 us (3%)
    ppermute x9, starting transfers between devices, send(): return lax.ppermute(block, ('replica', 'tensor'), pairs)  11.6 us
    ppermute x9, waiting for transfers between devices, send(): return lax.ppermute(block, ('replica', 'tensor'), pairs)  8.7 us
    pallas_call x7, Pallas kernels, call(): pl.pallas_call(kernel, name=name, out_shape=outs, cost_estimate=pl.CostEs...  6.37 us
  transfers between devices with their start and end apart: 9, of which 4 were waited for; matrix products, arithmetic and copies ran while one was open for 0% of the time, Pallas kernels for 11%

profile of v3, /device:TPU:0, one launch (start us, length us, event | category | flops | bytes accessed | tf_op | source)
XLA Modules:
  0.0 27.5 jit_solution(15619507061155934994)
XLA Ops:
  0.6 0.0 copy-start.1
  0.6 0.0 copy-start.2
  0.7 0.0 copy-start.5
  0.7 0.0 copy-start.6
  0.7 0.0 copy-start.9
  0.7 0.0 copy-start
  0.7 1.5 %pack.1 = (bf16[32,2048]{1,0:T(8,128)(2,1)S(1)}, bf16[16,2176]{1,0:T(8,128)(2,1)S(1)}, bf16[16,2176]{1,0:T(8,128)(2,1)S(1)}, bf16[16,2176]{1,0:T(8,128)(2,1)S(1)}, bf16[16,2176]{1,0:T(8,128)(2,1)S(1)}) custom-call(s32[1,32]{1,0:T(1,128)} %bitcast.8, s32[1,32]{1,0:T(1,128)} %bitcast.10, bf16[32,2048]{1,0:T(8,128)(2,1)} %rows_hbm.1), custom_call_target="tpu_custom_call" | custom-call | flops 40000000000 | bytes 540928 | tf_op jit(solution)/shard_map/pack/pallas_call | solution.py:22
  2.2 4.1 %collective-permute-start = (bf16[16,2176]{1,0:T(8,128)(2,1)S(1)}, bf16[16,2176]{1,0:T(8,128)(2,1)S(1)}, u32[]{:S(2)}, u32[]{:S(2)}) collective-permute-start(bf16[16,2176]{1,0:T(8,128)(2,1)S(1)} %get-tuple-element.24), channel_id=1, source_target_pairs={{0,8},{1,9},{2,10},{3,11},{4,12},{5,13},{6,14},{7,15},{8,0},{9,1},... | collective-permute-start | bytes 208904 | tf_op jit(solution)/shard_map/ppermute | solution.py:275
  6.3 1.6 %collective-permute-start.1 = (bf16[16,2176]{1,0:T(8,128)(2,1)S(1)}, bf16[16,2176]{1,0:T(8,128)(2,1)S(1)}, u32[]{:S(2)}, u32[]{:S(2)}) collective-permute-start(bf16[16,2176]{1,0:T(8,128)(2,1)S(1)} %get-tuple-element.25), channel_id=1, source_target_pairs={{0,4},{1,5},{2,6},{3,7},{4,0},{5,1},{6,2},{7,3},{8,12},{9,13},{10,... | collective-permute-start | bytes 208904 | tf_op jit(solution)/shard_map/ppermute | solution.py:275
  7.9 0.0 collective-permute-start.2
  7.9 0.0 copy-done.1
  7.9 0.0 copy-done.2
  7.9 0.0 copy-done.5
  8.0 0.0 copy-done.6
  8.0 0.0 copy-done.9
  8.0 1.9 %attention.1 = (f32[32,16,128]{2,1,0:T(8,128)S(1)}, f32[32,16,128]{2,1,0:T(8,128)S(1)}) custom-call(s32[32]{0:T(128)S(1)} %copy-done.9, bf16[32,16,128]{2,1,0:T(8,128)(2,1)S(1)} %copy-done.5, bf16[32,2,96,128]{3,2,1,0:T(8,128)(2,1)S(1)} %copy-done.1, bf16[32,2,96,128]{3,2,1,0:T(8,128)(2,1)S(1)} %copy-done.2, bf16[32,2,128]{2,1,0:T(2,128)(2,1)S(1)} %copy-done.6), custom_call_target="tpu_custom_call" | custom-call | flops 25165824 | bytes 3817600 | tf_op jit(solution)/shard_map/attention/pallas_call | solution.py:22
  9.9 0.0 copy-done
  9.9 0.0 copy-start.3
  9.9 0.8 %base.1.refs_5_.refs_3_ = f32[4,32,256]{2,1,0:T(8,128)S(1)} custom-call(bf16[32,2048]{1,0:T(8,128)(2,1)S(1)} %get-tuple-element.27.rows_ref, bf16[2048,1024]{1,0:T(8,128)(2,1)S(1)} %copy-done), custom_call_target="tpu_custom_call" | custom-call | flops 134217728 | bytes 4456448 | tf_op jit(solution)/shard_map/base/pallas_call | solution.py:22
  10.7 0.0 copy-start.4
  10.7 0.0 copy-start.7
  10.8 0.0 copy-start.8
  10.8 0.0 collective-permute-done.refs_1_
  10.8 0.0 collective-permute-done.1.refs_2_
  10.8 3.3 %collective-permute-done.2.refs_3_ = bf16[16,2176]{1,0:T(8,128)(2,1)S(1)} collective-permute-done((bf16[16,2176]{1,0:T(8,128)(2,1)S(1)}, bf16[16,2176]{1,0:T(8,128)(2,1)S(1)}, u32[]{:S(2)}, u32[]{:S(2)}) %collective-permute-start.2) | collective-permute-done | bytes 69664 | tf_op jit(solution)/shard_map/ppermute | solution.py:275
  14.0 0.0 copy-done.3
  14.0 0.6 %rank.1 = (f32[64,64]{1,0:T(8,128)S(1)}, f32[64,128]{1,0:T(8,128)S(1)}, bf16[128,128]{1,0:T(8,128)(2,1)S(1)}, bf16[128,128]{1,0:T(8,128)(2,1)S(1)}, bf16[128,128]{1,0:T(8,128)(2,1)S(1)}) custom-call(bf16[16,2176]{1,0:T(8,128)(2,1)S(1)} %get-tuple-element.23.refs_0_, bf16[16,2176]{1,0:T(8,128)(2,1)S(1)} %collective-permute-done.refs_1_, ...), custom_call_target="tpu_custom_call" | custom-call | flops 67108864 | bytes 1605632 | tf_op jit(solution)/shard_map/rank/pallas_call | solution.py:22
  14.6 0.1 collective-permute-start.3
  14.7 1.5 %collective-permute-start.4 = (bf16[128,128]{1,0:T(8,128)(2,1)S(1)}, bf16[128,128]{1,0:T(8,128)(2,1)S(1)}, u32[]{:S(2)}, u32[]{:S(2)}) collective-permute-start(bf16[128,128]{1,0:T(8,128)(2,1)S(1)} %get-tuple-element.32), channel_id=1, source_target_pairs={{0,2},{1,3},{2,0},{3,1},{4,6},{5,7},{6,4},{7,5},{8,10},{9,11},{10,... | collective-permute-start | bytes 98312 | tf_op jit(solution)/shard_map/ppermute | solution.py:275
  16.3 0.3 %collective-permute-start.5 = (bf16[128,128]{1,0:T(8,128)(2,1)S(1)}, bf16[128,128]{1,0:T(8,128)(2,1)S(1)}, u32[]{:S(2)}, u32[]{:S(2)}) collective-permute-start(bf16[128,128]{1,0:T(8,128)(2,1)S(1)} %get-tuple-element.33), channel_id=1, source_target_pairs={{0,3},{1,2},{2,1},{3,0},{4,7},{5,6},{6,5},{7,4},{8,11},{9,10},{10,... | collective-permute-start | bytes 98312 | tf_op jit(solution)/shard_map/ppermute | solution.py:275
  16.6 0.0 collective-permute-done.3.refs_0_
  16.6 2.1 %collective-permute-done.4.refs_1_ = bf16[128,128]{1,0:T(8,128)(2,1)S(1)} collective-permute-done((bf16[128,128]{1,0:T(8,128)(2,1)S(1)}, bf16[128,128]{1,0:T(8,128)(2,1)S(1)}, u32[]{:S(2)}, u32[]{:S(2)}) %collective-permute-start.4) | collective-permute-done | bytes 32800 | tf_op jit(solution)/shard_map/ppermute | solution.py:275
  18.7 0.9 %collective-permute-done.5.refs_2_ = bf16[128,128]{1,0:T(8,128)(2,1)S(1)} collective-permute-done((bf16[128,128]{1,0:T(8,128)(2,1)S(1)}, bf16[128,128]{1,0:T(8,128)(2,1)S(1)}, u32[]{:S(2)}, u32[]{:S(2)}) %collective-permute-start.5) | collective-permute-done | bytes 32800 | tf_op jit(solution)/shard_map/ppermute | solution.py:275
  19.6 0.0 copy-done.4
  19.6 0.3 %up.1 = (bf16[16,256]{1,0:T(8,128)(2,1)S(1)}, bf16[16,256]{1,0:T(8,128)(2,1)S(1)}, bf16[16,256]{1,0:T(8,128)(2,1)S(1)}, bf16[16,256]{1,0:T(8,128)(2,1)S(1)}) custom-call(bf16[128,128]{1,0:T(8,128)(2,1)S(1)} %collective-permute-done.3.refs_0_, bf16[128,128]{1,0:T(8,128)(2,1)S(1)} %collective-permute-done.4.refs_1_, ...), custom_call_target="tpu_custom_call" | custom-call | flops 33554432 | bytes 704512 | tf_op jit(solution)/shard_map/up/pallas_call | solution.py:22
  19.9 0.1 collective-permute-start.6
  20.0 1.7 %collective-permute-start.7 = (bf16[16,256]{1,0:T(8,128)(2,1)S(1)}, bf16[16,256]{1,0:T(8,128)(2,1)S(1)}, u32[]{:S(2)}, u32[]{:S(2)}) collective-permute-start(bf16[16,256]{1,0:T(8,128)(2,1)S(1)} %get-tuple-element.38), channel_id=1, source_target_pairs={{0,9},{1,8},{2,11},{3,10},{4,13},{5,12},{6,15},{7,14},{8,1},{9,0},... | collective-permute-start | bytes 24584 | tf_op jit(solution)/shard_map/ppermute | solution.py:275
  21.7 2.2 %collective-permute-start.8 = (bf16[16,256]{1,0:T(8,128)(2,1)S(1)}, bf16[16,256]{1,0:T(8,128)(2,1)S(1)}, u32[]{:S(2)}, u32[]{:S(2)}) collective-permute-start(bf16[16,256]{1,0:T(8,128)(2,1)S(1)} %get-tuple-element.39), channel_id=1, source_target_pairs={{0,13},{1,12},{2,15},{3,14},{4,9},{5,8},{6,11},{7,10},{8,5},{9,4},... | collective-permute-start | bytes 24584 | tf_op jit(solution)/shard_map/ppermute | solution.py:275
  23.9 0.0 copy-done.7
  23.9 0.0 copy-done.8
  23.9 0.3 %base_sum.1 = (f32[32,256]{1,0:T(8,128)S(1)}, bf16[32,64]{1,0:T(8,128)(2,1)S(1)}) custom-call(bf16[128,128]{1,0:T(8,128)(2,1)S(1)} %collective-permute-done.3.refs_0_, bf16[128,128]{1,0:T(8,128)(2,1)S(1)} %collective-permute-done.4.refs_1_, bf16[128,128]{1,0:T(8,128)(2,1)S(1)} %collective-permute-done.5.refs_2_, f32[4,32,256]{2,1,0:T(8,128)S(1)} %base.1.refs_5_.refs_3_, ...), custom_call_target="tpu_custom_call" | custom-call | flops 32768 | bytes 267392 | tf_op jit(solution)/shard_map/base_sum/pallas_call | solution.py:22
  24.2 0.0 collective-permute-done.6.refs_1_
  24.2 0.0 collective-permute-done.7.refs_2_
  24.2 2.4 %collective-permute-done.8.refs_3_ = bf16[16,256]{1,0:T(8,128)(2,1)S(1)} collective-permute-done((bf16[16,256]{1,0:T(8,128)(2,1)S(1)}, bf16[16,256]{1,0:T(8,128)(2,1)S(1)}, u32[]{:S(2)}, u32[]{:S(2)}) %collective-permute-start.8) | collective-permute-done | bytes 8224 | tf_op jit(solution)/shard_map/ppermute | solution.py:275
  26.6 0.9 %last.1 = (bf16[32,16,128]{2,1,0:T(8,128)(2,1)}, bf16[32,2,128]{2,1,0:T(2,128)(2,1)}) custom-call(bf16[16,256]{1,0:T(8,128)(2,1)S(1)} %get-tuple-element.36.refs_0_, bf16[16,256]{1,0:T(8,128)(2,1)S(1)} %collective-permute-done.6.refs_1_, bf16[16,256]{1,0:T(8,128)(2,1)S(1)} %collective-permute-done.7.refs_2_, ...), custom_call_target="tpu_custom_call" | custom-call | flops 1048576 | bytes 741376 | tf_op jit(solution)/shard_map/last/pallas_call | solution.py:22
Async XLA Ops:
  0.6 7.3 %copy-start.1 = (bf16[32,2,96,128]{3,2,1,0:T(8,128)(2,1)S(1)}, bf16[32,2,96,128]{3,2,1,0:T(8,128)(2,1)}, u32[]{:S(2)}) copy-start(bf16[32,2,96,128]{3,2,1,0:T(8,128)(2,1)} %key_ref.1) | copy-start | bytes 4718596
  0.6 7.3 %copy-start.2 = (bf16[32,2,96,128]{3,2,1,0:T(8,128)(2,1)S(1)}, bf16[32,2,96,128]{3,2,1,0:T(8,128)(2,1)}, u32[]{:S(2)}) copy-start(bf16[32,2,96,128]{3,2,1,0:T(8,128)(2,1)} %value_ref.1) | copy-start | bytes 4718596
  0.7 7.3 %copy-start.5 = (bf16[32,16,128]{2,1,0:T(8,128)(2,1)S(1)}, bf16[32,16,128]{2,1,0:T(8,128)(2,1)}, u32[]{:S(2)}) copy-start(bf16[32,16,128]{2,1,0:T(8,128)(2,1)} %query_ref.1) | copy-start | bytes 393220
  0.7 7.3 %copy-start.6 = (bf16[32,2,128]{2,1,0:T(2,128)(2,1)S(1)}, bf16[32,2,128]{2,1,0:T(2,128)(2,1)}, u32[]{:S(2)}) copy-start(bf16[32,2,128]{2,1,0:T(2,128)(2,1)} %new_ref.1) | copy-start | bytes 49156
  0.7 7.3 %copy-start.9 = (s32[32]{0:T(128)S(1)}, s32[32]{0:T(128)}, u32[]{:S(2)}) copy-start(s32[32]{0:T(128)} %length_ref.1) | copy-start | bytes 388
  0.7 9.2 %copy-start = (bf16[2048,1024]{1,0:T(8,128)(2,1)S(1)}, bf16[2048,1024]{1,0:T(8,128)(2,1)}, u32[]{:S(2)}) copy-start(bf16[2048,1024]{1,0:T(8,128)(2,1)} %matrix_ref.1) | copy-start | bytes 12582916
  2.2 8.5 %collective-permute-start = (bf16[16,2176]{1,0:T(8,128)(2,1)S(1)}, bf16[16,2176]{1,0:T(8,128)(2,1)S(1)}, u32[]{:S(2)}, u32[]{:S(2)}) collective-permute-start(bf16[16,2176]{1,0:T(8,128)(2,1)S(1)} %get-tuple-element.24), channel_id=1, source_target_pairs={{0,8},{1,9},{2,10},{3,11},{4,12},{5,13},{6,14},{7,15},{8,0},{9,1},... | collective-permute-start | bytes 208904 | tf_op jit(solution)/shard_map/ppermute | solution.py:275
  6.3 4.4 %collective-permute-start.1 = (bf16[16,2176]{1,0:T(8,128)(2,1)S(1)}, bf16[16,2176]{1,0:T(8,128)(2,1)S(1)}, u32[]{:S(2)}, u32[]{:S(2)}) collective-permute-start(bf16[16,2176]{1,0:T(8,128)(2,1)S(1)} %get-tuple-element.25), channel_id=1, source_target_pairs={{0,4},{1,5},{2,6},{3,7},{4,0},{5,1},{6,2},{7,3},{8,12},{9,13},{10,... | collective-permute-start | bytes 208904 | tf_op jit(solution)/shard_map/ppermute | solution.py:275
  7.9 6.1 %collective-permute-start.2 = (bf16[16,2176]{1,0:T(8,128)(2,1)S(1)}, bf16[16,2176]{1,0:T(8,128)(2,1)S(1)}, u32[]{:S(2)}, u32[]{:S(2)}) collective-permute-start(bf16[16,2176]{1,0:T(8,128)(2,1)S(1)} %get-tuple-element.26), channel_id=1, source_target_pairs={{0,12},{1,13},{2,14},{3,15},{4,8},{5,9},{6,10},{7,11},{8,4},{9,5},... | collective-permute-start | bytes 208904 | tf_op jit(solution)/shard_map/ppermute | solution.py:275
  9.9 4.1 %copy-start.3 = (bf16[4,64,2048]{2,1,0:T(8,128)(2,1)S(1)}, bf16[4,64,2048]{2,1,0:T(8,128)(2,1)}, u32[]{:S(2)}) copy-start(bf16[4,64,2048]{2,1,0:T(8,128)(2,1)} %param.15) | copy-start | bytes 3145732
  10.7 8.9 %copy-start.4 = (bf16[4,64,1024]{2,1,0:T(8,128)(2,1)S(1)}, bf16[4,64,1024]{2,1,0:T(8,128)(2,1)}, u32[]{:S(2)}) copy-start(bf16[4,64,1024]{2,1,0:T(8,128)(2,1)} %param.16) | copy-start | bytes 1572868
  10.7 13.1 %copy-start.7 = (f32[256]{0:T(256)S(1)}, f32[256]{0:T(256)}, u32[]{:S(2)}) copy-start(f32[256]{0:T(256)} %param.14) | copy-start | bytes 3076
  10.8 13.1 %copy-start.8 = (s32[32,1]{0,1:T(1,128)S(1)}, s32[32,1]{0,1:T(1,128)}, u32[]{:S(2)}) copy-start(s32[32,1]{0,1:T(1,128)} %param.17) | copy-start | bytes 388
  14.6 1.9 %collective-permute-start.3 = (bf16[128,128]{1,0:T(8,128)(2,1)S(1)}, bf16[128,128]{1,0:T(8,128)(2,1)S(1)}, u32[]{:S(2)}, u32[]{:S(2)}) collective-permute-start(bf16[128,128]{1,0:T(8,128)(2,1)S(1)} %get-tuple-element.31), channel_id=1, source_target_pairs={{0,1},{1,0},{2,3},{3,2},{4,5},{5,4},{6,7},{7,6},{8,9},{9,8},{10,11... | collective-permute-start | bytes 98312 | tf_op jit(solution)/shard_map/ppermute | solution.py:275
  14.7 4.0 %collective-permute-start.4 = (bf16[128,128]{1,0:T(8,128)(2,1)S(1)}, bf16[128,128]{1,0:T(8,128)(2,1)S(1)}, u32[]{:S(2)}, u32[]{:S(2)}) collective-permute-start(bf16[128,128]{1,0:T(8,128)(2,1)S(1)} %get-tuple-element.32), channel_id=1, source_target_pairs={{0,2},{1,3},{2,0},{3,1},{4,6},{5,7},{6,4},{7,5},{8,10},{9,11},{10,... | collective-permute-start | bytes 98312 | tf_op jit(solution)/shard_map/ppermute | solution.py:275
  16.3 3.3 %collective-permute-start.5 = (bf16[128,128]{1,0:T(8,128)(2,1)S(1)}, bf16[128,128]{1,0:T(8,128)(2,1)S(1)}, u32[]{:S(2)}, u32[]{:S(2)}) collective-permute-start(bf16[128,128]{1,0:T(8,128)(2,1)S(1)} %get-tuple-element.33), channel_id=1, source_target_pairs={{0,3},{1,2},{2,1},{3,0},{4,7},{5,6},{6,5},{7,4},{8,11},{9,10},{10,... | collective-permute-start | bytes 98312 | tf_op jit(solution)/shard_map/ppermute | solution.py:275
  19.9 4.2 %collective-permute-start.6 = (bf16[16,256]{1,0:T(8,128)(2,1)S(1)}, bf16[16,256]{1,0:T(8,128)(2,1)S(1)}, u32[]{:S(2)}, u32[]{:S(2)}) collective-permute-start(bf16[16,256]{1,0:T(8,128)(2,1)S(1)} %get-tuple-element.37), channel_id=1, source_target_pairs={{0,5},{1,4},{2,7},{3,6},{4,1},{5,0},{6,3},{7,2},{8,13},{9,12},{10,... | collective-permute-start | bytes 24584 | tf_op jit(solution)/shard_map/ppermute | solution.py:275
  20.0 4.2 %collective-permute-start.7 = (bf16[16,256]{1,0:T(8,128)(2,1)S(1)}, bf16[16,256]{1,0:T(8,128)(2,1)S(1)}, u32[]{:S(2)}, u32[]{:S(2)}) collective-permute-start(bf16[16,256]{1,0:T(8,128)(2,1)S(1)} %get-tuple-element.38), channel_id=1, source_target_pairs={{0,9},{1,8},{2,11},{3,10},{4,13},{5,12},{6,15},{7,14},{8,1},{9,0},... | collective-permute-start | bytes 24584 | tf_op jit(solution)/shard_map/ppermute | solution.py:275
  21.7 4.9 %collective-permute-start.8 = (bf16[16,256]{1,0:T(8,128)(2,1)S(1)}, bf16[16,256]{1,0:T(8,128)(2,1)S(1)}, u32[]{:S(2)}, u32[]{:S(2)}) collective-permute-start(bf16[16,256]{1,0:T(8,128)(2,1)S(1)} %get-tuple-element.39), channel_id=1, source_target_pairs={{0,13},{1,12},{2,15},{3,14},{4,9},{5,8},{6,11},{7,10},{8,5},{9,4},... | collective-permute-start | bytes 24584 | tf_op jit(solution)/shard_map/ppermute | solution.py:275

commit v4 on v3

--- a/solution.py
+++ b/solution.py
@@ -49,6 +49,14 @@
     if blocks == 4:
         return [0, 2, 1, 3], [0, 2, 1, 3]
     return list(range(blocks)), list(range(blocks))
+
+
+def tensor_order(parts):
+    return [3, 2, 1] if parts == 4 else list(range(1, parts))
+
+
+def return_order(pieces):
+    return [3, 2, 1] if pieces == 4 else list(range(1, pieces))
 
 
 def placement(home_row, blocks, capacity, relative, ordered):
@@ -179,7 +187,8 @@
 def last_kernel(pieces, *refs):
     got = refs[:pieces]
     place_ref, base_ref, cached_ref, fresh_ref, context_ref, values_ref = refs[pieces:]
-    terms = jnp.concatenate([ref[...] for ref in got], axis=0)
+    at = [0] + [1 + return_order(pieces).index(d) for d in range(1, pieces)]
+    terms = jnp.concatenate([got[i][...] for i in at], axis=0)
     picked = jnp.dot(place_ref[...], terms, preferred_element_type=f32)
     values = (base_ref[...] + picked).astype(bf16)
     heads, size = values_ref.shape[1:]
@@ -343,7 +352,7 @@
         in_specs=[VMEM] * (pieces + 2),
         out_specs=[VMEM] * (parts + 1),
     )
-    heard = [send(m, lambda r, t: (r, t ^ (d + 1))) for d, m in enumerate(messages)]
+    heard = [send(messages[d - 1], lambda r, t: (r, t ^ d)) for d in tensor_order(parts)]
     up_rows = adapter_up_factors.reshape(adapters * rank, parts * width)
     terms = call(
         functools.partial(up_kernel, parts - 1, adapters, direct),
@@ -356,7 +365,7 @@
     )
     if direct:
         returned = [terms[0]]
-        for d in range(1, replicas):
+        for d in return_order(replicas):
             returned.append(send(terms[d], lambda r, t: (r ^ d, t ^ 1)))
     else:
         returned = [shuffle(terms[0])]

time: 27.6 us -> 25.7 us (0.931)
  waiting for transfers between devices: 8.7 us -> 6.62 us
    ppermute x9, waiting for transfers between devices: 8.7 us -> 6.62 us  [send(): return lax.ppermute(block, ('replica', 'tensor'), pairs)]
  transfers between devices with their start and end apart: 9 -> 9, of which waited for: 4 -> 6; matrix products, arithmetic and copies ran while one was open for 0% -> 0% of each run, Pallas kernels for 11% -> 12%
where the time goes in v4:
time: 25.7 us; the launch traced here: 25.5 us
  starting transfers between devices  11.7 us (46%)
  waiting for transfers between devices  6.62 us (26%)
  Pallas kernels  6.37 us (25%)
  between operations  0.79 us (3%)
    ppermute x9, starting transfers between devices, send(): return lax.ppermute(block, ('replica', 'tensor'), pairs)  11.7 us
    ppermute x9, waiting for transfers between devices, send(): return lax.ppermute(block, ('replica', 'tensor'), pairs)  6.62 us
    pallas_call x7, Pallas kernels, call(): pl.pallas_call(kernel, name=name, out_shape=outs, cost_estimate=pl.CostEs...  6.37 us
  transfers between devices with their start and end apart: 9, of which 6 were waited for; matrix products, arithmetic and copies ran while one was open for 0% of the time, Pallas kernels for 12%

profile of v4, /device:TPU:0, one launch (start us, length us, event | category | flops | bytes accessed | tf_op | source)
XLA Modules:
  0.0 25.5 jit_solution(16548164575054186102)
XLA Ops:
  0.6 0.0 copy-start.1
  0.6 0.0 copy-start.2
  0.7 0.0 copy-start.5
  0.7 0.0 copy-start.6
  0.7 0.0 copy-start.9
  0.7 0.0 copy-start
  0.7 1.5 %pack.1 = (bf16[32,2048]{1,0:T(8,128)(2,1)S(1)}, bf16[16,2176]{1,0:T(8,128)(2,1)S(1)}, bf16[16,2176]{1,0:T(8,128)(2,1)S(1)}, bf16[16,2176]{1,0:T(8,128)(2,1)S(1)}, bf16[16,2176]{1,0:T(8,128)(2,1)S(1)}) custom-call(s32[1,32]{1,0:T(1,128)} %bitcast.8, s32[1,32]{1,0:T(1,128)} %bitcast.10, bf16[32,2048]{1,0:T(8,128)(2,1)} %rows_hbm.1), custom_call_target="tpu_custom_call" | custom-call | flops 40000000000 | bytes 540928 | tf_op jit(solution)/shard_map/pack/pallas_call | solution.py:22
  2.2 4.1 %collective-permute-start = (bf16[16,2176]{1,0:T(8,128)(2,1)S(1)}, bf16[16,2176]{1,0:T(8,128)(2,1)S(1)}, u32[]{:S(2)}, u32[]{:S(2)}) collective-permute-start(bf16[16,2176]{1,0:T(8,128)(2,1)S(1)} %get-tuple-element.24), channel_id=1, source_target_pairs={{0,8},{1,9},{2,10},{3,11},{4,12},{5,13},{6,14},{7,15},{8,0},{9,1},... | collective-permute-start | bytes 208904 | tf_op jit(solution)/shard_map/ppermute | solution.py:284
  6.3 1.6 %collective-permute-start.1 = (bf16[16,2176]{1,0:T(8,128)(2,1)S(1)}, bf16[16,2176]{1,0:T(8,128)(2,1)S(1)}, u32[]{:S(2)}, u32[]{:S(2)}) collective-permute-start(bf16[16,2176]{1,0:T(8,128)(2,1)S(1)} %get-tuple-element.25), channel_id=1, source_target_pairs={{0,4},{1,5},{2,6},{3,7},{4,0},{5,1},{6,2},{7,3},{8,12},{9,13},{10,... | collective-permute-start | bytes 208904 | tf_op jit(solution)/shard_map/ppermute | solution.py:284
  7.9 0.0 collective-permute-start.2
  7.9 0.0 copy-done.1
  7.9 0.0 copy-done.2
  7.9 0.0 copy-done.5
  8.0 0.0 copy-done.6
  8.0 0.0 copy-done.9
  8.0 1.9 %attention.1 = (f32[32,16,128]{2,1,0:T(8,128)S(1)}, f32[32,16,128]{2,1,0:T(8,128)S(1)}) custom-call(s32[32]{0:T(128)S(1)} %copy-done.9, bf16[32,16,128]{2,1,0:T(8,128)(2,1)S(1)} %copy-done.5, bf16[32,2,96,128]{3,2,1,0:T(8,128)(2,1)S(1)} %copy-done.1, bf16[32,2,96,128]{3,2,1,0:T(8,128)(2,1)S(1)} %copy-done.2, bf16[32,2,128]{2,1,0:T(2,128)(2,1)S(1)} %copy-done.6), custom_call_target="tpu_custom_call" | custom-call | flops 25165824 | bytes 3817600 | tf_op jit(solution)/shard_map/attention/pallas_call | solution.py:22
  9.9 0.0 copy-done
  9.9 0.0 copy-start.3
  9.9 0.8 %base.1.refs_5_.refs_3_ = f32[4,32,256]{2,1,0:T(8,128)S(1)} custom-call(bf16[32,2048]{1,0:T(8,128)(2,1)S(1)} %get-tuple-element.27.rows_ref, bf16[2048,1024]{1,0:T(8,128)(2,1)S(1)} %copy-done), custom_call_target="tpu_custom_call" | custom-call | flops 134217728 | bytes 4456448 | tf_op jit(solution)/shard_map/base/pallas_call | solution.py:22
  10.7 0.0 copy-start.4
  10.7 0.0 copy-start.7
  10.8 0.0 copy-start.8
  10.8 0.0 collective-permute-done.refs_1_
  10.8 0.0 collective-permute-done.1.refs_2_
  10.8 3.3 %collective-permute-done.2.refs_3_ = bf16[16,2176]{1,0:T(8,128)(2,1)S(1)} collective-permute-done((bf16[16,2176]{1,0:T(8,128)(2,1)S(1)}, bf16[16,2176]{1,0:T(8,128)(2,1)S(1)}, u32[]{:S(2)}, u32[]{:S(2)}) %collective-permute-start.2) | collective-permute-done | bytes 69664 | tf_op jit(solution)/shard_map/ppermute | solution.py:284
  14.0 0.0 copy-done.3
  14.0 0.6 %rank.1 = (f32[64,64]{1,0:T(8,128)S(1)}, f32[64,128]{1,0:T(8,128)S(1)}, bf16[128,128]{1,0:T(8,128)(2,1)S(1)}, bf16[128,128]{1,0:T(8,128)(2,1)S(1)}, bf16[128,128]{1,0:T(8,128)(2,1)S(1)}) custom-call(bf16[16,2176]{1,0:T(8,128)(2,1)S(1)} %get-tuple-element.23.refs_0_, bf16[16,2176]{1,0:T(8,128)(2,1)S(1)} %collective-permute-done.refs_1_, ...), custom_call_target="tpu_custom_call" | custom-call | flops 67108864 | bytes 1605632 | tf_op jit(solution)/shard_map/rank/pallas_call | solution.py:22
  14.6 0.1 collective-permute-start.3
  14.7 1.5 %collective-permute-start.4 = (bf16[128,128]{1,0:T(8,128)(2,1)S(1)}, bf16[128,128]{1,0:T(8,128)(2,1)S(1)}, u32[]{:S(2)}, u32[]{:S(2)}) collective-permute-start(bf16[128,128]{1,0:T(8,128)(2,1)S(1)} %get-tuple-element.32), channel_id=1, source_target_pairs={{0,2},{1,3},{2,0},{3,1},{4,6},{5,7},{6,4},{7,5},{8,10},{9,11},{10,... | collective-permute-start | bytes 98312 | tf_op jit(solution)/shard_map/ppermute | solution.py:284
  16.3 0.3 %collective-permute-start.5 = (bf16[128,128]{1,0:T(8,128)(2,1)S(1)}, bf16[128,128]{1,0:T(8,128)(2,1)S(1)}, u32[]{:S(2)}, u32[]{:S(2)}) collective-permute-start(bf16[128,128]{1,0:T(8,128)(2,1)S(1)} %get-tuple-element.33), channel_id=1, source_target_pairs={{0,1},{1,0},{2,3},{3,2},{4,5},{5,4},{6,7},{7,6},{8,9},{9,8},{10,11... | collective-permute-start | bytes 98312 | tf_op jit(solution)/shard_map/ppermute | solution.py:284
  16.6 1.8 %collective-permute-done.3.refs_0_ = bf16[128,128]{1,0:T(8,128)(2,1)S(1)} collective-permute-done((bf16[128,128]{1,0:T(8,128)(2,1)S(1)}, bf16[128,128]{1,0:T(8,128)(2,1)S(1)}, u32[]{:S(2)}, u32[]{:S(2)}) %collective-permute-start.3) | collective-permute-done | bytes 32800 | tf_op jit(solution)/shard_map/ppermute | solution.py:284
  18.4 0.4 %collective-permute-done.4.refs_1_ = bf16[128,128]{1,0:T(8,128)(2,1)S(1)} collective-permute-done((bf16[128,128]{1,0:T(8,128)(2,1)S(1)}, bf16[128,128]{1,0:T(8,128)(2,1)S(1)}, u32[]{:S(2)}, u32[]{:S(2)}) %collective-permute-start.4) | collective-permute-done | bytes 32800 | tf_op jit(solution)/shard_map/ppermute | solution.py:284
  18.7 0.0 collective-permute-done.5.refs_2_
  18.8 0.0 copy-done.4
  18.8 0.3 %up.1 = (bf16[16,256]{1,0:T(8,128)(2,1)S(1)}, bf16[16,256]{1,0:T(8,128)(2,1)S(1)}, bf16[16,256]{1,0:T(8,128)(2,1)S(1)}, bf16[16,256]{1,0:T(8,128)(2,1)S(1)}) custom-call(bf16[128,128]{1,0:T(8,128)(2,1)S(1)} %collective-permute-done.3.refs_0_, bf16[128,128]{1,0:T(8,128)(2,1)S(1)} %collective-permute-done.4.refs_1_, ...), custom_call_target="tpu_custom_call" | custom-call | flops 33554432 | bytes 704512 | tf_op jit(solution)/shard_map/up/pallas_call | solution.py:22
  19.1 1.4 %collective-permute-start.6 = (bf16[16,256]{1,0:T(8,128)(2,1)S(1)}, bf16[16,256]{1,0:T(8,128)(2,1)S(1)}, u32[]{:S(2)}, u32[]{:S(2)}) collective-permute-start(bf16[16,256]{1,0:T(8,128)(2,1)S(1)} %get-tuple-element.37), channel_id=1, source_target_pairs={{0,13},{1,12},{2,15},{3,14},{4,9},{5,8},{6,11},{7,10},{8,5},{9,4},... | collective-permute-start | bytes 24584 | tf_op jit(solution)/shard_map/ppermute | solution.py:284
  20.5 0.7 %collective-permute-start.7 = (bf16[16,256]{1,0:T(8,128)(2,1)S(1)}, bf16[16,256]{1,0:T(8,128)(2,1)S(1)}, u32[]{:S(2)}, u32[]{:S(2)}) collective-permute-start(bf16[16,256]{1,0:T(8,128)(2,1)S(1)} %get-tuple-element.38), channel_id=1, source_target_pairs={{0,9},{1,8},{2,11},{3,10},{4,13},{5,12},{6,15},{7,14},{8,1},{9,0},... | collective-permute-start | bytes 24584 | tf_op jit(solution)/shard_map/ppermute | solution.py:284
  21.2 1.9 %collective-permute-start.8 = (bf16[16,256]{1,0:T(8,128)(2,1)S(1)}, bf16[16,256]{1,0:T(8,128)(2,1)S(1)}, u32[]{:S(2)}, u32[]{:S(2)}) collective-permute-start(bf16[16,256]{1,0:T(8,128)(2,1)S(1)} %get-tuple-element.39), channel_id=1, source_target_pairs={{0,5},{1,4},{2,7},{3,6},{4,1},{5,0},{6,3},{7,2},{8,13},{9,12},{10,... | collective-permute-start | bytes 24584 | tf_op jit(solution)/shard_map/ppermute | solution.py:284
  23.2 0.0 copy-done.7
  23.2 0.0 copy-done.8
  23.2 0.3 %base_sum.1 = (f32[32,256]{1,0:T(8,128)S(1)}, bf16[32,64]{1,0:T(8,128)(2,1)S(1)}) custom-call(bf16[128,128]{1,0:T(8,128)(2,1)S(1)} %collective-permute-done.3.refs_0_, bf16[128,128]{1,0:T(8,128)(2,1)S(1)} %collective-permute-done.4.refs_1_, bf16[128,128]{1,0:T(8,128)(2,1)S(1)} %collective-permute-done.5.refs_2_, f32[4,32,256]{2,1,0:T(8,128)S(1)} %base.1.refs_5_.refs_3_, ...), custom_call_target="tpu_custom_call" | custom-call | flops 32768 | bytes 267392 | tf_op jit(solution)/shard_map/base_sum/pallas_call | solution.py:22
  23.5 0.5 %collective-permute-done.6.refs_1_ = bf16[16,256]{1,0:T(8,128)(2,1)S(1)} collective-permute-done((bf16[16,256]{1,0:T(8,128)(2,1)S(1)}, bf16[16,256]{1,0:T(8,128)(2,1)S(1)}, u32[]{:S(2)}, u32[]{:S(2)}) %collective-permute-start.6) | collective-permute-done | bytes 8224 | tf_op jit(solution)/shard_map/ppermute | solution.py:284
  24.0 0.5 %collective-permute-done.7.refs_2_ = bf16[16,256]{1,0:T(8,128)(2,1)S(1)} collective-permute-done((bf16[16,256]{1,0:T(8,128)(2,1)S(1)}, bf16[16,256]{1,0:T(8,128)(2,1)S(1)}, u32[]{:S(2)}, u32[]{:S(2)}) %collective-permute-start.7) | collective-permute-done | bytes 8224 | tf_op jit(solution)/shard_map/ppermute | solution.py:284
  24.5 0.2 collective-permute-done.8.refs_3_
  24.7 0.9 %last.1 = (bf16[32,16,128]{2,1,0:T(8,128)(2,1)}, bf16[32,2,128]{2,1,0:T(2,128)(2,1)}) custom-call(bf16[16,256]{1,0:T(8,128)(2,1)S(1)} %get-tuple-element.36.refs_0_, bf16[16,256]{1,0:T(8,128)(2,1)S(1)} %collective-permute-done.6.refs_1_, bf16[16,256]{1,0:T(8,128)(2,1)S(1)} %collective-permute-done.7.refs_2_, ...), custom_call_target="tpu_custom_call" | custom-call | flops 1048576 | bytes 741376 | tf_op jit(solution)/shard_map/last/pallas_call | solution.py:22
Async XLA Ops:
  0.6 7.3 %copy-start.1 = (bf16[32,2,96,128]{3,2,1,0:T(8,128)(2,1)S(1)}, bf16[32,2,96,128]{3,2,1,0:T(8,128)(2,1)}, u32[]{:S(2)}) copy-start(bf16[32,2,96,128]{3,2,1,0:T(8,128)(2,1)} %key_ref.1) | copy-start | bytes 4718596
  0.6 7.3 %copy-start.2 = (bf16[32,2,96,128]{3,2,1,0:T(8,128)(2,1)S(1)}, bf16[32,2,96,128]{3,2,1,0:T(8,128)(2,1)}, u32[]{:S(2)}) copy-start(bf16[32,2,96,128]{3,2,1,0:T(8,128)(2,1)} %value_ref.1) | copy-start | bytes 4718596
  0.7 7.3 %copy-start.5 = (bf16[32,16,128]{2,1,0:T(8,128)(2,1)S(1)}, bf16[32,16,128]{2,1,0:T(8,128)(2,1)}, u32[]{:S(2)}) copy-start(bf16[32,16,128]{2,1,0:T(8,128)(2,1)} %query_ref.1) | copy-start | bytes 393220
  0.7 7.3 %copy-start.6 = (bf16[32,2,128]{2,1,0:T(2,128)(2,1)S(1)}, bf16[32,2,128]{2,1,0:T(2,128)(2,1)}, u32[]{:S(2)}) copy-start(bf16[32,2,128]{2,1,0:T(2,128)(2,1)} %new_ref.1) | copy-start | bytes 49156
  0.7 7.3 %copy-start.9 = (s32[32]{0:T(128)S(1)}, s32[32]{0:T(128)}, u32[]{:S(2)}) copy-start(s32[32]{0:T(128)} %length_ref.1) | copy-start | bytes 388
  0.7 9.2 %copy-start = (bf16[2048,1024]{1,0:T(8,128)(2,1)S(1)}, bf16[2048,1024]{1,0:T(8,128)(2,1)}, u32[]{:S(2)}) copy-start(bf16[2048,1024]{1,0:T(8,128)(2,1)} %matrix_ref.1) | copy-start | bytes 12582916
  2.2 8.5 %collective-permute-start = (bf16[16,2176]{1,0:T(8,128)(2,1)S(1)}, bf16[16,2176]{1,0:T(8,128)(2,1)S(1)}, u32[]{:S(2)}, u32[]{:S(2)}) collective-permute-start(bf16[16,2176]{1,0:T(8,128)(2,1)S(1)} %get-tuple-element.24), channel_id=1, source_target_pairs={{0,8},{1,9},{2,10},{3,11},{4,12},{5,13},{6,14},{7,15},{8,0},{9,1},... | collective-permute-start | bytes 208904 | tf_op jit(solution)/shard_map/ppermute | solution.py:284
  6.3 4.4 %collective-permute-start.1 = (bf16[16,2176]{1,0:T(8,128)(2,1)S(1)}, bf16[16,2176]{1,0:T(8,128)(2,1)S(1)}, u32[]{:S(2)}, u32[]{:S(2)}) collective-permute-start(bf16[16,2176]{1,0:T(8,128)(2,1)S(1)} %get-tuple-element.25), channel_id=1, source_target_pairs={{0,4},{1,5},{2,6},{3,7},{4,0},{5,1},{6,2},{7,3},{8,12},{9,13},{10,... | collective-permute-start | bytes 208904 | tf_op jit(solution)/shard_map/ppermute | solution.py:284
  7.9 6.1 %collective-permute-start.2 = (bf16[16,2176]{1,0:T(8,128)(2,1)S(1)}, bf16[16,2176]{1,0:T(8,128)(2,1)S(1)}, u32[]{:S(2)}, u32[]{:S(2)}) collective-permute-start(bf16[16,2176]{1,0:T(8,128)(2,1)S(1)} %get-tuple-element.26), channel_id=1, source_target_pairs={{0,12},{1,13},{2,14},{3,15},{4,8},{5,9},{6,10},{7,11},{8,4},{9,5},... | collective-permute-start | bytes 208904 | tf_op jit(solution)/shard_map/ppermute | solution.py:284
  9.9 4.1 %copy-start.3 = (bf16[4,64,2048]{2,1,0:T(8,128)(2,1)S(1)}, bf16[4,64,2048]{2,1,0:T(8,128)(2,1)}, u32[]{:S(2)}) copy-start(bf16[4,64,2048]{2,1,0:T(8,128)(2,1)} %param.15) | copy-start | bytes 3145732
  10.7 8.0 %copy-start.4 = (bf16[4,64,1024]{2,1,0:T(8,128)(2,1)S(1)}, bf16[4,64,1024]{2,1,0:T(8,128)(2,1)}, u32[]{:S(2)}) copy-start(bf16[4,64,1024]{2,1,0:T(8,128)(2,1)} %param.16) | copy-start | bytes 1572868
  10.7 12.4 %copy-start.7 = (f32[256]{0:T(256)S(1)}, f32[256]{0:T(256)}, u32[]{:S(2)}) copy-start(f32[256]{0:T(256)} %param.14) | copy-start | bytes 3076
  10.8 12.4 %copy-start.8 = (s32[32,1]{0,1:T(1,128)S(1)}, s32[32,1]{0,1:T(1,128)}, u32[]{:S(2)}) copy-start(s32[32,1]{0,1:T(1,128)} %param.17) | copy-start | bytes 388
  14.6 3.7 %collective-permute-start.3 = (bf16[128,128]{1,0:T(8,128)(2,1)S(1)}, bf16[128,128]{1,0:T(8,128)(2,1)S(1)}, u32[]{:S(2)}, u32[]{:S(2)}) collective-permute-start(bf16[128,128]{1,0:T(8,128)(2,1)S(1)} %get-tuple-element.31), channel_id=1, source_target_pairs={{0,3},{1,2},{2,1},{3,0},{4,7},{5,6},{6,5},{7,4},{8,11},{9,10},{10,... | collective-permute-start | bytes 98312 | tf_op jit(solution)/shard_map/ppermute | solution.py:284
  14.7 4.0 %collective-permute-start.4 = (bf16[128,128]{1,0:T(8,128)(2,1)S(1)}, bf16[128,128]{1,0:T(8,128)(2,1)S(1)}, u32[]{:S(2)}, u32[]{:S(2)}) collective-permute-start(bf16[128,128]{1,0:T(8,128)(2,1)S(1)} %get-tuple-element.32), channel_id=1, source_target_pairs={{0,2},{1,3},{2,0},{3,1},{4,6},{5,7},{6,4},{7,5},{8,10},{9,11},{10,... | collective-permute-start | bytes 98312 | tf_op jit(solution)/shard_map/ppermute | solution.py:284
  16.3 2.5 %collective-permute-start.5 = (bf16[128,128]{1,0:T(8,128)(2,1)S(1)}, bf16[128,128]{1,0:T(8,128)(2,1)S(1)}, u32[]{:S(2)}, u32[]{:S(2)}) collective-permute-start(bf16[128,128]{1,0:T(8,128)(2,1)S(1)} %get-tuple-element.33), channel_id=1, source_target_pairs={{0,1},{1,0},{2,3},{3,2},{4,5},{5,4},{6,7},{7,6},{8,9},{9,8},{10,11... | collective-permute-start | bytes 98312 | tf_op jit(solution)/shard_map/ppermute | solution.py:284
  19.1 4.9 %collective-permute-start.6 = (bf16[16,256]{1,0:T(8,128)(2,1)S(1)}, bf16[16,256]{1,0:T(8,128)(2,1)S(1)}, u32[]{:S(2)}, u32[]{:S(2)}) collective-permute-start(bf16[16,256]{1,0:T(8,128)(2,1)S(1)} %get-tuple-element.37), channel_id=1, source_target_pairs={{0,13},{1,12},{2,15},{3,14},{4,9},{5,8},{6,11},{7,10},{8,5},{9,4},... | collective-permute-start | bytes 24584 | tf_op jit(solution)/shard_map/ppermute | solution.py:284
  20.5 4.0 %collective-permute-start.7 = (bf16[16,256]{1,0:T(8,128)(2,1)S(1)}, bf16[16,256]{1,0:T(8,128)(2,1)S(1)}, u32[]{:S(2)}, u32[]{:S(2)}) collective-permute-start(bf16[16,256]{1,0:T(8,128)(2,1)S(1)} %get-tuple-element.38), channel_id=1, source_target_pairs={{0,9},{1,8},{2,11},{3,10},{4,13},{5,12},{6,15},{7,14},{8,1},{9,0},... | collective-permute-start | bytes 24584 | tf_op jit(solution)/shard_map/ppermute | solution.py:284
  21.2 3.4 %collective-permute-start.8 = (bf16[16,256]{1,0:T(8,128)(2,1)S(1)}, bf16[16,256]{1,0:T(8,128)(2,1)S(1)}, u32[]{:S(2)}, u32[]{:S(2)}) collective-permute-start(bf16[16,256]{1,0:T(8,128)(2,1)S(1)} %get-tuple-element.39), channel_id=1, source_target_pairs={{0,5},{1,4},{2,7},{3,6},{4,1},{5,0},{6,3},{7,2},{8,13},{9,12},{10,... | collective-permute-start | bytes 24584 | tf_op jit(solution)/shard_map/ppermute | solution.py:284

commit v5 on v4

--- a/solution.py
+++ b/solution.py
@@ -59,16 +59,21 @@
     return [3, 2, 1] if pieces == 4 else list(range(1, pieces))
 
 
-def placement(home_row, blocks, capacity, relative, ordered):
-    home = column(home_row)
+def labels(home, blocks, relative, ordered):
+    if not relative:
+        return home
+    step = home ^ lax.axis_index("replica")
+    if not ordered:
+        return step
+    odd = lax.axis_index("tensor") % 2 == 1
+    for at, (a, b) in enumerate(zip(*orders(blocks))):
+        home = jnp.where(step == jnp.where(odd, b, a), at, home)
+    return home
+
+
+def placement(home_row, blocks, capacity, relative):
+    home = labels(column(home_row), blocks, relative, False)
     rows = home.shape[0]
-    if relative:
-        step = home ^ lax.axis_index("replica")
-        home = step
-        if ordered:
-            odd = lax.axis_index("tensor") % 2 == 1
-            for at, (a, b) in enumerate(zip(*orders(blocks))):
-                home = jnp.where(step == jnp.where(odd, b, a), at, home)
     hot = (home == lax.broadcasted_iota(jnp.int32, (rows, blocks), 1)).astype(f32)
     at = lax.broadcasted_iota(jnp.int32, (rows, rows), 0)
     below = (lax.broadcasted_iota(jnp.int32, (rows, rows), 1) < at).astype(bf16)
@@ -88,17 +93,22 @@
     ]
     for copy in copies:
         copy.start()
+    rows, width = rows_ref.shape
+    at = lax.broadcasted_iota(jnp.int32, (rows, rows), 0)
+    above = (at < lax.broadcasted_iota(jnp.int32, (rows, rows), 1)).astype(f32).astype(bf16)
     copies[0].wait()
-    place = placement(home_ref[...], blocks, capacity, relative, True)
-    rows, width = rows_ref.shape
+    label = labels(home_ref[...], blocks, relative, True)
+    hot = (label == lax.broadcasted_iota(jnp.int32, (blocks, rows), 0)).astype(f32)
+    before = jnp.dot(hot.astype(bf16), above, preferred_element_type=f32)
+    position = jnp.sum(before * hot, axis=0, keepdims=True).astype(jnp.int32)
+    flat = label * capacity + position
+    turned = flat == lax.broadcasted_iota(jnp.int32, (blocks * capacity, rows), 0)
     copies[1].wait()
-    slot = (column(slot_ref[...]) + 1).astype(f32)
-    spread = jnp.broadcast_to(slot, (rows, lanes)).astype(bf16)
-    turned = place.astype(f32).astype(bf16)
-    over = (((0,), (0,)), ((), ()))
-    slots = lax.dot_general(turned, spread, over, preferred_element_type=f32).astype(bf16)
+    slots = jnp.sum(jnp.where(turned, slot_ref[...] + 1, 0).astype(f32), axis=1, keepdims=True)
+    slots = jnp.broadcast_to(slots, (blocks * capacity, lanes)).astype(bf16)
+    turned = turned.astype(f32).astype(bf16)
     copies[2].wait()
-    packed = lax.dot_general(turned, rows_ref[...], over, preferred_element_type=f32).astype(bf16)
+    packed = jnp.dot(turned, rows_ref[...], preferred_element_type=f32).astype(bf16)
     size = outs[0].shape[0]
     for b, out in enumerate(outs):
         out[:, :width] = packed[b * size : (b + 1) * size]
@@ -173,7 +183,7 @@
 def sum_kernel(peers, blocks, capacity, relative, *refs):
     got = refs[:peers]
     base_ref, bias_ref, home_ref, out, place_ref = refs[peers:]
-    place = placement(home_ref[...], blocks, capacity, relative, False)
+    place = placement(home_ref[...], blocks, capacity, relative)
     place_ref[...] = place.astype(f32).astype(bf16)
     total = base_ref[lax.axis_index("tensor")] + bias_ref[...]
     rows = total.shape[0]

time: 25.7 us -> 25.4 us (0.988)
  no operation moved by 1% of the time
where the time goes in v5:
time: 25.4 us; the launch traced here: 25.3 us
  starting transfers between devices  11.7 us (46%)
  waiting for transfers between devices  6.61 us (26%)
  Pallas kernels  6.14 us (24%)
  between operations  0.79 us (3%)
    ppermute x9, starting transfers between devices, send(): return lax.ppermute(block, ('replica', 'tensor'), pairs)  11.7 us
    ppermute x9, waiting for transfers between devices, send(): return lax.ppermute(block, ('replica', 'tensor'), pairs)  6.61 us
    pallas_call x7, Pallas kernels, call(): pl.pallas_call(kernel, name=name, out_shape=outs, cost_estimate=pl.CostEs...  6.14 us
  transfers between devices with their start and end apart: 9, of which 6 were waited for; matrix products, arithmetic and copies ran while one was open for 0% of the time, Pallas kernels for 12%

profile of v5, /device:TPU:0, one launch (start us, length us, event | category | flops | bytes accessed | tf_op | source)
XLA Modules:
  0.0 25.3 jit_solution(9922909178926506079)
XLA Ops:
  0.6 0.0 copy-start.1
  0.6 0.0 copy-start.2
  0.7 0.0 copy-start.5
  0.7 0.0 copy-start.6
  0.7 0.0 copy-start.9
  0.7 0.0 copy-start
  0.7 1.3 %pack.1 = (bf16[32,2048]{1,0:T(8,128)(2,1)S(1)}, bf16[16,2176]{1,0:T(8,128)(2,1)S(1)}, bf16[16,2176]{1,0:T(8,128)(2,1)S(1)}, bf16[16,2176]{1,0:T(8,128)(2,1)S(1)}, bf16[16,2176]{1,0:T(8,128)(2,1)S(1)}) custom-call(s32[1,32]{1,0:T(1,128)} %bitcast.8, s32[1,32]{1,0:T(1,128)} %bitcast.10, bf16[32,2048]{1,0:T(8,128)(2,1)} %rows_hbm.1), custom_call_target="tpu_custom_call" | custom-call | flops 40000000000 | bytes 540928 | tf_op jit(solution)/shard_map/pack/pallas_call | solution.py:22
  2.0 4.1 %collective-permute-start = (bf16[16,2176]{1,0:T(8,128)(2,1)S(1)}, bf16[16,2176]{1,0:T(8,128)(2,1)S(1)}, u32[]{:S(2)}, u32[]{:S(2)}) collective-permute-start(bf16[16,2176]{1,0:T(8,128)(2,1)S(1)} %get-tuple-element.24), channel_id=1, source_target_pairs={{0,8},{1,9},{2,10},{3,11},{4,12},{5,13},{6,14},{7,15},{8,0},{9,1},... | collective-permute-start | bytes 208904 | tf_op jit(solution)/shard_map/ppermute | solution.py:294
  6.1 1.6 %collective-permute-start.1 = (bf16[16,2176]{1,0:T(8,128)(2,1)S(1)}, bf16[16,2176]{1,0:T(8,128)(2,1)S(1)}, u32[]{:S(2)}, u32[]{:S(2)}) collective-permute-start(bf16[16,2176]{1,0:T(8,128)(2,1)S(1)} %get-tuple-element.25), channel_id=1, source_target_pairs={{0,4},{1,5},{2,6},{3,7},{4,0},{5,1},{6,2},{7,3},{8,12},{9,13},{10,... | collective-permute-start | bytes 208904 | tf_op jit(solution)/shard_map/ppermute | solution.py:294
  7.7 0.0 collective-permute-start.2
  7.7 0.0 copy-done.1
  7.7 0.0 copy-done.2
  7.7 0.0 copy-done.5
  7.7 0.0 copy-done.6
  7.7 0.0 copy-done.9
  7.7 1.9 %attention.1 = (f32[32,16,128]{2,1,0:T(8,128)S(1)}, f32[32,16,128]{2,1,0:T(8,128)S(1)}) custom-call(s32[32]{0:T(128)S(1)} %copy-done.9, bf16[32,16,128]{2,1,0:T(8,128)(2,1)S(1)} %copy-done.5, bf16[32,2,96,128]{3,2,1,0:T(8,128)(2,1)S(1)} %copy-done.1, bf16[32,2,96,128]{3,2,1,0:T(8,128)(2,1)S(1)} %copy-done.2, bf16[32,2,128]{2,1,0:T(2,128)(2,1)S(1)} %copy-done.6), custom_call_target="tpu_custom_call" | custom-call | flops 25165824 | bytes 3817600 | tf_op jit(solution)/shard_map/attention/pallas_call | solution.py:22
  9.7 0.0 copy-done
  9.7 0.0 copy-start.3
  9.7 0.8 %base.1.refs_5_.refs_3_ = f32[4,32,256]{2,1,0:T(8,128)S(1)} custom-call(bf16[32,2048]{1,0:T(8,128)(2,1)S(1)} %get-tuple-element.27.rows_ref, bf16[2048,1024]{1,0:T(8,128)(2,1)S(1)} %copy-done), custom_call_target="tpu_custom_call" | custom-call | flops 134217728 | bytes 4456448 | tf_op jit(solution)/shard_map/base/pallas_call | solution.py:22
  10.5 0.0 copy-start.4
  10.5 0.0 copy-start.7
  10.5 0.0 copy-start.8
  10.5 0.0 collective-permute-done.refs_1_
  10.5 0.0 collective-permute-done.1.refs_2_
  10.5 3.3 %collective-permute-done.2.refs_3_ = bf16[16,2176]{1,0:T(8,128)(2,1)S(1)} collective-permute-done((bf16[16,2176]{1,0:T(8,128)(2,1)S(1)}, bf16[16,2176]{1,0:T(8,128)(2,1)S(1)}, u32[]{:S(2)}, u32[]{:S(2)}) %collective-permute-start.2) | collective-permute-done | bytes 69664 | tf_op jit(solution)/shard_map/ppermute | solution.py:294
  13.8 0.0 copy-done.3
  13.8 0.6 %rank.1 = (f32[64,64]{1,0:T(8,128)S(1)}, f32[64,128]{1,0:T(8,128)S(1)}, bf16[128,128]{1,0:T(8,128)(2,1)S(1)}, bf16[128,128]{1,0:T(8,128)(2,1)S(1)}, bf16[128,128]{1,0:T(8,128)(2,1)S(1)}) custom-call(bf16[16,2176]{1,0:T(8,128)(2,1)S(1)} %get-tuple-element.23.refs_0_, bf16[16,2176]{1,0:T(8,128)(2,1)S(1)} %collective-permute-done.refs_1_, ...), custom_call_target="tpu_custom_call" | custom-call | flops 67108864 | bytes 1605632 | tf_op jit(solution)/shard_map/rank/pallas_call | solution.py:22
  14.4 0.1 collective-permute-start.3
  14.5 1.6 %collective-permute-start.4 = (bf16[128,128]{1,0:T(8,128)(2,1)S(1)}, bf16[128,128]{1,0:T(8,128)(2,1)S(1)}, u32[]{:S(2)}, u32[]{:S(2)}) collective-permute-start(bf16[128,128]{1,0:T(8,128)(2,1)S(1)} %get-tuple-element.32), channel_id=1, source_target_pairs={{0,2},{1,3},{2,0},{3,1},{4,6},{5,7},{6,4},{7,5},{8,10},{9,11},{10,... | collective-permute-start | bytes 98312 | tf_op jit(solution)/shard_map/ppermute | solution.py:294
  16.0 0.3 %collective-permute-start.5 = (bf16[128,128]{1,0:T(8,128)(2,1)S(1)}, bf16[128,128]{1,0:T(8,128)(2,1)S(1)}, u32[]{:S(2)}, u32[]{:S(2)}) collective-permute-start(bf16[128,128]{1,0:T(8,128)(2,1)S(1)} %get-tuple-element.33), channel_id=1, source_target_pairs={{0,1},{1,0},{2,3},{3,2},{4,5},{5,4},{6,7},{7,6},{8,9},{9,8},{10,11... | collective-permute-start | bytes 98312 | tf_op jit(solution)/shard_map/ppermute | solution.py:294
  16.3 1.8 %collective-permute-done.3.refs_0_ = bf16[128,128]{1,0:T(8,128)(2,1)S(1)} collective-permute-done((bf16[128,128]{1,0:T(8,128)(2,1)S(1)}, bf16[128,128]{1,0:T(8,128)(2,1)S(1)}, u32[]{:S(2)}, u32[]{:S(2)}) %collective-permute-start.3) | collective-permute-done | bytes 32800 | tf_op jit(solution)/shard_map/ppermute | solution.py:294
  18.1 0.4 %collective-permute-done.4.refs_1_ = bf16[128,128]{1,0:T(8,128)(2,1)S(1)} collective-permute-done((bf16[128,128]{1,0:T(8,128)(2,1)S(1)}, bf16[128,128]{1,0:T(8,128)(2,1)S(1)}, u32[]{:S(2)}, u32[]{:S(2)}) %collective-permute-start.4) | collective-permute-done | bytes 32800 | tf_op jit(solution)/shard_map/ppermute | solution.py:294
  18.5 0.0 collective-permute-done.5.refs_2_
  18.5 0.0 copy-done.4
  18.5 0.3 %up.1 = (bf16[16,256]{1,0:T(8,128)(2,1)S(1)}, bf16[16,256]{1,0:T(8,128)(2,1)S(1)}, bf16[16,256]{1,0:T(8,128)(2,1)S(1)}, bf16[16,256]{1,0:T(8,128)(2,1)S(1)}) custom-call(bf16[128,128]{1,0:T(8,128)(2,1)S(1)} %collective-permute-done.3.refs_0_, bf16[128,128]{1,0:T(8,128)(2,1)S(1)} %collective-permute-done.4.refs_1_, ...), custom_call_target="tpu_custom_call" | custom-call | flops 33554432 | bytes 704512 | tf_op jit(solution)/shard_map/up/pallas_call | solution.py:22
  18.8 1.4 %collective-permute-start.6 = (bf16[16,256]{1,0:T(8,128)(2,1)S(1)}, bf16[16,256]{1,0:T(8,128)(2,1)S(1)}, u32[]{:S(2)}, u32[]{:S(2)}) collective-permute-start(bf16[16,256]{1,0:T(8,128)(2,1)S(1)} %get-tuple-element.37), channel_id=1, source_target_pairs={{0,13},{1,12},{2,15},{3,14},{4,9},{5,8},{6,11},{7,10},{8,5},{9,4},... | collective-permute-start | bytes 24584 | tf_op jit(solution)/shard_map/ppermute | solution.py:294
  20.3 0.7 %collective-permute-start.7 = (bf16[16,256]{1,0:T(8,128)(2,1)S(1)}, bf16[16,256]{1,0:T(8,128)(2,1)S(1)}, u32[]{:S(2)}, u32[]{:S(2)}) collective-permute-start(bf16[16,256]{1,0:T(8,128)(2,1)S(1)} %get-tuple-element.38), channel_id=1, source_target_pairs={{0,9},{1,8},{2,11},{3,10},{4,13},{5,12},{6,15},{7,14},{8,1},{9,0},... | collective-permute-start | bytes 24584 | tf_op jit(solution)/shard_map/ppermute | solution.py:294
  21.0 1.9 %collective-permute-start.8 = (bf16[16,256]{1,0:T(8,128)(2,1)S(1)}, bf16[16,256]{1,0:T(8,128)(2,1)S(1)}, u32[]{:S(2)}, u32[]{:S(2)}) collective-permute-start(bf16[16,256]{1,0:T(8,128)(2,1)S(1)} %get-tuple-element.39), channel_id=1, source_target_pairs={{0,5},{1,4},{2,7},{3,6},{4,1},{5,0},{6,3},{7,2},{8,13},{9,12},{10,... | collective-permute-start | bytes 24584 | tf_op jit(solution)/shard_map/ppermute | solution.py:294
  23.0 0.0 copy-done.7
  23.0 0.0 copy-done.8
  23.0 0.3 %base_sum.1 = (f32[32,256]{1,0:T(8,128)S(1)}, bf16[32,64]{1,0:T(8,128)(2,1)S(1)}) custom-call(bf16[128,128]{1,0:T(8,128)(2,1)S(1)} %collective-permute-done.3.refs_0_, bf16[128,128]{1,0:T(8,128)(2,1)S(1)} %collective-permute-done.4.refs_1_, bf16[128,128]{1,0:T(8,128)(2,1)S(1)} %collective-permute-done.5.refs_2_, f32[4,32,256]{2,1,0:T(8,128)S(1)} %base.1.refs_5_.refs_3_, ...), custom_call_target="tpu_custom_call" | custom-call | flops 32768 | bytes 267392 | tf_op jit(solution)/shard_map/base_sum/pallas_call | solution.py:22
  23.3 0.5 %collective-permute-done.6.refs_1_ = bf16[16,256]{1,0:T(8,128)(2,1)S(1)} collective-permute-done((bf16[16,256]{1,0:T(8,128)(2,1)S(1)}, bf16[16,256]{1,0:T(8,128)(2,1)S(1)}, u32[]{:S(2)}, u32[]{:S(2)}) %collective-permute-start.6) | collective-permute-done | bytes 8224 | tf_op jit(solution)/shard_map/ppermute | solution.py:294
  23.8 0.5 %collective-permute-done.7.refs_2_ = bf16[16,256]{1,0:T(8,128)(2,1)S(1)} collective-permute-done((bf16[16,256]{1,0:T(8,128)(2,1)S(1)}, bf16[16,256]{1,0:T(8,128)(2,1)S(1)}, u32[]{:S(2)}, u32[]{:S(2)}) %collective-permute-start.7) | collective-permute-done | bytes 8224 | tf_op jit(solution)/shard_map/ppermute | solution.py:294
  24.3 0.2 collective-permute-done.8.refs_3_
  24.4 0.9 %last.1 = (bf16[32,16,128]{2,1,0:T(8,128)(2,1)}, bf16[32,2,128]{2,1,0:T(2,128)(2,1)}) custom-call(bf16[16,256]{1,0:T(8,128)(2,1)S(1)} %get-tuple-element.36.refs_0_, bf16[16,256]{1,0:T(8,128)(2,1)S(1)} %collective-permute-done.6.refs_1_, bf16[16,256]{1,0:T(8,128)(2,1)S(1)} %collective-permute-done.7.refs_2_, ...), custom_call_target="tpu_custom_call" | custom-call | flops 1048576 | bytes 741376 | tf_op jit(solution)/shard_map/last/pallas_call | solution.py:22
Async XLA Ops:
  0.6 7.1 %copy-start.1 = (bf16[32,2,96,128]{3,2,1,0:T(8,128)(2,1)S(1)}, bf16[32,2,96,128]{3,2,1,0:T(8,128)(2,1)}, u32[]{:S(2)}) copy-start(bf16[32,2,96,128]{3,2,1,0:T(8,128)(2,1)} %key_ref.1) | copy-start | bytes 4718596
  0.6 7.1 %copy-start.2 = (bf16[32,2,96,128]{3,2,1,0:T(8,128)(2,1)S(1)}, bf16[32,2,96,128]{3,2,1,0:T(8,128)(2,1)}, u32[]{:S(2)}) copy-start(bf16[32,2,96,128]{3,2,1,0:T(8,128)(2,1)} %value_ref.1) | copy-start | bytes 4718596
  0.7 7.1 %copy-start.5 = (bf16[32,16,128]{2,1,0:T(8,128)(2,1)S(1)}, bf16[32,16,128]{2,1,0:T(8,128)(2,1)}, u32[]{:S(2)}) copy-start(bf16[32,16,128]{2,1,0:T(8,128)(2,1)} %query_ref.1) | copy-start | bytes 393220
  0.7 7.1 %copy-start.6 = (bf16[32,2,128]{2,1,0:T(2,128)(2,1)S(1)}, bf16[32,2,128]{2,1,0:T(2,128)(2,1)}, u32[]{:S(2)}) copy-start(bf16[32,2,128]{2,1,0:T(2,128)(2,1)} %new_ref.1) | copy-start | bytes 49156
  0.7 7.1 %copy-start.9 = (s32[32]{0:T(128)S(1)}, s32[32]{0:T(128)}, u32[]{:S(2)}) copy-start(s32[32]{0:T(128)} %length_ref.1) | copy-start | bytes 388
  0.7 9.0 %copy-start = (bf16[2048,1024]{1,0:T(8,128)(2,1)S(1)}, bf16[2048,1024]{1,0:T(8,128)(2,1)}, u32[]{:S(2)}) copy-start(bf16[2048,1024]{1,0:T(8,128)(2,1)} %matrix_ref.1) | copy-start | bytes 12582916
  2.0 8.5 %collective-permute-start = (bf16[16,2176]{1,0:T(8,128)(2,1)S(1)}, bf16[16,2176]{1,0:T(8,128)(2,1)S(1)}, u32[]{:S(2)}, u32[]{:S(2)}) collective-permute-start(bf16[16,2176]{1,0:T(8,128)(2,1)S(1)} %get-tuple-element.24), channel_id=1, source_target_pairs={{0,8},{1,9},{2,10},{3,11},{4,12},{5,13},{6,14},{7,15},{8,0},{9,1},... | collective-permute-start | bytes 208904 | tf_op jit(solution)/shard_map/ppermute | solution.py:294
  6.1 4.4 %collective-permute-start.1 = (bf16[16,2176]{1,0:T(8,128)(2,1)S(1)}, bf16[16,2176]{1,0:T(8,128)(2,1)S(1)}, u32[]{:S(2)}, u32[]{:S(2)}) collective-permute-start(bf16[16,2176]{1,0:T(8,128)(2,1)S(1)} %get-tuple-element.25), channel_id=1, source_target_pairs={{0,4},{1,5},{2,6},{3,7},{4,0},{5,1},{6,2},{7,3},{8,12},{9,13},{10,... | collective-permute-start | bytes 208904 | tf_op jit(solution)/shard_map/ppermute | solution.py:294
  7.7 6.1 %collective-permute-start.2 = (bf16[16,2176]{1,0:T(8,128)(2,1)S(1)}, bf16[16,2176]{1,0:T(8,128)(2,1)S(1)}, u32[]{:S(2)}, u32[]{:S(2)}) collective-permute-start(bf16[16,2176]{1,0:T(8,128)(2,1)S(1)} %get-tuple-element.26), channel_id=1, source_target_pairs={{0,12},{1,13},{2,14},{3,15},{4,8},{5,9},{6,10},{7,11},{8,4},{9,5},... | collective-permute-start | bytes 208904 | tf_op jit(solution)/shard_map/ppermute | solution.py:294
  9.7 4.1 %copy-start.3 = (bf16[4,64,2048]{2,1,0:T(8,128)(2,1)S(1)}, bf16[4,64,2048]{2,1,0:T(8,128)(2,1)}, u32[]{:S(2)}) copy-start(bf16[4,64,2048]{2,1,0:T(8,128)(2,1)} %param.15) | copy-start | bytes 3145732
  10.5 8.0 %copy-start.4 = (bf16[4,64,1024]{2,1,0:T(8,128)(2,1)S(1)}, bf16[4,64,1024]{2,1,0:T(8,128)(2,1)}, u32[]{:S(2)}) copy-start(bf16[4,64,1024]{2,1,0:T(8,128)(2,1)} %param.16) | copy-start | bytes 1572868
  10.5 12.5 %copy-start.7 = (f32[256]{0:T(256)S(1)}, f32[256]{0:T(256)}, u32[]{:S(2)}) copy-start(f32[256]{0:T(256)} %param.14) | copy-start | bytes 3076
  10.5 12.5 %copy-start.8 = (s32[32,1]{0,1:T(1,128)S(1)}, s32[32,1]{0,1:T(1,128)}, u32[]{:S(2)}) copy-start(s32[32,1]{0,1:T(1,128)} %param.17) | copy-start | bytes 388
  14.4 3.7 %collective-permute-start.3 = (bf16[128,128]{1,0:T(8,128)(2,1)S(1)}, bf16[128,128]{1,0:T(8,128)(2,1)S(1)}, u32[]{:S(2)}, u32[]{:S(2)}) collective-permute-start(bf16[128,128]{1,0:T(8,128)(2,1)S(1)} %get-tuple-element.31), channel_id=1, source_target_pairs={{0,3},{1,2},{2,1},{3,0},{4,7},{5,6},{6,5},{7,4},{8,11},{9,10},{10,... | collective-permute-start | bytes 98312 | tf_op jit(solution)/shard_map/ppermute | solution.py:294
  14.5 4.0 %collective-permute-start.4 = (bf16[128,128]{1,0:T(8,128)(2,1)S(1)}, bf16[128,128]{1,0:T(8,128)(2,1)S(1)}, u32[]{:S(2)}, u32[]{:S(2)}) collective-permute-start(bf16[128,128]{1,0:T(8,128)(2,1)S(1)} %get-tuple-element.32), channel_id=1, source_target_pairs={{0,2},{1,3},{2,0},{3,1},{4,6},{5,7},{6,4},{7,5},{8,10},{9,11},{10,... | collective-permute-start | bytes 98312 | tf_op jit(solution)/shard_map/ppermute | solution.py:294
  16.0 2.5 %collective-permute-start.5 = (bf16[128,128]{1,0:T(8,128)(2,1)S(1)}, bf16[128,128]{1,0:T(8,128)(2,1)S(1)}, u32[]{:S(2)}, u32[]{:S(2)}) collective-permute-start(bf16[128,128]{1,0:T(8,128)(2,1)S(1)} %get-tuple-element.33), channel_id=1, source_target_pairs={{0,1},{1,0},{2,3},{3,2},{4,5},{5,4},{6,7},{7,6},{8,9},{9,8},{10,11... | collective-permute-start | bytes 98312 | tf_op jit(solution)/shard_map/ppermute | solution.py:294
  18.8 4.9 %collective-permute-start.6 = (bf16[16,256]{1,0:T(8,128)(2,1)S(1)}, bf16[16,256]{1,0:T(8,128)(2,1)S(1)}, u32[]{:S(2)}, u32[]{:S(2)}) collective-permute-start(bf16[16,256]{1,0:T(8,128)(2,1)S(1)} %get-tuple-element.37), channel_id=1, source_target_pairs={{0,13},{1,12},{2,15},{3,14},{4,9},{5,8},{6,11},{7,10},{8,5},{9,4},... | collective-permute-start | bytes 24584 | tf_op jit(solution)/shard_map/ppermute | solution.py:294
  20.3 4.0 %collective-permute-start.7 = (bf16[16,256]{1,0:T(8,128)(2,1)S(1)}, bf16[16,256]{1,0:T(8,128)(2,1)S(1)}, u32[]{:S(2)}, u32[]{:S(2)}) collective-permute-start(bf16[16,256]{1,0:T(8,128)(2,1)S(1)} %get-tuple-element.38), channel_id=1, source_target_pairs={{0,9},{1,8},{2,11},{3,10},{4,13},{5,12},{6,15},{7,14},{8,1},{9,0},... | collective-permute-start | bytes 24584 | tf_op jit(solution)/shard_map/ppermute | solution.py:294
  21.0 3.4 %collective-permute-start.8 = (bf16[16,256]{1,0:T(8,128)(2,1)S(1)}, bf16[16,256]{1,0:T(8,128)(2,1)S(1)}, u32[]{:S(2)}, u32[]{:S(2)}) collective-permute-start(bf16[16,256]{1,0:T(8,128)(2,1)S(1)} %get-tuple-element.39), channel_id=1, source_target_pairs={{0,5},{1,4},{2,7},{3,6},{4,1},{5,0},{6,3},{7,2},{8,13},{9,12},{10,... | collective-permute-start | bytes 24584 | tf_op jit(solution)/shard_map/ppermute | solution.py:294

commit v6 on v5

--- a/solution.py
+++ b/solution.py
@@ -109,23 +109,42 @@
     turned = turned.astype(f32).astype(bf16)
     copies[2].wait()
     packed = jnp.dot(turned, rows_ref[...], preferred_element_type=f32).astype(bf16)
-    size = outs[0].shape[0]
+    size = blocks * capacity // len(outs)
     for b, out in enumerate(outs):
-        out[:, :width] = packed[b * size : (b + 1) * size]
-        out[:, width:] = slots[b * size : (b + 1) * size]
+        block, marks = packed[b * size : (b + 1) * size], slots[b * size : (b + 1) * size]
+        if not relative:
+            out[:, :width] = block
+            out[:, width:] = marks
+            continue
+        for c in range(width // lanes):
+            out[c * size : (c + 1) * size, :] = block[:, c * lanes : (c + 1) * lanes]
+        half, wide = size // 2, lanes // 2
+        out[size * (width // lanes) :, :] = jnp.concatenate(
+            [marks[:half, :wide], marks[half:, :wide]], axis=1
+        )
 
 
 def rank_kernel(pieces, adapters, *refs):
     got = refs[:pieces]
     down_ref, base_ref, rank_ref, slot_ref = refs[pieces : pieces + 4]
     messages = refs[pieces + 4 :]
-    features = down_ref.shape[1]
-    rows = jnp.concatenate([ref[:, :features] for ref in got], axis=0)
-    slots = jnp.concatenate([ref[:, features:] for ref in got], axis=0).astype(f32)
-    slot_ref[...] = slots
-    across = (((1,), (1,)), ((), ()))
-    projected = lax.dot_general(rows, down_ref[...], across, preferred_element_type=f32)
-    width = down_ref.shape[0] // adapters
+    features = down_ref.shape[0]
+    if pieces == 1:
+        rows, slots = got[0][:, :features], got[0][:, features:].astype(f32)
+    else:
+        size, tiles, wide = slot_ref.shape[0] // pieces, features // lanes, lanes // 2
+        rows = jnp.concatenate(
+            [
+                jnp.concatenate([ref[c * size : (c + 1) * size, :] for ref in got], axis=0)
+                for c in range(tiles)
+            ],
+            axis=1,
+        )
+        marks = [ref[tiles * size :, :].astype(f32) for ref in got]
+        slots = jnp.concatenate([m[:, h : h + wide] for m in marks for h in (0, wide)], axis=0)
+    slot_ref[...] = slots[:, : slot_ref.shape[1]]
+    projected = jnp.dot(rows, down_ref[...], preferred_element_type=f32)
+    width = down_ref.shape[1] // adapters
     total = None
     for a in range(adapters):
         term = projected[:, a * width : (a + 1) * width]
@@ -163,8 +182,9 @@
     half = outs[0].shape[1]
     first = pl.multiple_of(lax.axis_index("tensor") // 2 * 2 * half, 2 * half)
     factor = up_ref[:, pl.ds(first, 2 * half)]
-    term = jnp.dot(upper, factor, preferred_element_type=f32)
-    term = adapter_scale * (term + jnp.dot(lower, factor, preferred_element_type=f32))
+    both = jnp.concatenate([upper, lower], axis=0)
+    both = jnp.dot(both, factor, preferred_element_type=f32)
+    term = adapter_scale * (both[:count] + both[count:])
     term = term.astype(bf16).astype(f32)
     odd = lax.axis_index("tensor") % 2 == 1
     own = jnp.where(odd, term[:, half:], term[:, :half])
@@ -209,6 +229,10 @@
         own = slice(h * group, (h + 1) * group)
         context = cached_ref[:, own, :] + fresh_ref[:, own, :] * value[:, None, :]
         context_ref[:, own, :] = context.astype(bf16)
+
+
+def turn_kernel(in_ref, out):
+    out[...] = in_ref[...].T
 
 
 def base_kernel(rows_ref, matrix_ref, out):
@@ -326,10 +350,13 @@
 
     pieces = replicas if direct else 1
     piece = slots // pieces
+    message = (piece, features + lanes)
+    if direct:
+        message = (piece * (features // lanes) + piece // 2, lanes)
     local_rows, *packed = call(
         functools.partial(pack_kernel, replicas, capacity, direct),
         "pack",
-        [struct(activations.shape, bf16)] + [struct((piece, features + lanes), bf16)] * pieces,
+        [struct(activations.shape, bf16)] + [struct(message, bf16)] * pieces,
         [stay(home_row), stay(adapter_position.reshape(1, rows)), stay(activations)],
         pack_cost,
         in_specs=[HBM] * 3,
@@ -347,22 +374,32 @@
     else:
         got = [shuffle(packed[0])]
     base = base_product(local_rows, value_matrix, parts)
-    cached, fresh = attention(
-        lengths, queries, cached_key_rows, cached_value_rows, incoming_keys
-    )
-    base, cached, fresh = lax.optimization_barrier((base, cached, fresh))
+    (down,) = call(
+        turn_kernel,
+        "turn",
+        [struct((features, adapters * rank), bf16)],
+        [adapter_down_factors.reshape(adapters * rank, features)],
+        200_000_000,
+        in_specs=[VMEM],
+        out_specs=[VMEM],
+    )
     long = rows * (width // lanes) + slots
     rank_own, slot_ids, *messages = call(
         functools.partial(rank_kernel, pieces, adapters),
         "rank",
-        [struct((slots, rank), f32), struct((slots, lanes), f32)]
+        [struct((slots, rank), f32), struct((slots, rank), f32)]
         + [struct((long, lanes), bf16)] * (parts - 1),
-        [*got, adapter_down_factors.reshape(adapters * rank, features), base],
+        [*got, down, base],
         2 * slots * adapters * rank * features,
         in_specs=[VMEM] * (pieces + 2),
         out_specs=[VMEM] * (parts + 1),
     )
     heard = [send(messages[d - 1], lambda r, t: (r, t ^ d)) for d in tensor_order(parts)]
+    rank_own, held_lengths = lax.optimization_barrier((rank_own, lengths))
+    cached, fresh = attention(
+        held_lengths, queries, cached_key_rows, cached_value_rows, incoming_keys
+    )
+    rank_own, cached, fresh = lax.optimization_barrier((rank_own, cached, fresh))
     up_rows = adapter_up_factors.reshape(adapters * rank, parts * width)
     terms = call(
         functools.partial(up_kernel, parts - 1, adapters, direct),

time: 25.4 us -> 25.1 us (0.988)
  waiting for transfers between devices: 6.61 us -> 5.76 us
  local copies, waits for them, and re-layouts: 0.04 us -> 0.45 us
    ppermute x9, waiting for transfers between devices: 6.61 us -> 5.76 us  [send(): return lax.ppermute(block, ('replica', 'tensor'), pairs)]
    unnamed x20, local copies, waits for them, and re-layouts: 0.04 us -> 0.45 us
    pallas_call x7 -> x8, Pallas kernels: 6.14 us -> 6.29 us  [call(): pl.pallas_call(kernel, name=name, out_shape=outs, cost_estimate=pl.CostEs...]
  transfers between devices with their start and end apart: 9 -> 9, of which waited for: 6 -> 6; matrix products, arithmetic and copies ran while one was open for 0% -> 0% of each run, Pallas kernels for 12% -> 13%
where the time goes in v6:
time: 25.1 us; the launch traced here: 24.9 us
  starting transfers between devices  11.7 us (47%)
  Pallas kernels  6.29 us (25%)
  waiting for transfers between devices  5.76 us (23%)
  between operations  0.74 us (3%)
  local copies, waits for them, and re-layouts  0.45 us (2%)
    ppermute x9, starting transfers between devices, send(): return lax.ppermute(block, ('replica', 'tensor'), pairs)  11.7 us
    pallas_call x8, Pallas kernels, call(): pl.pallas_call(kernel, name=name, out_shape=outs, cost_estimate=pl.CostEs...  6.29 us
    ppermute x9, waiting for transfers between devices, send(): return lax.ppermute(block, ('replica', 'tensor'), pairs)  5.76 us
  transfers between devices with their start and end apart: 9, of which 6 were waited for; matrix products, arithmetic and copies ran while one was open for 0% of the time, Pallas kernels for 13%

profile of v6, /device:TPU:0, one launch (start us, length us, event | category | flops | bytes accessed | tf_op | source)
XLA Modules:
  0.0 24.9 jit_solution(6721707299979334450)
XLA Ops:
  0.6 0.0 copy-start
  0.6 1.3 %pack.1 = (bf16[32,2048]{1,0:T(8,128)(2,1)S(1)}, bf16[264,128]{1,0:T(8,128)(2,1)S(1)}, bf16[264,128]{1,0:T(8,128)(2,1)S(1)}, bf16[264,128]{1,0:T(8,128)(2,1)S(1)}, bf16[264,128]{1,0:T(8,128)(2,1)S(1)}) custom-call(s32[1,32]{1,0:T(1,128)} %bitcast.8, s32[1,32]{1,0:T(1,128)} %bitcast.10, bf16[32,2048]{1,0:T(8,128)(2,1)} %rows_hbm.1), custom_call_target="tpu_custom_call" | custom-call | flops 40000000000 | bytes 532736 | tf_op jit(solution)/shard_map/pack/pallas_call | solution.py:22
  2.0 4.1 %collective-permute-start = (bf16[264,128]{1,0:T(8,128)(2,1)S(1)}, bf16[264,128]{1,0:T(8,128)(2,1)S(1)}, u32[]{:S(2)}, u32[]{:S(2)}) collective-permute-start(bf16[264,128]{1,0:T(8,128)(2,1)S(1)} %get-tuple-element.26), channel_id=1, source_target_pairs={{0,8},{1,9},{2,10},{3,11},{4,12},{5,13},{6,14},{7,15},{8,0},{9,1},... | collective-permute-start | bytes 202760 | tf_op jit(solution)/shard_map/ppermute | solution.py:318
  6.1 1.6 %collective-permute-start.1 = (bf16[264,128]{1,0:T(8,128)(2,1)S(1)}, bf16[264,128]{1,0:T(8,128)(2,1)S(1)}, u32[]{:S(2)}, u32[]{:S(2)}) collective-permute-start(bf16[264,128]{1,0:T(8,128)(2,1)S(1)} %get-tuple-element.27), channel_id=1, source_target_pairs={{0,4},{1,5},{2,6},{3,7},{4,0},{5,1},{6,2},{7,3},{8,12},{9,13},{10,... | collective-permute-start | bytes 202760 | tf_op jit(solution)/shard_map/ppermute | solution.py:318
  7.6 0.0 collective-permute-start.2
  7.7 0.0 copy-done
  7.7 0.0 copy-start.3
  7.7 0.8 %base.1.refs_5_.refs_3_ = f32[4,32,256]{2,1,0:T(8,128)S(1)} custom-call(bf16[32,2048]{1,0:T(8,128)(2,1)S(1)} %get-tuple-element.29.rows_ref, bf16[2048,1024]{1,0:T(8,128)(2,1)S(1)} %copy-done), custom_call_target="tpu_custom_call" | custom-call | flops 134217728 | bytes 4456448 | tf_op jit(solution)/shard_map/base/pallas_call | solution.py:22
  8.5 0.4 %copy-done.3 = bf16[4,64,2048]{2,1,0:T(8,128)(2,1)S(1)} copy-done((bf16[4,64,2048]{2,1,0:T(8,128)(2,1)S(1)}, bf16[4,64,2048]{2,1,0:T(8,128)(2,1)}, u32[]{:S(2)}) %copy-start.3) | copy-done | bytes 1048600
  8.9 0.0 copy-start.1
  8.9 0.0 copy-start.2
  8.9 0.0 copy-start.5
  8.9 0.0 copy-start.6
  8.9 0.0 copy-start.9
  8.9 0.3 %turn.1.refs_4_ = bf16[2048,256]{1,0:T(8,128)(2,1)S(1)} custom-call(bf16[256,2048]{1,0:T(8,128)(2,1)S(1)} %bitcast.5), custom_call_target="tpu_custom_call" | custom-call | flops 200000000 | bytes 2097152 | tf_op jit(solution)/shard_map/turn/pallas_call | solution.py:22
  9.2 0.0 collective-permute-done.refs_1_
  9.2 1.1 %collective-permute-done.1.refs_2_ = bf16[264,128]{1,0:T(8,128)(2,1)S(1)} collective-permute-done((bf16[264,128]{1,0:T(8,128)(2,1)S(1)}, bf16[264,128]{1,0:T(8,128)(2,1)S(1)}, u32[]{:S(2)}, u32[]{:S(2)}) %collective-permute-start.1) | collective-permute-done | bytes 67616 | tf_op jit(solution)/shard_map/ppermute | solution.py:318
  10.4 3.4 %collective-permute-done.2.refs_3_ = bf16[264,128]{1,0:T(8,128)(2,1)S(1)} collective-permute-done((bf16[264,128]{1,0:T(8,128)(2,1)S(1)}, bf16[264,128]{1,0:T(8,128)(2,1)S(1)}, u32[]{:S(2)}, u32[]{:S(2)}) %collective-permute-start.2) | collective-permute-done | bytes 67616 | tf_op jit(solution)/shard_map/ppermute | solution.py:318
  13.7 0.4 %rank.1 = (f32[64,64]{1,0:T(8,128)S(1)}, f32[64,64]{1,0:T(8,128)S(1)}, bf16[128,128]{1,0:T(8,128)(2,1)S(1)}, bf16[128,128]{1,0:T(8,128)(2,1)S(1)}, bf16[128,128]{1,0:T(8,128)(2,1)S(1)}) custom-call(bf16[264,128]{1,0:T(8,128)(2,1)S(1)} %get-tuple-element.25.refs_0_, bf16[264,128]{1,0:T(8,128)(2,1)S(1)} %collective-permute-done.refs_1_, ...), custom_call_target="tpu_custom_call" | custom-call | flops 67108864 | bytes 1581056 | tf_op jit(solution)/shard_map/rank/pallas_call | solution.py:22
  14.2 0.1 collective-permute-start.3
  14.3 1.5 %collective-permute-start.4 = (bf16[128,128]{1,0:T(8,128)(2,1)S(1)}, bf16[128,128]{1,0:T(8,128)(2,1)S(1)}, u32[]{:S(2)}, u32[]{:S(2)}) collective-permute-start(bf16[128,128]{1,0:T(8,128)(2,1)S(1)} %get-tuple-element.31), channel_id=1, source_target_pairs={{0,2},{1,3},{2,0},{3,1},{4,6},{5,7},{6,4},{7,5},{8,10},{9,11},{10,... | collective-permute-start | bytes 98312 | tf_op jit(solution)/shard_map/ppermute | solution.py:318
  15.8 0.3 %collective-permute-start.5 = (bf16[128,128]{1,0:T(8,128)(2,1)S(1)}, bf16[128,128]{1,0:T(8,128)(2,1)S(1)}, u32[]{:S(2)}, u32[]{:S(2)}) collective-permute-start(bf16[128,128]{1,0:T(8,128)(2,1)S(1)} %get-tuple-element.32), channel_id=1, source_target_pairs={{0,1},{1,0},{2,3},{3,2},{4,5},{5,4},{6,7},{7,6},{8,9},{9,8},{10,11... | collective-permute-start | bytes 98312 | tf_op jit(solution)/shard_map/ppermute | solution.py:318
  16.1 0.0 copy-done.1
  16.1 0.0 copy-done.2
  16.1 0.0 copy-done.5
  16.1 0.0 copy-done.6
  16.1 0.0 copy-done.9
  16.1 0.0 copy-start.4
  16.1 0.0 copy-start.7
  16.2 0.0 copy-start.8
  16.2 1.9 %attention.1 = (f32[32,16,128]{2,1,0:T(8,128)S(1)}, f32[32,16,128]{2,1,0:T(8,128)S(1)}) custom-call(s32[32]{0:T(128)S(1)} %copy-done.9, bf16[32,16,128]{2,1,0:T(8,128)(2,1)S(1)} %copy-done.5, bf16[32,2,96,128]{3,2,1,0:T(8,128)(2,1)S(1)} %copy-done.1, bf16[32,2,96,128]{3,2,1,0:T(8,128)(2,1)S(1)} %copy-done.2, bf16[32,2,128]{2,1,0:T(2,128)(2,1)S(1)} %copy-done.6), custom_call_target="tpu_custom_call" | custom-call | flops 25165824 | bytes 3817600 | tf_op jit(solution)/shard_map/attention/pallas_call | solution.py:22
  18.1 0.0 collective-permute-done.3.refs_0_
  18.1 0.2 collective-permute-done.4.refs_1_
  18.3 0.0 collective-permute-done.5.refs_2_
  18.3 0.0 copy-done.4
  18.3 0.3 %up.1 = (bf16[16,256]{1,0:T(8,128)(2,1)S(1)}, bf16[16,256]{1,0:T(8,128)(2,1)S(1)}, bf16[16,256]{1,0:T(8,128)(2,1)S(1)}, bf16[16,256]{1,0:T(8,128)(2,1)S(1)}) custom-call(bf16[128,128]{1,0:T(8,128)(2,1)S(1)} %collective-permute-done.3.refs_0_, bf16[128,128]{1,0:T(8,128)(2,1)S(1)} %collective-permute-done.4.refs_1_, ...), custom_call_target="tpu_custom_call" | custom-call | flops 33554432 | bytes 688128 | tf_op jit(solution)/shard_map/up/pallas_call | solution.py:22
  18.6 1.3 %collective-permute-start.6 = (bf16[16,256]{1,0:T(8,128)(2,1)S(1)}, bf16[16,256]{1,0:T(8,128)(2,1)S(1)}, u32[]{:S(2)}, u32[]{:S(2)}) collective-permute-start(bf16[16,256]{1,0:T(8,128)(2,1)S(1)} %get-tuple-element.41), channel_id=1, source_target_pairs={{0,13},{1,12},{2,15},{3,14},{4,9},{5,8},{6,11},{7,10},{8,5},{9,4},... | collective-permute-start | bytes 24584 | tf_op jit(solution)/shard_map/ppermute | solution.py:318
  20.0 0.7 %collective-permute-start.7 = (bf16[16,256]{1,0:T(8,128)(2,1)S(1)}, bf16[16,256]{1,0:T(8,128)(2,1)S(1)}, u32[]{:S(2)}, u32[]{:S(2)}) collective-permute-start(bf16[16,256]{1,0:T(8,128)(2,1)S(1)} %get-tuple-element.42), channel_id=1, source_target_pairs={{0,9},{1,8},{2,11},{3,10},{4,13},{5,12},{6,15},{7,14},{8,1},{9,0},... | collective-permute-start | bytes 24584 | tf_op jit(solution)/shard_map/ppermute | solution.py:318
  20.7 2.1 %collective-permute-start.8 = (bf16[16,256]{1,0:T(8,128)(2,1)S(1)}, bf16[16,256]{1,0:T(8,128)(2,1)S(1)}, u32[]{:S(2)}, u32[]{:S(2)}) collective-permute-start(bf16[16,256]{1,0:T(8,128)(2,1)S(1)} %get-tuple-element.43), channel_id=1, source_target_pairs={{0,5},{1,4},{2,7},{3,6},{4,1},{5,0},{6,3},{7,2},{8,13},{9,12},{10,... | collective-permute-start | bytes 24584 | tf_op jit(solution)/shard_map/ppermute | solution.py:318
  22.7 0.0 copy-done.7
  22.7 0.0 copy-done.8
  22.7 0.3 %base_sum.1 = (f32[32,256]{1,0:T(8,128)S(1)}, bf16[32,64]{1,0:T(8,128)(2,1)S(1)}) custom-call(bf16[128,128]{1,0:T(8,128)(2,1)S(1)} %collective-permute-done.3.refs_0_, bf16[128,128]{1,0:T(8,128)(2,1)S(1)} %collective-permute-done.4.refs_1_, bf16[128,128]{1,0:T(8,128)(2,1)S(1)} %collective-permute-done.5.refs_2_, f32[4,32,256]{2,1,0:T(8,128)S(1)} %base.1.refs_5_.refs_3_, ...), custom_call_target="tpu_custom_call" | custom-call | flops 32768 | bytes 267392 | tf_op jit(solution)/shard_map/base_sum/pallas_call | solution.py:22
  23.0 0.5 %collective-permute-done.6.refs_1_ = bf16[16,256]{1,0:T(8,128)(2,1)S(1)} collective-permute-done((bf16[16,256]{1,0:T(8,128)(2,1)S(1)}, bf16[16,256]{1,0:T(8,128)(2,1)S(1)}, u32[]{:S(2)}, u32[]{:S(2)}) %collective-permute-start.6) | collective-permute-done | bytes 8224 | tf_op jit(solution)/shard_map/ppermute | solution.py:318
  23.5 0.4 %collective-permute-done.7.refs_2_ = bf16[16,256]{1,0:T(8,128)(2,1)S(1)} collective-permute-done((bf16[16,256]{1,0:T(8,128)(2,1)S(1)}, bf16[16,256]{1,0:T(8,128)(2,1)S(1)}, u32[]{:S(2)}, u32[]{:S(2)}) %collective-permute-start.7) | collective-permute-done | bytes 8224 | tf_op jit(solution)/shard_map/ppermute | solution.py:318
  23.9 0.1 collective-permute-done.8.refs_3_
  24.1 0.9 %last.1 = (bf16[32,16,128]{2,1,0:T(8,128)(2,1)}, bf16[32,2,128]{2,1,0:T(2,128)(2,1)}) custom-call(bf16[16,256]{1,0:T(8,128)(2,1)S(1)} %get-tuple-element.40.refs_0_, bf16[16,256]{1,0:T(8,128)(2,1)S(1)} %collective-permute-done.6.refs_1_, bf16[16,256]{1,0:T(8,128)(2,1)S(1)} %collective-permute-done.7.refs_2_, ...), custom_call_target="tpu_custom_call" | custom-call | flops 1048576 | bytes 741376 | tf_op jit(solution)/shard_map/last/pallas_call | solution.py:22
Async XLA Ops:
  0.6 7.0 %copy-start = (bf16[2048,1024]{1,0:T(8,128)(2,1)S(1)}, bf16[2048,1024]{1,0:T(8,128)(2,1)}, u32[]{:S(2)}) copy-start(bf16[2048,1024]{1,0:T(8,128)(2,1)} %matrix_ref.1) | copy-start | bytes 12582916
  2.0 7.3 %collective-permute-start = (bf16[264,128]{1,0:T(8,128)(2,1)S(1)}, bf16[264,128]{1,0:T(8,128)(2,1)S(1)}, u32[]{:S(2)}, u32[]{:S(2)}) collective-permute-start(bf16[264,128]{1,0:T(8,128)(2,1)S(1)} %get-tuple-element.26), channel_id=1, source_target_pairs={{0,8},{1,9},{2,10},{3,11},{4,12},{5,13},{6,14},{7,15},{8,0},{9,1},... | collective-permute-start | bytes 202760 | tf_op jit(solution)/shard_map/ppermute | solution.py:318
  6.1 4.3 %collective-permute-start.1 = (bf16[264,128]{1,0:T(8,128)(2,1)S(1)}, bf16[264,128]{1,0:T(8,128)(2,1)S(1)}, u32[]{:S(2)}, u32[]{:S(2)}) collective-permute-start(bf16[264,128]{1,0:T(8,128)(2,1)S(1)} %get-tuple-element.27), channel_id=1, source_target_pairs={{0,4},{1,5},{2,6},{3,7},{4,0},{5,1},{6,2},{7,3},{8,12},{9,13},{10,... | collective-permute-start | bytes 202760 | tf_op jit(solution)/shard_map/ppermute | solution.py:318
  7.6 6.1 %collective-permute-start.2 = (bf16[264,128]{1,0:T(8,128)(2,1)S(1)}, bf16[264,128]{1,0:T(8,128)(2,1)S(1)}, u32[]{:S(2)}, u32[]{:S(2)}) collective-permute-start(bf16[264,128]{1,0:T(8,128)(2,1)S(1)} %get-tuple-element.28), channel_id=1, source_target_pairs={{0,12},{1,13},{2,14},{3,15},{4,8},{5,9},{6,10},{7,11},{8,4},{9,5},... | collective-permute-start | bytes 202760 | tf_op jit(solution)/shard_map/ppermute | solution.py:318
  7.7 1.2 %copy-start.3 = (bf16[4,64,2048]{2,1,0:T(8,128)(2,1)S(1)}, bf16[4,64,2048]{2,1,0:T(8,128)(2,1)}, u32[]{:S(2)}) copy-start(bf16[4,64,2048]{2,1,0:T(8,128)(2,1)} %param.15) | copy-start | bytes 3145732
  8.9 7.2 %copy-start.1 = (bf16[32,2,96,128]{3,2,1,0:T(8,128)(2,1)S(1)}, bf16[32,2,96,128]{3,2,1,0:T(8,128)(2,1)}, u32[]{:S(2)}) copy-start(bf16[32,2,96,128]{3,2,1,0:T(8,128)(2,1)} %key_ref.1) | copy-start | bytes 4718596
  8.9 7.2 %copy-start.2 = (bf16[32,2,96,128]{3,2,1,0:T(8,128)(2,1)S(1)}, bf16[32,2,96,128]{3,2,1,0:T(8,128)(2,1)}, u32[]{:S(2)}) copy-start(bf16[32,2,96,128]{3,2,1,0:T(8,128)(2,1)} %value_ref.1) | copy-start | bytes 4718596
  8.9 7.2 %copy-start.5 = (bf16[32,16,128]{2,1,0:T(8,128)(2,1)S(1)}, bf16[32,16,128]{2,1,0:T(8,128)(2,1)}, u32[]{:S(2)}) copy-start(bf16[32,16,128]{2,1,0:T(8,128)(2,1)} %query_ref.1) | copy-start | bytes 393220
  8.9 7.2 %copy-start.6 = (bf16[32,2,128]{2,1,0:T(2,128)(2,1)S(1)}, bf16[32,2,128]{2,1,0:T(2,128)(2,1)}, u32[]{:S(2)}) copy-start(bf16[32,2,128]{2,1,0:T(2,128)(2,1)} %new_ref.1) | copy-start | bytes 49156
  8.9 7.2 %copy-start.9 = (s32[32]{0:T(128)S(1)}, s32[32]{0:T(128)}, u32[]{:S(2)}) copy-start(s32[32]{0:T(128)} %length_ref) | copy-start | bytes 388
  14.2 3.9 %collective-permute-start.3 = (bf16[128,128]{1,0:T(8,128)(2,1)S(1)}, bf16[128,128]{1,0:T(8,128)(2,1)S(1)}, u32[]{:S(2)}, u32[]{:S(2)}) collective-permute-start(bf16[128,128]{1,0:T(8,128)(2,1)S(1)} %get-tuple-element.30), channel_id=1, source_target_pairs={{0,3},{1,2},{2,1},{3,0},{4,7},{5,6},{6,5},{7,4},{8,11},{9,10},{10,... | collective-permute-start | bytes 98312 | tf_op jit(solution)/shard_map/ppermute | solution.py:318
  14.3 4.0 %collective-permute-start.4 = (bf16[128,128]{1,0:T(8,128)(2,1)S(1)}, bf16[128,128]{1,0:T(8,128)(2,1)S(1)}, u32[]{:S(2)}, u32[]{:S(2)}) collective-permute-start(bf16[128,128]{1,0:T(8,128)(2,1)S(1)} %get-tuple-element.31), channel_id=1, source_target_pairs={{0,2},{1,3},{2,0},{3,1},{4,6},{5,7},{6,4},{7,5},{8,10},{9,11},{10,... | collective-permute-start | bytes 98312 | tf_op jit(solution)/shard_map/ppermute | solution.py:318
  15.8 2.5 %collective-permute-start.5 = (bf16[128,128]{1,0:T(8,128)(2,1)S(1)}, bf16[128,128]{1,0:T(8,128)(2,1)S(1)}, u32[]{:S(2)}, u32[]{:S(2)}) collective-permute-start(bf16[128,128]{1,0:T(8,128)(2,1)S(1)} %get-tuple-element.32), channel_id=1, source_target_pairs={{0,1},{1,0},{2,3},{3,2},{4,5},{5,4},{6,7},{7,6},{8,9},{9,8},{10,11... | collective-permute-start | bytes 98312 | tf_op jit(solution)/shard_map/ppermute | solution.py:318
  16.1 2.2 %copy-start.4 = (bf16[4,64,1024]{2,1,0:T(8,128)(2,1)S(1)}, bf16[4,64,1024]{2,1,0:T(8,128)(2,1)}, u32[]{:S(2)}) copy-start(bf16[4,64,1024]{2,1,0:T(8,128)(2,1)} %param.16) | copy-start | bytes 1572868
  16.1 6.6 %copy-start.7 = (f32[256]{0:T(256)S(1)}, f32[256]{0:T(256)}, u32[]{:S(2)}) copy-start(f32[256]{0:T(256)} %param.14) | copy-start | bytes 3076
  16.2 6.6 %copy-start.8 = (s32[32,1]{0,1:T(1,128)S(1)}, s32[32,1]{0,1:T(1,128)}, u32[]{:S(2)}) copy-start(s32[32,1]{0,1:T(1,128)} %param.17) | copy-start | bytes 388
  18.6 4.9 %collective-permute-start.6 = (bf16[16,256]{1,0:T(8,128)(2,1)S(1)}, bf16[16,256]{1,0:T(8,128)(2,1)S(1)}, u32[]{:S(2)}, u32[]{:S(2)}) collective-permute-start(bf16[16,256]{1,0:T(8,128)(2,1)S(1)} %get-tuple-element.41), channel_id=1, source_target_pairs={{0,13},{1,12},{2,15},{3,14},{4,9},{5,8},{6,11},{7,10},{8,5},{9,4},... | collective-permute-start | bytes 24584 | tf_op jit(solution)/shard_map/ppermute | solution.py:318
  20.0 4.0 %collective-permute-start.7 = (bf16[16,256]{1,0:T(8,128)(2,1)S(1)}, bf16[16,256]{1,0:T(8,128)(2,1)S(1)}, u32[]{:S(2)}, u32[]{:S(2)}) collective-permute-start(bf16[16,256]{1,0:T(8,128)(2,1)S(1)} %get-tuple-element.42), channel_id=1, source_target_pairs={{0,9},{1,8},{2,11},{3,10},{4,13},{5,12},{6,15},{7,14},{8,1},{9,0},... | collective-permute-start | bytes 24584 | tf_op jit(solution)/shard_map/ppermute | solution.py:318
  20.7 3.4 %collective-permute-start.8 = (bf16[16,256]{1,0:T(8,128)(2,1)S(1)}, bf16[16,256]{1,0:T(8,128)(2,1)S(1)}, u32[]{:S(2)}, u32[]{:S(2)}) collective-permute-start(bf16[16,256]{1,0:T(8,128)(2,1)S(1)} %get-tuple-element.43), channel_id=1, source_target_pairs={{0,5},{1,4},{2,7},{3,6},{4,1},{5,0},{6,3},{7,2},{8,13},{9,12},{10,... | collective-permute-start | bytes 24584 | tf_op jit(solution)/shard_map/ppermute | solution.py:318

commit v7 on v6

--- a/solution.py
+++ b/solution.py
@@ -151,9 +151,8 @@
         term = jnp.where(slots[:, :width] == a + 1.0, term, 0.0)
         total = term if total is None else total + term
     rank_ref[...] = total
-    upper = total.astype(bf16)
-    lower = (total - upper.astype(f32)).astype(bf16)
-    pair = jnp.concatenate([upper, lower], axis=1)
+    half = total.shape[0] // 2
+    pair = jnp.concatenate([total[:half], total[half:]], axis=1).astype(bf16)
     me = lax.axis_index("tensor")
     for d, message in enumerate(messages):
         block = base_ref[me ^ (d + 1)].astype(bf16)
@@ -171,8 +170,8 @@
     total = rank_ref[...]
     count, width = total.shape
     for ref in got:
-        pair = ref[ref.shape[0] - count :, :].astype(f32)
-        total = total + (pair[:, :width] + pair[:, width:])
+        pair = ref[ref.shape[0] - count // 2 :, :].astype(f32)
+        total = total + jnp.concatenate([pair[:, :width], pair[:, width:]], axis=0)
     slots = slot_ref[:, :width]
     wide = jnp.concatenate(
         [jnp.where(slots == a + 1.0, total, 0.0) for a in range(adapters)], axis=1
@@ -383,7 +382,7 @@
         in_specs=[VMEM],
         out_specs=[VMEM],
     )
-    long = rows * (width // lanes) + slots
+    long = rows * (width // lanes) + slots // 2
     rank_own, slot_ids, *messages = call(
         functools.partial(rank_kernel, pieces, adapters),
         "rank",

time: 25.1 us -> 24.9 us (level)
  transfers between devices with their start and end apart: 9 -> 9, of which waited for: 6 -> 6; matrix products, arithmetic and copies ran while one was open for 0% -> 0% of each run, Pallas kernels for 13% -> 14%
where the time goes in v7:
time: 24.9 us; the launch traced here: 24.8 us
  starting transfers between devices  11.7 us (47%)
  Pallas kernels  6.28 us (25%)
  waiting for transfers between devices  5.62 us (23%)
  between operations  0.74 us (3%)
  local copies, waits for them, and re-layouts  0.45 us (2%)
    ppermute x9, starting transfers between devices, send(): return lax.ppermute(block, ('replica', 'tensor'), pairs)  11.7 us
    pallas_call x8, Pallas kernels, call(): pl.pallas_call(kernel, name=name, out_shape=outs, cost_estimate=pl.CostEs...  6.28 us
    ppermute x9, waiting for transfers between devices, send(): return lax.ppermute(block, ('replica', 'tensor'), pairs)  5.62 us
  transfers between devices with their start and end apart: 9, of which 6 were waited for; matrix products, arithmetic and copies ran while one was open for 0% of the time, Pallas kernels for 14%

profile of v7, /device:TPU:0, one launch (start us, length us, event | category | flops | bytes accessed | tf_op | source)
XLA Modules:
  0.0 24.8 jit_solution(9629340544768963440)
XLA Ops:
  0.6 0.0 copy-start
  0.6 1.3 %pack.1 = (bf16[32,2048]{1,0:T(8,128)(2,1)S(1)}, bf16[264,128]{1,0:T(8,128)(2,1)S(1)}, bf16[264,128]{1,0:T(8,128)(2,1)S(1)}, bf16[264,128]{1,0:T(8,128)(2,1)S(1)}, bf16[264,128]{1,0:T(8,128)(2,1)S(1)}) custom-call(s32[1,32]{1,0:T(1,128)} %bitcast.8, s32[1,32]{1,0:T(1,128)} %bitcast.10, bf16[32,2048]{1,0:T(8,128)(2,1)} %rows_hbm.1), custom_call_target="tpu_custom_call" | custom-call | flops 40000000000 | bytes 532736 | tf_op jit(solution)/shard_map/pack/pallas_call | solution.py:22
  2.0 4.1 %collective-permute-start = (bf16[264,128]{1,0:T(8,128)(2,1)S(1)}, bf16[264,128]{1,0:T(8,128)(2,1)S(1)}, u32[]{:S(2)}, u32[]{:S(2)}) collective-permute-start(bf16[264,128]{1,0:T(8,128)(2,1)S(1)} %get-tuple-element.26), channel_id=1, source_target_pairs={{0,8},{1,9},{2,10},{3,11},{4,12},{5,13},{6,14},{7,15},{8,0},{9,1},... | collective-permute-start | bytes 202760 | tf_op jit(solution)/shard_map/ppermute | solution.py:317
  6.1 1.6 %collective-permute-start.1 = (bf16[264,128]{1,0:T(8,128)(2,1)S(1)}, bf16[264,128]{1,0:T(8,128)(2,1)S(1)}, u32[]{:S(2)}, u32[]{:S(2)}) collective-permute-start(bf16[264,128]{1,0:T(8,128)(2,1)S(1)} %get-tuple-element.27), channel_id=1, source_target_pairs={{0,4},{1,5},{2,6},{3,7},{4,0},{5,1},{6,2},{7,3},{8,12},{9,13},{10,... | collective-permute-start | bytes 202760 | tf_op jit(solution)/shard_map/ppermute | solution.py:317
  7.6 0.0 collective-permute-start.2
  7.7 0.0 copy-done
  7.7 0.0 copy-start.3
  7.7 0.8 %base.1.refs_5_.refs_3_ = f32[4,32,256]{2,1,0:T(8,128)S(1)} custom-call(bf16[32,2048]{1,0:T(8,128)(2,1)S(1)} %get-tuple-element.29.rows_ref, bf16[2048,1024]{1,0:T(8,128)(2,1)S(1)} %copy-done), custom_call_target="tpu_custom_call" | custom-call | flops 134217728 | bytes 4456448 | tf_op jit(solution)/shard_map/base/pallas_call | solution.py:22
  8.5 0.4 %copy-done.3 = bf16[4,64,2048]{2,1,0:T(8,128)(2,1)S(1)} copy-done((bf16[4,64,2048]{2,1,0:T(8,128)(2,1)S(1)}, bf16[4,64,2048]{2,1,0:T(8,128)(2,1)}, u32[]{:S(2)}) %copy-start.3) | copy-done | bytes 1048600
  8.9 0.0 copy-start.1
  8.9 0.0 copy-start.2
  8.9 0.0 copy-start.5
  8.9 0.0 copy-start.6
  8.9 0.0 copy-start.9
  8.9 0.3 %turn.1.refs_4_ = bf16[2048,256]{1,0:T(8,128)(2,1)S(1)} custom-call(bf16[256,2048]{1,0:T(8,128)(2,1)S(1)} %bitcast.5), custom_call_target="tpu_custom_call" | custom-call | flops 200000000 | bytes 2097152 | tf_op jit(solution)/shard_map/turn/pallas_call | solution.py:22
  9.2 0.0 collective-permute-done.refs_1_
  9.2 1.1 %collective-permute-done.1.refs_2_ = bf16[264,128]{1,0:T(8,128)(2,1)S(1)} collective-permute-done((bf16[264,128]{1,0:T(8,128)(2,1)S(1)}, bf16[264,128]{1,0:T(8,128)(2,1)S(1)}, u32[]{:S(2)}, u32[]{:S(2)}) %collective-permute-start.1) | collective-permute-done | bytes 67616 | tf_op jit(solution)/shard_map/ppermute | solution.py:317
  10.4 3.4 %collective-permute-done.2.refs_3_ = bf16[264,128]{1,0:T(8,128)(2,1)S(1)} collective-permute-done((bf16[264,128]{1,0:T(8,128)(2,1)S(1)}, bf16[264,128]{1,0:T(8,128)(2,1)S(1)}, u32[]{:S(2)}, u32[]{:S(2)}) %collective-permute-start.2) | collective-permute-done | bytes 67616 | tf_op jit(solution)/shard_map/ppermute | solution.py:317
  13.7 0.4 %rank.1 = (f32[64,64]{1,0:T(8,128)S(1)}, f32[64,64]{1,0:T(8,128)S(1)}, bf16[96,128]{1,0:T(8,128)(2,1)S(1)}, bf16[96,128]{1,0:T(8,128)(2,1)S(1)}, bf16[96,128]{1,0:T(8,128)(2,1)S(1)}) custom-call(bf16[264,128]{1,0:T(8,128)(2,1)S(1)} %get-tuple-element.25.refs_0_, bf16[264,128]{1,0:T(8,128)(2,1)S(1)} %collective-permute-done.refs_1_, ...), custom_call_target="tpu_custom_call" | custom-call | flops 67108864 | bytes 1556480 | tf_op jit(solution)/shard_map/rank/pallas_call | solution.py:22
  14.2 0.0 collective-permute-start.3
  14.2 1.5 %collective-permute-start.4 = (bf16[96,128]{1,0:T(8,128)(2,1)S(1)}, bf16[96,128]{1,0:T(8,128)(2,1)S(1)}, u32[]{:S(2)}, u32[]{:S(2)}) collective-permute-start(bf16[96,128]{1,0:T(8,128)(2,1)S(1)} %get-tuple-element.31), channel_id=1, source_target_pairs={{0,2},{1,3},{2,0},{3,1},{4,6},{5,7},{6,4},{7,5},{8,10},{9,11},{10,... | collective-permute-start | bytes 73736 | tf_op jit(solution)/shard_map/ppermute | solution.py:317
  15.8 0.3 %collective-permute-start.5 = (bf16[96,128]{1,0:T(8,128)(2,1)S(1)}, bf16[96,128]{1,0:T(8,128)(2,1)S(1)}, u32[]{:S(2)}, u32[]{:S(2)}) collective-permute-start(bf16[96,128]{1,0:T(8,128)(2,1)S(1)} %get-tuple-element.32), channel_id=1, source_target_pairs={{0,1},{1,0},{2,3},{3,2},{4,5},{5,4},{6,7},{7,6},{8,9},{9,8},{10,11... | collective-permute-start | bytes 73736 | tf_op jit(solution)/shard_map/ppermute | solution.py:317
  16.1 0.0 copy-done.1
  16.1 0.0 copy-done.2
  16.1 0.0 copy-done.5
  16.1 0.0 copy-done.6
  16.1 0.0 copy-done.9
  16.1 0.0 copy-start.4
  16.1 0.0 copy-start.7
  16.1 0.0 copy-start.8
  16.1 1.9 %attention.1 = (f32[32,16,128]{2,1,0:T(8,128)S(1)}, f32[32,16,128]{2,1,0:T(8,128)S(1)}) custom-call(s32[32]{0:T(128)S(1)} %copy-done.9, bf16[32,16,128]{2,1,0:T(8,128)(2,1)S(1)} %copy-done.5, bf16[32,2,96,128]{3,2,1,0:T(8,128)(2,1)S(1)} %copy-done.1, bf16[32,2,96,128]{3,2,1,0:T(8,128)(2,1)S(1)} %copy-done.2, bf16[32,2,128]{2,1,0:T(2,128)(2,1)S(1)} %copy-done.6), custom_call_target="tpu_custom_call" | custom-call | flops 25165824 | bytes 3817600 | tf_op jit(solution)/shard_map/attention/pallas_call | solution.py:22
  18.0 0.0 collective-permute-done.3.refs_0_
  18.0 0.1 collective-permute-done.4.refs_1_
  18.1 0.0 collective-permute-done.5.refs_2_
  18.1 0.0 copy-done.4
  18.1 0.3 %up.1 = (bf16[16,256]{1,0:T(8,128)(2,1)S(1)}, bf16[16,256]{1,0:T(8,128)(2,1)S(1)}, bf16[16,256]{1,0:T(8,128)(2,1)S(1)}, bf16[16,256]{1,0:T(8,128)(2,1)S(1)}) custom-call(bf16[96,128]{1,0:T(8,128)(2,1)S(1)} %collective-permute-done.3.refs_0_, bf16[96,128]{1,0:T(8,128)(2,1)S(1)} %collective-permute-done.4.refs_1_, ...), custom_call_target="tpu_custom_call" | custom-call | flops 33554432 | bytes 663552 | tf_op jit(solution)/shard_map/up/pallas_call | solution.py:22
  18.4 1.4 %collective-permute-start.6 = (bf16[16,256]{1,0:T(8,128)(2,1)S(1)}, bf16[16,256]{1,0:T(8,128)(2,1)S(1)}, u32[]{:S(2)}, u32[]{:S(2)}) collective-permute-start(bf16[16,256]{1,0:T(8,128)(2,1)S(1)} %get-tuple-element.41), channel_id=1, source_target_pairs={{0,13},{1,12},{2,15},{3,14},{4,9},{5,8},{6,11},{7,10},{8,5},{9,4},... | collective-permute-start | bytes 24584 | tf_op jit(solution)/shard_map/ppermute | solution.py:317
  19.8 0.6 %collective-permute-start.7 = (bf16[16,256]{1,0:T(8,128)(2,1)S(1)}, bf16[16,256]{1,0:T(8,128)(2,1)S(1)}, u32[]{:S(2)}, u32[]{:S(2)}) collective-permute-start(bf16[16,256]{1,0:T(8,128)(2,1)S(1)} %get-tuple-element.42), channel_id=1, source_target_pairs={{0,9},{1,8},{2,11},{3,10},{4,13},{5,12},{6,15},{7,14},{8,1},{9,0},... | collective-permute-start | bytes 24584 | tf_op jit(solution)/shard_map/ppermute | solution.py:317
  20.4 2.1 %collective-permute-start.8 = (bf16[16,256]{1,0:T(8,128)(2,1)S(1)}, bf16[16,256]{1,0:T(8,128)(2,1)S(1)}, u32[]{:S(2)}, u32[]{:S(2)}) collective-permute-start(bf16[16,256]{1,0:T(8,128)(2,1)S(1)} %get-tuple-element.43), channel_id=1, source_target_pairs={{0,5},{1,4},{2,7},{3,6},{4,1},{5,0},{6,3},{7,2},{8,13},{9,12},{10,... | collective-permute-start | bytes 24584 | tf_op jit(solution)/shard_map/ppermute | solution.py:317
  22.6 0.0 copy-done.7
  22.6 0.0 copy-done.8
  22.6 0.3 %base_sum.1 = (f32[32,256]{1,0:T(8,128)S(1)}, bf16[32,64]{1,0:T(8,128)(2,1)S(1)}) custom-call(bf16[96,128]{1,0:T(8,128)(2,1)S(1)} %collective-permute-done.3.refs_0_, bf16[96,128]{1,0:T(8,128)(2,1)S(1)} %collective-permute-done.4.refs_1_, bf16[96,128]{1,0:T(8,128)(2,1)S(1)} %collective-permute-done.5.refs_2_, f32[4,32,256]{2,1,0:T(8,128)S(1)} %base.1.refs_5_.refs_3_, ...), custom_call_target="tpu_custom_call" | custom-call | flops 32768 | bytes 242816 | tf_op jit(solution)/shard_map/base_sum/pallas_call | solution.py:22
  22.8 0.5 %collective-permute-done.6.refs_1_ = bf16[16,256]{1,0:T(8,128)(2,1)S(1)} collective-permute-done((bf16[16,256]{1,0:T(8,128)(2,1)S(1)}, bf16[16,256]{1,0:T(8,128)(2,1)S(1)}, u32[]{:S(2)}, u32[]{:S(2)}) %collective-permute-start.6) | collective-permute-done | bytes 8224 | tf_op jit(solution)/shard_map/ppermute | solution.py:317
  23.4 0.4 %collective-permute-done.7.refs_2_ = bf16[16,256]{1,0:T(8,128)(2,1)S(1)} collective-permute-done((bf16[16,256]{1,0:T(8,128)(2,1)S(1)}, bf16[16,256]{1,0:T(8,128)(2,1)S(1)}, u32[]{:S(2)}, u32[]{:S(2)}) %collective-permute-start.7) | collective-permute-done | bytes 8224 | tf_op jit(solution)/shard_map/ppermute | solution.py:317
  23.8 0.1 collective-permute-done.8.refs_3_
  23.9 0.9 %last.1 = (bf16[32,16,128]{2,1,0:T(8,128)(2,1)}, bf16[32,2,128]{2,1,0:T(2,128)(2,1)}) custom-call(bf16[16,256]{1,0:T(8,128)(2,1)S(1)} %get-tuple-element.40.refs_0_, bf16[16,256]{1,0:T(8,128)(2,1)S(1)} %collective-permute-done.6.refs_1_, bf16[16,256]{1,0:T(8,128)(2,1)S(1)} %collective-permute-done.7.refs_2_, ...), custom_call_target="tpu_custom_call" | custom-call | flops 1048576 | bytes 741376 | tf_op jit(solution)/shard_map/last/pallas_call | solution.py:22
Async XLA Ops:
  0.6 7.0 %copy-start = (bf16[2048,1024]{1,0:T(8,128)(2,1)S(1)}, bf16[2048,1024]{1,0:T(8,128)(2,1)}, u32[]{:S(2)}) copy-start(bf16[2048,1024]{1,0:T(8,128)(2,1)} %matrix_ref.1) | copy-start | bytes 12582916
  2.0 7.3 %collective-permute-start = (bf16[264,128]{1,0:T(8,128)(2,1)S(1)}, bf16[264,128]{1,0:T(8,128)(2,1)S(1)}, u32[]{:S(2)}, u32[]{:S(2)}) collective-permute-start(bf16[264,128]{1,0:T(8,128)(2,1)S(1)} %get-tuple-element.26), channel_id=1, source_target_pairs={{0,8},{1,9},{2,10},{3,11},{4,12},{5,13},{6,14},{7,15},{8,0},{9,1},... | collective-permute-start | bytes 202760 | tf_op jit(solution)/shard_map/ppermute | solution.py:317
  6.1 4.3 %collective-permute-start.1 = (bf16[264,128]{1,0:T(8,128)(2,1)S(1)}, bf16[264,128]{1,0:T(8,128)(2,1)S(1)}, u32[]{:S(2)}, u32[]{:S(2)}) collective-permute-start(bf16[264,128]{1,0:T(8,128)(2,1)S(1)} %get-tuple-element.27), channel_id=1, source_target_pairs={{0,4},{1,5},{2,6},{3,7},{4,0},{5,1},{6,2},{7,3},{8,12},{9,13},{10,... | collective-permute-start | bytes 202760 | tf_op jit(solution)/shard_map/ppermute | solution.py:317
  7.6 6.1 %collective-permute-start.2 = (bf16[264,128]{1,0:T(8,128)(2,1)S(1)}, bf16[264,128]{1,0:T(8,128)(2,1)S(1)}, u32[]{:S(2)}, u32[]{:S(2)}) collective-permute-start(bf16[264,128]{1,0:T(8,128)(2,1)S(1)} %get-tuple-element.28), channel_id=1, source_target_pairs={{0,12},{1,13},{2,14},{3,15},{4,8},{5,9},{6,10},{7,11},{8,4},{9,5},... | collective-permute-start | bytes 202760 | tf_op jit(solution)/shard_map/ppermute | solution.py:317
  7.7 1.2 %copy-start.3 = (bf16[4,64,2048]{2,1,0:T(8,128)(2,1)S(1)}, bf16[4,64,2048]{2,1,0:T(8,128)(2,1)}, u32[]{:S(2)}) copy-start(bf16[4,64,2048]{2,1,0:T(8,128)(2,1)} %param.15) | copy-start | bytes 3145732
  8.9 7.2 %copy-start.1 = (bf16[32,2,96,128]{3,2,1,0:T(8,128)(2,1)S(1)}, bf16[32,2,96,128]{3,2,1,0:T(8,128)(2,1)}, u32[]{:S(2)}) copy-start(bf16[32,2,96,128]{3,2,1,0:T(8,128)(2,1)} %key_ref.1) | copy-start | bytes 4718596
  8.9 7.2 %copy-start.2 = (bf16[32,2,96,128]{3,2,1,0:T(8,128)(2,1)S(1)}, bf16[32,2,96,128]{3,2,1,0:T(8,128)(2,1)}, u32[]{:S(2)}) copy-start(bf16[32,2,96,128]{3,2,1,0:T(8,128)(2,1)} %value_ref.1) | copy-start | bytes 4718596
  8.9 7.2 %copy-start.5 = (bf16[32,16,128]{2,1,0:T(8,128)(2,1)S(1)}, bf16[32,16,128]{2,1,0:T(8,128)(2,1)}, u32[]{:S(2)}) copy-start(bf16[32,16,128]{2,1,0:T(8,128)(2,1)} %query_ref.1) | copy-start | bytes 393220
  8.9 7.2 %copy-start.6 = (bf16[32,2,128]{2,1,0:T(2,128)(2,1)S(1)}, bf16[32,2,128]{2,1,0:T(2,128)(2,1)}, u32[]{:S(2)}) copy-start(bf16[32,2,128]{2,1,0:T(2,128)(2,1)} %new_ref.1) | copy-start | bytes 49156
  8.9 7.2 %copy-start.9 = (s32[32]{0:T(128)S(1)}, s32[32]{0:T(128)}, u32[]{:S(2)}) copy-start(s32[32]{0:T(128)} %length_ref) | copy-start | bytes 388
  14.2 3.9 %collective-permute-start.3 = (bf16[96,128]{1,0:T(8,128)(2,1)S(1)}, bf16[96,128]{1,0:T(8,128)(2,1)S(1)}, u32[]{:S(2)}, u32[]{:S(2)}) collective-permute-start(bf16[96,128]{1,0:T(8,128)(2,1)S(1)} %get-tuple-element.30), channel_id=1, source_target_pairs={{0,3},{1,2},{2,1},{3,0},{4,7},{5,6},{6,5},{7,4},{8,11},{9,10},{10,... | collective-permute-start | bytes 73736 | tf_op jit(solution)/shard_map/ppermute | solution.py:317
  14.2 3.9 %collective-permute-start.4 = (bf16[96,128]{1,0:T(8,128)(2,1)S(1)}, bf16[96,128]{1,0:T(8,128)(2,1)S(1)}, u32[]{:S(2)}, u32[]{:S(2)}) collective-permute-start(bf16[96,128]{1,0:T(8,128)(2,1)S(1)} %get-tuple-element.31), channel_id=1, source_target_pairs={{0,2},{1,3},{2,0},{3,1},{4,6},{5,7},{6,4},{7,5},{8,10},{9,11},{10,... | collective-permute-start | bytes 73736 | tf_op jit(solution)/shard_map/ppermute | solution.py:317
  15.8 2.3 %collective-permute-start.5 = (bf16[96,128]{1,0:T(8,128)(2,1)S(1)}, bf16[96,128]{1,0:T(8,128)(2,1)S(1)}, u32[]{:S(2)}, u32[]{:S(2)}) collective-permute-start(bf16[96,128]{1,0:T(8,128)(2,1)S(1)} %get-tuple-element.32), channel_id=1, source_target_pairs={{0,1},{1,0},{2,3},{3,2},{4,5},{5,4},{6,7},{7,6},{8,9},{9,8},{10,11... | collective-permute-start | bytes 73736 | tf_op jit(solution)/shard_map/ppermute | solution.py:317
  16.1 2.0 %copy-start.4 = (bf16[4,64,1024]{2,1,0:T(8,128)(2,1)S(1)}, bf16[4,64,1024]{2,1,0:T(8,128)(2,1)}, u32[]{:S(2)}) copy-start(bf16[4,64,1024]{2,1,0:T(8,128)(2,1)} %param.16) | copy-start | bytes 1572868
  16.1 6.5 %copy-start.7 = (f32[256]{0:T(256)S(1)}, f32[256]{0:T(256)}, u32[]{:S(2)}) copy-start(f32[256]{0:T(256)} %param.14) | copy-start | bytes 3076
  16.1 6.5 %copy-start.8 = (s32[32,1]{0,1:T(1,128)S(1)}, s32[32,1]{0,1:T(1,128)}, u32[]{:S(2)}) copy-start(s32[32,1]{0,1:T(1,128)} %param.17) | copy-start | bytes 388
  18.4 5.0 %collective-permute-start.6 = (bf16[16,256]{1,0:T(8,128)(2,1)S(1)}, bf16[16,256]{1,0:T(8,128)(2,1)S(1)}, u32[]{:S(2)}, u32[]{:S(2)}) collective-permute-start(bf16[16,256]{1,0:T(8,128)(2,1)S(1)} %get-tuple-element.41), channel_id=1, source_target_pairs={{0,13},{1,12},{2,15},{3,14},{4,9},{5,8},{6,11},{7,10},{8,5},{9,4},... | collective-permute-start | bytes 24584 | tf_op jit(solution)/shard_map/ppermute | solution.py:317
  19.8 4.0 %collective-permute-start.7 = (bf16[16,256]{1,0:T(8,128)(2,1)S(1)}, bf16[16,256]{1,0:T(8,128)(2,1)S(1)}, u32[]{:S(2)}, u32[]{:S(2)}) collective-permute-start(bf16[16,256]{1,0:T(8,128)(2,1)S(1)} %get-tuple-element.42), channel_id=1, source_target_pairs={{0,9},{1,8},{2,11},{3,10},{4,13},{5,12},{6,15},{7,14},{8,1},{9,0},... | collective-permute-start | bytes 24584 | tf_op jit(solution)/shard_map/ppermute | solution.py:317
  20.4 3.5 %collective-permute-start.8 = (bf16[16,256]{1,0:T(8,128)(2,1)S(1)}, bf16[16,256]{1,0:T(8,128)(2,1)S(1)}, u32[]{:S(2)}, u32[]{:S(2)}) collective-permute-start(bf16[16,256]{1,0:T(8,128)(2,1)S(1)} %get-tuple-element.43), channel_id=1, source_target_pairs={{0,5},{1,4},{2,7},{3,6},{4,1},{5,0},{6,3},{7,2},{8,13},{9,12},{10,... | collective-permute-start | bytes 24584 | tf_op jit(solution)/shard_map/ppermute | solution.py:317

commit v8 on v7

--- a/solution.py
+++ b/solution.py
@@ -8,7 +8,6 @@
 from jax.sharding import PartitionSpec as P
 
 adapter_scale = 0.5
-pack_cost = 40_000_000_000
 lanes = 128
 f32 = jnp.float32
 bf16 = jnp.bfloat16
@@ -357,7 +356,7 @@
         "pack",
         [struct(activations.shape, bf16)] + [struct(message, bf16)] * pieces,
         [stay(home_row), stay(adapter_position.reshape(1, rows)), stay(activations)],
-        pack_cost,
+        2 * rows * slots * features,
         in_specs=[HBM] * 3,
         out_specs=[VMEM] * (pieces + 1),
         scratch_shapes=[

time: 24.9 us -> 25 us (level)
  local copies, waits for them, and re-layouts: 0.45 us -> 2.63 us
  waiting for transfers between devices: 5.62 us -> 3.57 us
    unnamed x20, local copies, waits for them, and re-layouts: 0.45 us -> 2.63 us
    ppermute x9, waiting for transfers between devices: 5.62 us -> 3.57 us  [send(): return lax.ppermute(block, ('replica', 'tensor'), pairs)]
  transfers between devices with their start and end apart: 9 -> 9, of which waited for: 6 -> 4; matrix products, arithmetic and copies ran while one was open for 0% -> 0% of each run, Pallas kernels for 14% -> 14%
where the time goes in v8:
time: 25 us; the launch traced here: 24.8 us
  starting transfers between devices  11.7 us (47%)
  Pallas kernels  6.13 us (25%)
  waiting for transfers between devices  3.57 us (14%)
  local copies, waits for them, and re-layouts  2.63 us (11%)
  between operations  0.74 us (3%)
    ppermute x9, starting transfers between devices, send(): return lax.ppermute(block, ('replica', 'tensor'), pairs)  11.7 us
    pallas_call x8, Pallas kernels, call(): pl.pallas_call(kernel, name=name, out_shape=outs, cost_estimate=pl.CostEs...  6.13 us
    ppermute x9, waiting for transfers between devices, send(): return lax.ppermute(block, ('replica', 'tensor'), pairs)  3.57 us
    unnamed x20, local copies, waits for them, and re-layouts  2.63 us
  transfers between devices with their start and end apart: 9, of which 4 were waited for; matrix products, arithmetic and copies ran while one was open for 0% of the time, Pallas kernels for 14%

profile of v8, /device:TPU:0, one launch (start us, length us, event | category | flops | bytes accessed | tf_op | source)
XLA Modules:
  0.0 24.8 jit_solution(17694673267063645455)
XLA Ops:
  0.6 1.2 %pack.1 = (bf16[32,2048]{1,0:T(8,128)(2,1)S(1)}, bf16[264,128]{1,0:T(8,128)(2,1)S(1)}, bf16[264,128]{1,0:T(8,128)(2,1)S(1)}, bf16[264,128]{1,0:T(8,128)(2,1)S(1)}, bf16[264,128]{1,0:T(8,128)(2,1)S(1)}) custom-call(s32[1,32]{1,0:T(1,128)} %bitcast.7, s32[1,32]{1,0:T(1,128)} %bitcast.10, bf16[32,2048]{1,0:T(8,128)(2,1)} %rows_hbm.1), custom_call_target="tpu_custom_call" | custom-call | flops 8388608 | bytes 532736 | tf_op jit(solution)/shard_map/pack/pallas_call | solution.py:21
  1.8 4.1 %collective-permute-start = (bf16[264,128]{1,0:T(8,128)(2,1)S(1)}, bf16[264,128]{1,0:T(8,128)(2,1)S(1)}, u32[]{:S(2)}, u32[]{:S(2)}) collective-permute-start(bf16[264,128]{1,0:T(8,128)(2,1)S(1)} %get-tuple-element.26), channel_id=1, source_target_pairs={{0,8},{1,9},{2,10},{3,11},{4,12},{5,13},{6,14},{7,15},{8,0},{9,1},... | collective-permute-start | bytes 202760 | tf_op jit(solution)/shard_map/ppermute | solution.py:316
  5.9 1.6 %collective-permute-start.1 = (bf16[264,128]{1,0:T(8,128)(2,1)S(1)}, bf16[264,128]{1,0:T(8,128)(2,1)S(1)}, u32[]{:S(2)}, u32[]{:S(2)}) collective-permute-start(bf16[264,128]{1,0:T(8,128)(2,1)S(1)} %get-tuple-element.27), channel_id=1, source_target_pairs={{0,4},{1,5},{2,6},{3,7},{4,0},{5,1},{6,2},{7,3},{8,12},{9,13},{10,... | collective-permute-start | bytes 202760 | tf_op jit(solution)/shard_map/ppermute | solution.py:316
  7.5 0.0 collective-permute-start.2
  7.5 0.0 copy-start
  7.5 2.2 %copy-done = bf16[2048,1024]{1,0:T(8,128)(2,1)S(1)} copy-done((bf16[2048,1024]{1,0:T(8,128)(2,1)S(1)}, bf16[2048,1024]{1,0:T(8,128)(2,1)}, u32[]{:S(2)}) %copy-start) | copy-done | bytes 4194328
  9.7 0.0 copy-start.3
  9.7 0.8 %base.1.refs_5_.refs_3_ = f32[4,32,256]{2,1,0:T(8,128)S(1)} custom-call(bf16[32,2048]{1,0:T(8,128)(2,1)S(1)} %get-tuple-element.29.rows_ref, bf16[2048,1024]{1,0:T(8,128)(2,1)S(1)} %copy-done), custom_call_target="tpu_custom_call" | custom-call | flops 134217728 | bytes 4456448 | tf_op jit(solution)/shard_map/base/pallas_call | solution.py:21
  10.5 0.4 %copy-done.3 = bf16[4,64,2048]{2,1,0:T(8,128)(2,1)S(1)} copy-done((bf16[4,64,2048]{2,1,0:T(8,128)(2,1)S(1)}, bf16[4,64,2048]{2,1,0:T(8,128)(2,1)}, u32[]{:S(2)}) %copy-start.3) | copy-done | bytes 1048600
  10.9 0.0 copy-start.1
  10.9 0.0 copy-start.2
  10.9 0.0 copy-start.5
  10.9 0.0 copy-start.6
  10.9 0.0 copy-start.9
  10.9 0.3 %turn.1.refs_4_ = bf16[2048,256]{1,0:T(8,128)(2,1)S(1)} custom-call(bf16[256,2048]{1,0:T(8,128)(2,1)S(1)} %bitcast.5), custom_call_target="tpu_custom_call" | custom-call | flops 200000000 | bytes 2097152 | tf_op jit(solution)/shard_map/turn/pallas_call | solution.py:21
  11.3 0.0 collective-permute-done.refs_1_
  11.3 0.0 collective-permute-done.1.refs_2_
  11.3 2.3 %collective-permute-done.2.refs_3_ = bf16[264,128]{1,0:T(8,128)(2,1)S(1)} collective-permute-done((bf16[264,128]{1,0:T(8,128)(2,1)S(1)}, bf16[264,128]{1,0:T(8,128)(2,1)S(1)}, u32[]{:S(2)}, u32[]{:S(2)}) %collective-permute-start.2) | collective-permute-done | bytes 67616 | tf_op jit(solution)/shard_map/ppermute | solution.py:316
  13.6 0.4 %rank.1 = (f32[64,64]{1,0:T(8,128)S(1)}, f32[64,64]{1,0:T(8,128)S(1)}, bf16[96,128]{1,0:T(8,128)(2,1)S(1)}, bf16[96,128]{1,0:T(8,128)(2,1)S(1)}, bf16[96,128]{1,0:T(8,128)(2,1)S(1)}) custom-call(bf16[264,128]{1,0:T(8,128)(2,1)S(1)} %get-tuple-element.25.refs_0_, bf16[264,128]{1,0:T(8,128)(2,1)S(1)} %collective-permute-done.refs_1_, ...), custom_call_target="tpu_custom_call" | custom-call | flops 67108864 | bytes 1556480 | tf_op jit(solution)/shard_map/rank/pallas_call | solution.py:21
  14.0 0.0 collective-permute-start.3
  14.1 1.6 %collective-permute-start.4 = (bf16[96,128]{1,0:T(8,128)(2,1)S(1)}, bf16[96,128]{1,0:T(8,128)(2,1)S(1)}, u32[]{:S(2)}, u32[]{:S(2)}) collective-permute-start(bf16[96,128]{1,0:T(8,128)(2,1)S(1)} %get-tuple-element.31), channel_id=1, source_target_pairs={{0,2},{1,3},{2,0},{3,1},{4,6},{5,7},{6,4},{7,5},{8,10},{9,11},{10,... | collective-permute-start | bytes 73736 | tf_op jit(solution)/shard_map/ppermute | solution.py:316
  15.6 0.3 %collective-permute-start.5 = (bf16[96,128]{1,0:T(8,128)(2,1)S(1)}, bf16[96,128]{1,0:T(8,128)(2,1)S(1)}, u32[]{:S(2)}, u32[]{:S(2)}) collective-permute-start(bf16[96,128]{1,0:T(8,128)(2,1)S(1)} %get-tuple-element.32), channel_id=1, source_target_pairs={{0,1},{1,0},{2,3},{3,2},{4,5},{5,4},{6,7},{7,6},{8,9},{9,8},{10,11... | collective-permute-start | bytes 73736 | tf_op jit(solution)/shard_map/ppermute | solution.py:316
  15.9 0.0 copy-done.1
  15.9 0.0 copy-done.2
  15.9 0.0 copy-done.5
  15.9 0.0 copy-done.6
  15.9 0.0 copy-done.9
  15.9 0.0 copy-start.4
  15.9 0.0 copy-start.7
  15.9 0.0 copy-start.8
  16.0 1.9 %attention.1 = (f32[32,16,128]{2,1,0:T(8,128)S(1)}, f32[32,16,128]{2,1,0:T(8,128)S(1)}) custom-call(s32[32]{0:T(128)S(1)} %copy-done.9, bf16[32,16,128]{2,1,0:T(8,128)(2,1)S(1)} %copy-done.5, bf16[32,2,96,128]{3,2,1,0:T(8,128)(2,1)S(1)} %copy-done.1, bf16[32,2,96,128]{3,2,1,0:T(8,128)(2,1)S(1)} %copy-done.2, bf16[32,2,128]{2,1,0:T(2,128)(2,1)S(1)} %copy-done.6), custom_call_target="tpu_custom_call" | custom-call | flops 25165824 | bytes 3817600 | tf_op jit(solution)/shard_map/attention/pallas_call | solution.py:21
  17.9 0.0 collective-permute-done.3.refs_0_
  17.9 0.1 collective-permute-done.4.refs_1_
  17.9 0.0 collective-permute-done.5.refs_2_
  17.9 0.0 copy-done.4
  17.9 0.3 %up.1 = (bf16[16,256]{1,0:T(8,128)(2,1)S(1)}, bf16[16,256]{1,0:T(8,128)(2,1)S(1)}, bf16[16,256]{1,0:T(8,128)(2,1)S(1)}, bf16[16,256]{1,0:T(8,128)(2,1)S(1)}) custom-call(bf16[96,128]{1,0:T(8,128)(2,1)S(1)} %collective-permute-done.3.refs_0_, bf16[96,128]{1,0:T(8,128)(2,1)S(1)} %collective-permute-done.4.refs_1_, ...), custom_call_target="tpu_custom_call" | custom-call | flops 33554432 | bytes 663552 | tf_op jit(solution)/shard_map/up/pallas_call | solution.py:21
  18.2 1.6 %collective-permute-start.6 = (bf16[16,256]{1,0:T(8,128)(2,1)S(1)}, bf16[16,256]{1,0:T(8,128)(2,1)S(1)}, u32[]{:S(2)}, u32[]{:S(2)}) collective-permute-start(bf16[16,256]{1,0:T(8,128)(2,1)S(1)} %get-tuple-element.41), channel_id=1, source_target_pairs={{0,13},{1,12},{2,15},{3,14},{4,9},{5,8},{6,11},{7,10},{8,5},{9,4},... | collective-permute-start | bytes 24584 | tf_op jit(solution)/shard_map/ppermute | solution.py:316
  19.8 0.4 %collective-permute-start.7 = (bf16[16,256]{1,0:T(8,128)(2,1)S(1)}, bf16[16,256]{1,0:T(8,128)(2,1)S(1)}, u32[]{:S(2)}, u32[]{:S(2)}) collective-permute-start(bf16[16,256]{1,0:T(8,128)(2,1)S(1)} %get-tuple-element.42), channel_id=1, source_target_pairs={{0,9},{1,8},{2,11},{3,10},{4,13},{5,12},{6,15},{7,14},{8,1},{9,0},... | collective-permute-start | bytes 24584 | tf_op jit(solution)/shard_map/ppermute | solution.py:316
  20.2 2.2 %collective-permute-start.8 = (bf16[16,256]{1,0:T(8,128)(2,1)S(1)}, bf16[16,256]{1,0:T(8,128)(2,1)S(1)}, u32[]{:S(2)}, u32[]{:S(2)}) collective-permute-start(bf16[16,256]{1,0:T(8,128)(2,1)S(1)} %get-tuple-element.43), channel_id=1, source_target_pairs={{0,5},{1,4},{2,7},{3,6},{4,1},{5,0},{6,3},{7,2},{8,13},{9,12},{10,... | collective-permute-start | bytes 24584 | tf_op jit(solution)/shard_map/ppermute | solution.py:316
  22.4 0.0 copy-done.7
  22.4 0.0 copy-done.8
  22.4 0.3 %base_sum.1 = (f32[32,256]{1,0:T(8,128)S(1)}, bf16[32,64]{1,0:T(8,128)(2,1)S(1)}) custom-call(bf16[96,128]{1,0:T(8,128)(2,1)S(1)} %collective-permute-done.3.refs_0_, bf16[96,128]{1,0:T(8,128)(2,1)S(1)} %collective-permute-done.4.refs_1_, bf16[96,128]{1,0:T(8,128)(2,1)S(1)} %collective-permute-done.5.refs_2_, f32[4,32,256]{2,1,0:T(8,128)S(1)} %base.1.refs_5_.refs_3_, ...), custom_call_target="tpu_custom_call" | custom-call | flops 32768 | bytes 242816 | tf_op jit(solution)/shard_map/base_sum/pallas_call | solution.py:21
  22.7 0.5 %collective-permute-done.6.refs_1_ = bf16[16,256]{1,0:T(8,128)(2,1)S(1)} collective-permute-done((bf16[16,256]{1,0:T(8,128)(2,1)S(1)}, bf16[16,256]{1,0:T(8,128)(2,1)S(1)}, u32[]{:S(2)}, u32[]{:S(2)}) %collective-permute-start.6) | collective-permute-done | bytes 8224 | tf_op jit(solution)/shard_map/ppermute | solution.py:316
  23.2 0.7 %collective-permute-done.7.refs_2_ = bf16[16,256]{1,0:T(8,128)(2,1)S(1)} collective-permute-done((bf16[16,256]{1,0:T(8,128)(2,1)S(1)}, bf16[16,256]{1,0:T(8,128)(2,1)S(1)}, u32[]{:S(2)}, u32[]{:S(2)}) %collective-permute-start.7) | collective-permute-done | bytes 8224 | tf_op jit(solution)/shard_map/ppermute | solution.py:316
  23.9 0.0 collective-permute-done.8.refs_3_
  23.9 0.9 %last.1 = (bf16[32,16,128]{2,1,0:T(8,128)(2,1)}, bf16[32,2,128]{2,1,0:T(2,128)(2,1)}) custom-call(bf16[16,256]{1,0:T(8,128)(2,1)S(1)} %get-tuple-element.40.refs_0_, bf16[16,256]{1,0:T(8,128)(2,1)S(1)} %collective-permute-done.6.refs_1_, bf16[16,256]{1,0:T(8,128)(2,1)S(1)} %collective-permute-done.7.refs_2_, ...), custom_call_target="tpu_custom_call" | custom-call | flops 1048576 | bytes 741376 | tf_op jit(solution)/shard_map/last/pallas_call | solution.py:21
Async XLA Ops:
  1.8 9.5 %collective-permute-start = (bf16[264,128]{1,0:T(8,128)(2,1)S(1)}, bf16[264,128]{1,0:T(8,128)(2,1)S(1)}, u32[]{:S(2)}, u32[]{:S(2)}) collective-permute-start(bf16[264,128]{1,0:T(8,128)(2,1)S(1)} %get-tuple-element.26), channel_id=1, source_target_pairs={{0,8},{1,9},{2,10},{3,11},{4,12},{5,13},{6,14},{7,15},{8,0},{9,1},... | collective-permute-start | bytes 202760 | tf_op jit(solution)/shard_map/ppermute | solution.py:316
  5.9 5.4 %collective-permute-start.1 = (bf16[264,128]{1,0:T(8,128)(2,1)S(1)}, bf16[264,128]{1,0:T(8,128)(2,1)S(1)}, u32[]{:S(2)}, u32[]{:S(2)}) collective-permute-start(bf16[264,128]{1,0:T(8,128)(2,1)S(1)} %get-tuple-element.27), channel_id=1, source_target_pairs={{0,4},{1,5},{2,6},{3,7},{4,0},{5,1},{6,2},{7,3},{8,12},{9,13},{10,... | collective-permute-start | bytes 202760 | tf_op jit(solution)/shard_map/ppermute | solution.py:316
  7.5 6.1 %collective-permute-start.2 = (bf16[264,128]{1,0:T(8,128)(2,1)S(1)}, bf16[264,128]{1,0:T(8,128)(2,1)S(1)}, u32[]{:S(2)}, u32[]{:S(2)}) collective-permute-start(bf16[264,128]{1,0:T(8,128)(2,1)S(1)} %get-tuple-element.28), channel_id=1, source_target_pairs={{0,12},{1,13},{2,14},{3,15},{4,8},{5,9},{6,10},{7,11},{8,4},{9,5},... | collective-permute-start | bytes 202760 | tf_op jit(solution)/shard_map/ppermute | solution.py:316
  7.5 2.2 %copy-start = (bf16[2048,1024]{1,0:T(8,128)(2,1)S(1)}, bf16[2048,1024]{1,0:T(8,128)(2,1)}, u32[]{:S(2)}) copy-start(bf16[2048,1024]{1,0:T(8,128)(2,1)} %matrix_ref.1) | copy-start | bytes 12582916
  9.7 1.2 %copy-start.3 = (bf16[4,64,2048]{2,1,0:T(8,128)(2,1)S(1)}, bf16[4,64,2048]{2,1,0:T(8,128)(2,1)}, u32[]{:S(2)}) copy-start(bf16[4,64,2048]{2,1,0:T(8,128)(2,1)} %param.15) | copy-start | bytes 3145732
  10.9 5.0 %copy-start.1 = (bf16[32,2,96,128]{3,2,1,0:T(8,128)(2,1)S(1)}, bf16[32,2,96,128]{3,2,1,0:T(8,128)(2,1)}, u32[]{:S(2)}) copy-start(bf16[32,2,96,128]{3,2,1,0:T(8,128)(2,1)} %key_ref.1) | copy-start | bytes 4718596
  10.9 5.0 %copy-start.2 = (bf16[32,2,96,128]{3,2,1,0:T(8,128)(2,1)S(1)}, bf16[32,2,96,128]{3,2,1,0:T(8,128)(2,1)}, u32[]{:S(2)}) copy-start(bf16[32,2,96,128]{3,2,1,0:T(8,128)(2,1)} %value_ref.1) | copy-start | bytes 4718596
  10.9 5.0 %copy-start.5 = (bf16[32,16,128]{2,1,0:T(8,128)(2,1)S(1)}, bf16[32,16,128]{2,1,0:T(8,128)(2,1)}, u32[]{:S(2)}) copy-start(bf16[32,16,128]{2,1,0:T(8,128)(2,1)} %query_ref.1) | copy-start | bytes 393220
  10.9 5.0 %copy-start.6 = (bf16[32,2,128]{2,1,0:T(2,128)(2,1)S(1)}, bf16[32,2,128]{2,1,0:T(2,128)(2,1)}, u32[]{:S(2)}) copy-start(bf16[32,2,128]{2,1,0:T(2,128)(2,1)} %new_ref.1) | copy-start | bytes 49156
  10.9 5.0 %copy-start.9 = (s32[32]{0:T(128)S(1)}, s32[32]{0:T(128)}, u32[]{:S(2)}) copy-start(s32[32]{0:T(128)} %length_ref) | copy-start | bytes 388
  14.0 3.9 %collective-permute-start.3 = (bf16[96,128]{1,0:T(8,128)(2,1)S(1)}, bf16[96,128]{1,0:T(8,128)(2,1)S(1)}, u32[]{:S(2)}, u32[]{:S(2)}) collective-permute-start(bf16[96,128]{1,0:T(8,128)(2,1)S(1)} %get-tuple-element.30), channel_id=1, source_target_pairs={{0,3},{1,2},{2,1},{3,0},{4,7},{5,6},{6,5},{7,4},{8,11},{9,10},{10,... | collective-permute-start | bytes 73736 | tf_op jit(solution)/shard_map/ppermute | solution.py:316
  14.1 3.9 %collective-permute-start.4 = (bf16[96,128]{1,0:T(8,128)(2,1)S(1)}, bf16[96,128]{1,0:T(8,128)(2,1)S(1)}, u32[]{:S(2)}, u32[]{:S(2)}) collective-permute-start(bf16[96,128]{1,0:T(8,128)(2,1)S(1)} %get-tuple-element.31), channel_id=1, source_target_pairs={{0,2},{1,3},{2,0},{3,1},{4,6},{5,7},{6,4},{7,5},{8,10},{9,11},{10,... | collective-permute-start | bytes 73736 | tf_op jit(solution)/shard_map/ppermute | solution.py:316
  15.6 2.3 %collective-permute-start.5 = (bf16[96,128]{1,0:T(8,128)(2,1)S(1)}, bf16[96,128]{1,0:T(8,128)(2,1)S(1)}, u32[]{:S(2)}, u32[]{:S(2)}) collective-permute-start(bf16[96,128]{1,0:T(8,128)(2,1)S(1)} %get-tuple-element.32), channel_id=1, source_target_pairs={{0,1},{1,0},{2,3},{3,2},{4,5},{5,4},{6,7},{7,6},{8,9},{9,8},{10,11... | collective-permute-start | bytes 73736 | tf_op jit(solution)/shard_map/ppermute | solution.py:316
  15.9 2.0 %copy-start.4 = (bf16[4,64,1024]{2,1,0:T(8,128)(2,1)S(1)}, bf16[4,64,1024]{2,1,0:T(8,128)(2,1)}, u32[]{:S(2)}) copy-start(bf16[4,64,1024]{2,1,0:T(8,128)(2,1)} %param.16) | copy-start | bytes 1572868
  15.9 6.5 %copy-start.7 = (s32[32,1]{0,1:T(1,128)S(1)}, s32[32,1]{0,1:T(1,128)}, u32[]{:S(2)}) copy-start(s32[32,1]{0,1:T(1,128)} %param.17) | copy-start | bytes 388
  15.9 6.5 %copy-start.8 = (f32[256]{0:T(256)S(1)}, f32[256]{0:T(256)}, u32[]{:S(2)}) copy-start(f32[256]{0:T(256)} %param.14) | copy-start | bytes 3076
  18.2 5.0 %collective-permute-start.6 = (bf16[16,256]{1,0:T(8,128)(2,1)S(1)}, bf16[16,256]{1,0:T(8,128)(2,1)S(1)}, u32[]{:S(2)}, u32[]{:S(2)}) collective-permute-start(bf16[16,256]{1,0:T(8,128)(2,1)S(1)} %get-tuple-element.41), channel_id=1, source_target_pairs={{0,13},{1,12},{2,15},{3,14},{4,9},{5,8},{6,11},{7,10},{8,5},{9,4},... | collective-permute-start | bytes 24584 | tf_op jit(solution)/shard_map/ppermute | solution.py:316
  19.8 4.1 %collective-permute-start.7 = (bf16[16,256]{1,0:T(8,128)(2,1)S(1)}, bf16[16,256]{1,0:T(8,128)(2,1)S(1)}, u32[]{:S(2)}, u32[]{:S(2)}) collective-permute-start(bf16[16,256]{1,0:T(8,128)(2,1)S(1)} %get-tuple-element.42), channel_id=1, source_target_pairs={{0,9},{1,8},{2,11},{3,10},{4,13},{5,12},{6,15},{7,14},{8,1},{9,0},... | collective-permute-start | bytes 24584 | tf_op jit(solution)/shard_map/ppermute | solution.py:316
  20.2 3.7 %collective-permute-start.8 = (bf16[16,256]{1,0:T(8,128)(2,1)S(1)}, bf16[16,256]{1,0:T(8,128)(2,1)S(1)}, u32[]{:S(2)}, u32[]{:S(2)}) collective-permute-start(bf16[16,256]{1,0:T(8,128)(2,1)S(1)} %get-tuple-element.43), channel_id=1, source_target_pairs={{0,5},{1,4},{2,7},{3,6},{4,1},{5,0},{6,3},{7,2},{8,13},{9,12},{10,... | collective-permute-start | bytes 24584 | tf_op jit(solution)/shard_map/ppermute | solution.py:316
